TPU v7x, 32 devices: a whole 2x2x4 slice. The times are simulated.
32 devices in a mesh: dp: 8 (over z, y), seq: 4 (over x, core).
Axes of the slice: x: 2, y: 2, z: 4, core: 2. Of those that a mesh axis runs over, the one named last changes fastest.
Arguments:
- queries: bfloat16 [8, 512, 1024], P('dp', 'seq'), may hold values from -6 to 6
- key_rows: bfloat16 [8, 512, 1024], P('dp', 'seq'), may hold values from -6 to 6
- value_rows: bfloat16 [8, 512, 1024], P('dp', 'seq'), may hold values from -6 to 6
- inputs: bfloat16 [8, 512, 1024], P('dp', 'seq'), may hold values from -6 to 6
- w_gate: float32 [1024, 32], replicated, may hold values from -0.1875 to 0.1875
- poly_coef: float32 [1024], replicated, may hold values from -0.6 to 0.6
- decay_rate: float32 [16], replicated, may hold values from 0.0003 to 0.05
- cotangent: bfloat16 [8, 512, 1024], P('dp', 'seq'), may hold values from -6 to 6
Outputs:
- grad_queries: bfloat16 [8, 512, 1024], P('dp', 'seq')
- grad_keys: bfloat16 [8, 512, 1024], P('dp', 'seq')
- grad_values: bfloat16 [8, 512, 1024], P('dp', 'seq')
- grad_inputs: bfloat16 [8, 512, 1024], P('dp', 'seq')
- grad_gate: float32 [1024, 32], replicated
- grad_coef: float32 [1024], replicated
- grad_rate: float32 [16], replicated
All inputs are finite; a program needn't handle non-finite values.
Results may differ from a plain program's by a relative error of at most 0.02.
Values may be sent and summed in bfloat16 or wider, within the bound.
No kernel may reach another device: no remote copies, remote signals or barrier semaphores. Data moves between devices by JAX's collectives and lax.ppermute only.
A program may use at most 64 MiB of HBM per device.

v0:
```python
import jax
import jax.numpy as jnp
from jax import lax
from jax.sharding import PartitionSpec as P

WINDOW = 64


highest = lax.Precision.HIGHEST


def passed_along(value, axis, steps):
    count = lax.axis_size(axis)
    first, last = (max(0, -steps), min(count, count - steps))
    return lax.ppermute(value, axis, [(source, source + steps) for source in range(first, last)])


def prefix(x, axis, join, neutral):
    place = lax.axis_index(axis)
    gathered = jax.tree.map(
        lambda a, kind: lax.all_gather(a.astype(kind), axis), x, (jnp.bfloat16, jnp.bfloat16)
    )
    state = jax.tree.map(lambda a, e: jnp.zeros_like(a) + jnp.asarray(e, a.dtype), x, neutral)

    def one(hop, state):
        return join(
            state,
            jax.tree.map(
                lambda a, own: lax.dynamic_index_in_dim(a, hop, 0, False).astype(own.dtype),
                gathered,
                x,
            ),
        )

    return lax.fori_loop(0, place, one, state)


def entering(x, axis, combine, identity):
    count, index = (lax.axis_size(axis), lax.axis_index(axis))
    everything = jax.tree.map(
        lambda part, kind: lax.all_gather(part.astype(kind), axis),
        x,
        jax.tree.map(lambda a: jnp.bfloat16 if a.dtype == jnp.float32 else a.dtype, x),
    )
    start = jax.tree.map(
        lambda part, zero: jnp.broadcast_to(jnp.asarray(zero, part.dtype), part.shape), x, identity
    )

    def hop(k, before):
        at = count - 1 - k
        reached = at > index
        new = combine(
            before, jax.tree.map(lambda part, own: part[at].astype(own.dtype), everything, x)
        )
        return jax.tree.map(lambda a, b: jnp.where(reached, a, b), new, before)

    return lax.fori_loop(0, count, hop, start)


def features(raw, poly_coef):
    as_float = raw.astype(jnp.float32)
    return 0.125 * (as_float + poly_coef * as_float * as_float)


def window_table(window):
    step_ids = lax.broadcasted_iota(jnp.int32, (window, 2 * window), 0)
    slot_ids = lax.broadcasted_iota(jnp.int32, (window, 2 * window), 1)
    offset = step_ids - slot_ids + window
    return ((offset >= 0) & (offset < window)).astype(jnp.float32)


def block_step(memory, block_in):
    q_block, key_pairs, value_pairs, decay_log = block_in
    window = q_block.shape[0]
    head_count = decay_log.shape[1]
    head_dim = q_block.shape[1] // head_count
    log_decay = jnp.cumsum(decay_log, axis=0)
    row_ids = lax.broadcasted_iota(jnp.int32, (window, window), 0)
    col_ids = lax.broadcasted_iota(jnp.int32, (window, window), 1)
    causal = col_ids <= row_ids
    gap_log = jnp.where(causal[:, :, None], log_decay[:, None, :] - log_decay[None, :, :], 0.0)
    decay_mat = jnp.where(causal[:, :, None], jnp.exp(gap_log), 0.0)
    window_mask = window_table(window)
    kernel = jnp.einsum("tsh,si->hti", decay_mat, window_mask, precision=highest)
    q_heads = q_block.reshape(window, head_count, head_dim)
    key_heads = key_pairs.reshape(2 * window, head_count, head_dim)
    value_heads = value_pairs.reshape(2 * window, head_count, head_dim)
    scores = jnp.einsum("thd,ihd->hti", q_heads, key_heads, preferred_element_type=jnp.float32)
    weights = (scores * kernel).astype(jnp.bfloat16)
    inside = jnp.einsum("hti,ihd->thd", weights, value_heads, preferred_element_type=jnp.float32)
    carried_out = (
        jnp.einsum("thd,hde->the", q_heads.astype(jnp.float32), memory, precision=highest)
        * jnp.exp(log_decay)[:, :, None]
    )
    last_row = kernel[:, window - 1, :]
    carried = (key_heads.astype(jnp.float32) * jnp.transpose(last_row)[:, :, None]).astype(
        jnp.bfloat16
    )
    update = jnp.einsum("ihd,ihe->hde", carried, value_heads, preferred_element_type=jnp.float32)
    memory_next = jnp.exp(log_decay[window - 1])[:, None, None] * memory + update
    return (memory_next, (inside + carried_out).reshape(window, head_count * head_dim))


def state_step(memory, block_in):
    key_pairs, value_pairs, decay_log = block_in
    window = decay_log.shape[0]
    head_count = decay_log.shape[1]
    head_dim = key_pairs.shape[1] // head_count
    log_decay = jnp.cumsum(decay_log, axis=0)
    tail_decay = jnp.exp(log_decay[window - 1][None, :] - log_decay)
    last_row = jnp.einsum("sh,si->hi", tail_decay, window_table(window), precision=highest)
    key_heads = key_pairs.reshape(2 * window, head_count, head_dim)
    value_heads = value_pairs.reshape(2 * window, head_count, head_dim)
    carried = (key_heads.astype(jnp.float32) * jnp.transpose(last_row)[:, :, None]).astype(
        jnp.bfloat16
    )
    update = jnp.einsum("ihd,ihe->hde", carried, value_heads, preferred_element_type=jnp.float32)
    return (jnp.exp(log_decay[window - 1])[:, None, None] * memory + update, None)


def prepare(
    key_rows, value_rows, inputs, w_gate, poly_coef, decay_rate, key_rim, value_rim, input_rim
):
    length = key_rows.shape[0]
    window = key_rim.shape[0]
    head_count = decay_rate.shape[0]
    width_all = key_rows.shape[1]
    head_dim = width_all // head_count
    blocks = length // window
    all_inputs = jnp.concatenate([input_rim, inputs], axis=0)
    logits = jnp.dot(all_inputs.astype(jnp.float32), w_gate, precision=highest)
    decay_log = -decay_rate * jax.nn.softplus(logits[window:, :head_count])
    gamma = jax.nn.sigmoid(logits[:, head_count:]) / window
    all_keys = jnp.concatenate([key_rim, key_rows], axis=0)
    all_values = jnp.concatenate([value_rim, value_rows], axis=0)
    weighted = (
        (features(all_keys, poly_coef).reshape(-1, head_count, head_dim) * gamma[:, :, None])
        .astype(jnp.bfloat16)
        .reshape(-1, width_all)
    )
    key_pairs = jnp.concatenate(
        [
            weighted[:length].reshape(blocks, window, width_all),
            weighted[window:].reshape(blocks, window, width_all),
        ],
        axis=1,
    )
    value_pairs = jnp.concatenate(
        [
            all_values[:length].reshape(blocks, window, width_all),
            all_values[window:].reshape(blocks, window, width_all),
        ],
        axis=1,
    )
    return (key_pairs, value_pairs, decay_log)


def state_pass(
    key_rows, value_rows, inputs, w_gate, poly_coef, decay_rate, key_rim, value_rim, input_rim
):
    key_pairs, value_pairs, decay_log = prepare(
        key_rows, value_rows, inputs, w_gate, poly_coef, decay_rate, key_rim, value_rim, input_rim
    )
    window = key_rim.shape[0]
    head_count = decay_rate.shape[0]
    head_dim = key_rows.shape[1] // head_count
    blocks = key_rows.shape[0] // window
    start = jnp.zeros((head_count, head_dim, head_dim), jnp.float32)
    memory_end = lax.scan(
        state_step, start, (key_pairs, value_pairs, decay_log.reshape(blocks, window, head_count))
    )[0]
    return (memory_end, jnp.sum(decay_log, axis=0))


def local_forward(
    queries,
    key_rows,
    value_rows,
    inputs,
    w_gate,
    poly_coef,
    decay_rate,
    key_rim,
    value_rim,
    input_rim,
    memory,
):
    length = queries.shape[0]
    window = key_rim.shape[0]
    head_count = decay_rate.shape[0]
    width_all = queries.shape[1]
    blocks = length // window
    key_pairs, value_pairs, decay_log = prepare(
        key_rows, value_rows, inputs, w_gate, poly_coef, decay_rate, key_rim, value_rim, input_rim
    )
    query_feat = features(queries, poly_coef).astype(jnp.bfloat16)
    memory_end, outputs = lax.scan(
        block_step,
        memory,
        (
            query_feat.reshape(blocks, window, width_all),
            key_pairs,
            value_pairs,
            decay_log.reshape(blocks, window, head_count),
        ),
    )
    return (outputs.reshape(length, width_all), memory_end, jnp.sum(decay_log, axis=0))


def compose(earlier, later):
    return (later[0] * earlier[0], later[0][:, None, None] * earlier[1] + later[1])


def on_device(queries, key_rows, value_rows, inputs, w_gate, poly_coef, decay_rate, cotangent):
    own_queries = queries[0]
    own_keys = key_rows[0]
    own_values = value_rows[0]
    own_inputs = inputs[0]
    rim_parts = passed_along(
        (own_keys[-WINDOW:], own_values[-WINDOW:], own_inputs[-WINDOW:]), "seq", 1
    )
    operands = (
        own_queries,
        own_keys,
        own_values,
        own_inputs,
        w_gate,
        poly_coef,
        decay_rate,
        rim_parts[0],
        rim_parts[1],
        rim_parts[2],
    )
    partial_memory, decay_total = state_pass(
        own_keys,
        own_values,
        own_inputs,
        w_gate,
        poly_coef,
        decay_rate,
        rim_parts[0],
        rim_parts[1],
        rim_parts[2],
    )
    factor = jnp.exp(decay_total)
    identity = (jnp.ones_like(factor), jnp.zeros_like(partial_memory))
    memory_in = prefix((factor, partial_memory), "seq", compose, identity)[1]
    primal, pullback = jax.vjp(local_forward, *operands, memory_in)
    upstream = cotangent[0].astype(jnp.float32)
    local_adjoint = pullback((upstream, jnp.zeros_like(primal[1]), jnp.zeros_like(primal[2])))[10]
    memory_grad = entering((factor, local_adjoint), "seq", compose, identity)[1]
    grads = pullback((upstream, memory_grad, jnp.zeros_like(primal[2])))
    returned = passed_along((grads[7], grads[8], grads[9]), "seq", -1)
    grad_keys = jnp.concatenate([grads[1][:-WINDOW], grads[1][-WINDOW:] + returned[0]], axis=0)
    grad_values = jnp.concatenate([grads[2][:-WINDOW], grads[2][-WINDOW:] + returned[1]], axis=0)
    grad_inputs = jnp.concatenate([grads[3][:-WINDOW], grads[3][-WINDOW:] + returned[2]], axis=0)
    totals = lax.psum((grads[4], grads[5], grads[6]), ("dp", "seq"))
    return (
        grads[0][None],
        grad_keys[None],
        grad_values[None],
        grad_inputs[None],
        totals[0],
        totals[1],
        totals[2],
    )


def solution(mesh):
    placed = (
        P("dp", "seq", None),
        P("dp", "seq", None),
        P("dp", "seq", None),
        P("dp", "seq", None),
        P(),
        P(),
        P(),
        P("dp", "seq", None),
    )
    return jax.shard_map(
        on_device,
        mesh=mesh,
        in_specs=placed,
        out_specs=(
            P("dp", "seq", None),
            P("dp", "seq", None),
            P("dp", "seq", None),
            P("dp", "seq", None),
            P(),
            P(),
            P(),
        ),
        check_vma=False,
    )
```

profile of v0, /device:TPU:0, one launch (start us, length us, event | category | flops | bytes accessed | tf_op | source)
XLA Modules:
  0.0 304.0 jit_solution(5101860999777266344)
XLA Ops:
  8.2 2.5 collective-permute-start
  10.8 4.5 %collective-permute-start.1 = (bf16[64,1024]{1,0:T(8,128)(2,1)S(1)}, bf16[64,1024]{1,0:T(8,128)(2,1)S(1)}, u32[]{:S(2)}, u32[]{:S(2)}) collective-permute-start(bf16[64,1024]{1,0:T(8,128)(2,1)S(1)} %slice_bitcast_fusion.3), channel_id=1, source_target_pairs={{0,1},{1,2},{2,3},{4,5},{5,6},{6,7},{8,9},{9,10},{10,11},{12,13},{... | collective-permute-start | bytes 393224 | tf_op jit(solution)/shard_map/ppermute | solution.py:15
  16.0 2.6 collective-permute-start.2
  18.5 1.7 fusion.130
  32.0 3.2 %while.130 = (s32[]{:T(128)}, f32[16,64,64]{2,1,0:T(8,128)S(1)}, f32[2,64,16]{2,1,0:T(8,128)S(1)}, bf16[2,128,1024]{1,2,0:T(8,128)(2,1)S(1)}, bf16[2,128,1024]{1...) while((s32[]{:T(128)}, f32[16,64,64]{2,1,0:T(8,128)S(1)}, f32[2,64,16]{2,1,0:T(8,128)S(1)}, ...), condition=%wide.region_3.4_spmd.clone, body=%wide.region_1.3_spmd.clone.sunk | while | flops 19046404 | bytes 2134507 | solution.py:169
  35.3 9.2 %all-gather.1 = bf16[64,64,64]{2,1,0:T(8,128)(2,1)S(1)} all-gather(bf16[16,64,64]{2,1,0:T(8,128)(2,1)S(1)} %convert_element_type.327), channel_id=3, replica_groups=mesh['dp'=8,'seq'=4] {'seq'}, dimensions={0}, use_global_device_ids=true | all-gather | bytes 655360 | tf_op jit(solution)/shard_map/all_gather | solution.py:21
  44.7 7.0 %all-reduce.8 = bf16[64]{0:T(256)(128)(2,1)S(1)} all-reduce(bf16[64]{0:T(256)(128)(2,1)S(1)} %dynamic-update-slice), channel_id=2, replica_groups=mesh['dp'=8,'seq'=4] {'seq'}, use_global_device_ids=true, to_apply=%add.8 | all-reduce | flops 64 | bytes 256
  52.5 32.4 %while.128 = (s32[]{:T(128)}, f32[16,64,64]{2,1,0:T(8,128)S(1)}, f32[2,64,64,16]{2,3,1,0:T(8,128)}, bf16[2,128,16,64]{1,3,2,0:T(8,128)(2,1)}, bf16[2,64,16,64]{3...) while((s32[]{:T(128)}, f32[16,64,64]{2,1,0:T(8,128)S(1)}, ...), condition=%wide.region_8.9_spmd.clone.clone, body=%wide.region_6.8_spmd.clone.clone.sunk | while | flops 186301440 | bytes 31898088 | solution.py:197
  52.7 1.5 bitcast_dynamic-update-slice_fusion.12
  63.4 1.3 dynamic_update_slice.252
  68.9 1.5 bitcast_dynamic-update-slice_fusion.12
  85.8 7.9 %while.131 = (s32[]{:T(128)}, f32[16,64,64]{2,1,0:T(8,128)}, f32[2,16,1,1]{1,3,2,0:T(1,128)S(1)}, f32[2,64,16,64]{1,3,2,0:T(8,128)}, f32[2,64,1024]{2,1,0:T(8,12...) while((s32[]{:T(128)}, f32[16,64,64]{2,1,0:T(8,128)}, ...), condition=%wide.region_10.11_spmd.clone, body=%wide.region_9.10_spmd.clone.sunk | while | flops 50593796 | bytes 4469107 | solution.py:197
  86.9 2.0 convolution_add_fusion.11
  90.9 2.0 convolution_add_fusion.11
  94.8 9.8 %all-gather.2 = bf16[64,64,64]{2,1,0:T(8,128)(2,1)S(1)} all-gather(bf16[16,64,64]{2,1,0:T(8,128)(2,1)S(1)} %convert_element_type.334), channel_id=4, replica_groups=mesh['dp'=8,'seq'=4] {'seq'}, dimensions={0}, use_global_device_ids=true | all-gather | bytes 655360 | tf_op jit(solution)/shard_map/all_gather | solution.py:41
  107.8 57.0 %while.129 = (s32[]{:T(128)}, f32[16,64,64]{2,1,0:T(8,128)S(1)}, bf16[2,64,1024]{2,1,0:T(8,128)(2,1)}, bf16[2,128,1024]{2,1,0:T(8,128)(2,1)}, bf16[2,128,1024]{1...) while((s32[]{:T(128)}, f32[16,64,64]{2,1,0:T(8,128)S(1)}, ...), condition=%wide.region_20.21_spmd.clone.clone, body=%wide.region_13.20_spmd.clone.clone.sunk | while | flops 304790528 | bytes 45722872 | solution.py:197
  109.9 1.4 fusion.235
  116.0 1.3 fusion.241
  119.1 2.2 convolution_convert_fusion.9
  123.7 1.6 constant_dynamic-update-slice_fusion.19
  133.0 2.0 convolution_add_fusion.9
  138.4 1.4 fusion.235
  144.5 1.3 fusion.241
  147.6 2.2 convolution_convert_fusion.9
  152.2 1.6 constant_dynamic-update-slice_fusion.19
  161.6 2.0 convolution_add_fusion.9
  173.0 1.3 collective-permute-start.5
  175.6 1.3 collective-permute-start.4
  177.4 1.4 collective-permute-start.3
  179.0 43.2 %all-reduce.9 = (f32[1024]{0:T(1024)}, f32[16]{0:T(128)}) all-reduce(f32[1024]{0:T(1024)S(1)} %add_any.125, f32[16]{0:T(128)S(1)} %neg.24), channel_id=1, replica_groups=mesh['dp'=8,'seq'=4] {'dp','seq'}, use_global_device_ids=true, to_apply=%region_25.26 | all-reduce | flops 1040 | bytes 8320 | tf_op jit(solution)/shard_map/psum | solution.py:257
  227.3 68.3 %all-reduce.12.cloned.1.call-done = f32[1024,32]{0,1:T(8,128)} async-done(((f32[1024,32]{0,1:T(8,128)}), f32[1024,32]{0,1:T(8,128)}) %all-reduce.12.cloned.1.call-update) | async-done | bytes 131088 | tf_op jit(solution)/shard_map/psum | solution.py:257
  295.6 1.6 copy.434
  (412 shorter events, 108.8 us)
Async XLA Ops:
  7.2 17.0 %copy-start = (f32[1024,32]{0,1:T(8,128)S(1)}, f32[1024,32]{0,1:T(8,128)}, u32[]{:S(2)}) copy-start(f32[1024,32]{0,1:T(8,128)} %param.24) | copy-start | bytes 393220
  7.2 3.6 %copy-start.28 = (bf16[1,128,1024]{2,1,0:T(8,128)(2,1)S(1)}, bf16[1,128,1024]{2,1,0:T(8,128)(2,1)}, u32[]{:S(2)}) copy-start(bf16[1,128,1024]{2,1,0:T(8,128)(2,1)} %param.21) | copy-start | bytes 786436
  7.2 8.1 %copy-start.27 = (bf16[1,128,1024]{2,1,0:T(8,128)(2,1)S(1)}, bf16[1,128,1024]{2,1,0:T(8,128)(2,1)}, u32[]{:S(2)}) copy-start(bf16[1,128,1024]{2,1,0:T(8,128)(2,1)} %param.22) | copy-start | bytes 786436
  7.2 288.4 %all-reduce.12.cloned.1.call-start = ((), (), s32[]{:S(2)}) async-start(), calls=%async_computation | async-start | bytes 262144 | tf_op jit(solution)/shard_map/psum | solution.py:257
  8.2 10.3 %copy-start.31 = (bf16[1,128,1024]{2,1,0:T(8,128)(2,1)S(1)}, bf16[1,128,1024]{2,1,0:T(8,128)(2,1)}, u32[]{:S(2)}) copy-start(bf16[1,128,1024]{2,1,0:T(8,128)(2,1)} %param.20) | copy-start | bytes 786436
  8.2 15.9 %collective-permute-start = (bf16[64,1024]{1,0:T(8,128)(2,1)S(1)}, bf16[64,1024]{1,0:T(8,128)(2,1)S(1)}, u32[]{:S(2)}, u32[]{:S(2)}) collective-permute-start(bf16[64,1024]{1,0:T(8,128)(2,1)S(1)} %slice_bitcast_fusion.4), channel_id=1, source_target_pairs={{0,1},{1,2},{2,3},{4,5},{5,6},{6,7},{8,9},{9,10},{10,11},{12,13},{... | collective-permute-start | bytes 393224 | tf_op jit(solution)/shard_map/ppermute | solution.py:15
  10.8 14.7 %collective-permute-start.1 = (bf16[64,1024]{1,0:T(8,128)(2,1)S(1)}, bf16[64,1024]{1,0:T(8,128)(2,1)S(1)}, u32[]{:S(2)}, u32[]{:S(2)}) collective-permute-start(bf16[64,1024]{1,0:T(8,128)(2,1)S(1)} %slice_bitcast_fusion.3), channel_id=1, source_target_pairs={{0,1},{1,2},{2,3},{4,5},{5,6},{6,7},{8,9},{9,10},{10,11},{12,13},{... | collective-permute-start | bytes 393224 | tf_op jit(solution)/shard_map/ppermute | solution.py:15
  16.0 14.0 %collective-permute-start.2 = (bf16[64,1024]{1,0:T(8,128)(2,1)}, bf16[64,1024]{1,0:T(8,128)(2,1)}, u32[]{:S(2)}, u32[]{:S(2)}) collective-permute-start(bf16[64,1024]{1,0:T(8,128)(2,1)} %slice_bitcast_fusion.2), channel_id=1, source_target_pairs={{0,1},{1,2},{2,3},{4,5},{5,6},{6,7},{8,9},{9,10},{10,11},{12,13},{... | collective-permute-start | bytes 393224 | tf_op jit(solution)/shard_map/ppermute | solution.py:15
  20.2 2.1 copy-start.38
  20.9 5.2 %copy-start.20 = (bf16[1,128,1024]{1,2,0:T(8,128)(2,1)}, bf16[1,128,1024]{1,2,0:T(8,128)(2,1)S(1)}, u32[]{:S(2)}) copy-start(bf16[1,128,1024]{1,2,0:T(8,128)(2,1)S(1)} %copy.176) | copy-start | bytes 786436
  22.3 1.9 copy-start.47
  62.2 2.5 copy-start.33
  78.4 2.5 copy-start.33
  119.0 2.3 copy-start.5
  119.1 2.2 copy-start.39
  129.2 1.9 copy-start.16
  133.0 2.1 copy-start.6
  133.0 2.9 copy-start.40
  147.5 2.3 copy-start.5
  147.6 2.2 copy-start.39
  157.7 1.9 copy-start.16
  161.6 2.1 copy-start.6
  161.6 2.9 copy-start.40
  171.2 3.0 copy-start.8
  173.0 50.1 %collective-permute-start.5 = (bf16[64,1024]{1,0:T(8,128)(2,1)}, bf16[64,1024]{1,0:T(8,128)(2,1)}, u32[]{:S(2)}, u32[]{:S(2)}) collective-permute-start(bf16[64,1024]{1,0:T(8,128)(2,1)} %get-tuple-element.1970), channel_id=1, source_target_pairs={{1,0},{2,1},{3,2},{5,4},{6,5},{7,6},{9,8},{10,9},{11,10},{13,12},{... | collective-permute-start | bytes 393224 | tf_op jit(solution)/shard_map/ppermute | solution.py:15
  174.9 2.1 copy-start.29
  174.9 2.1 copy-start.36
  174.9 2.1 copy-start.46
  175.6 48.3 %collective-permute-start.4 = (bf16[64,1024]{1,0:T(8,128)(2,1)}, bf16[64,1024]{1,0:T(8,128)(2,1)}, u32[]{:S(2)}, u32[]{:S(2)}) collective-permute-start(bf16[64,1024]{1,0:T(8,128)(2,1)} %get-tuple-element.1962), channel_id=1, source_target_pairs={{1,0},{2,1},{3,2},{5,4},{6,5},{7,6},{9,8},{10,9},{11,10},{13,12},{... | collective-permute-start | bytes 393224 | tf_op jit(solution)/shard_map/ppermute | solution.py:15
  177.0 1.8 copy-start.30
  177.4 49.2 %collective-permute-start.3 = (bf16[64,1024]{1,0:T(8,128)(2,1)S(1)}, bf16[64,1024]{1,0:T(8,128)(2,1)S(1)}, u32[]{:S(2)}, u32[]{:S(2)}) collective-permute-start(bf16[64,1024]{1,0:T(8,128)(2,1)S(1)} %get-tuple-element.1972), channel_id=1, source_target_pairs={{1,0},{2,1},{3,2},{5,4},{6,5},{7,6},{9,8},{10,9},{11,10},{13,12},{... | collective-permute-start | bytes 393224 | tf_op jit(solution)/shard_map/ppermute | solution.py:15
  178.8 43.3 %copy-start.32 = (bf16[1,128,1024]{2,1,0:T(8,128)(2,1)S(1)}, bf16[1,128,1024]{2,1,0:T(8,128)(2,1)}, u32[]{:S(2)}) copy-start(bf16[1,128,1024]{2,1,0:T(8,128)(2,1)} %param.20) | copy-start | bytes 786436
  (65 other events, 62.9 us)
Sparse Core Ops, SparseCore 0:
  172.4 123.1 all-reduce.11
where the time goes:
time: 307 us; the launch traced here: 304 us
  local copies, waits for them, and re-layouts  73.7 us (24%)
  blocking collectives  69.1 us (23%)
  waiting for transfers between devices  68.4 us (22%)
  matrix products  35.3 us (11%)
  other arithmetic  27.4 us (9%)
  between operations  15.4 us (5%)
  starting transfers between devices  13.6 us (4%)
    psum x1, waiting for transfers between devices, on_device(): totals = lax.psum((grads[4], grads[5], grads[6]), ('dp', 'seq'))  68.3 us
    psum x1, blocking collectives, on_device(): totals = lax.psum((grads[4], grads[5], grads[6]), ('dp', 'seq'))  43.2 us
    while x116, local copies, waits for them, and re-layouts  20.7 us
    dot_general x8, matrix products, block_step(): jnp.einsum('thd,hde->the', q_heads.astype(jnp.float32), memory, precision...  15 us
    ppermute x6, starting transfers between devices, passed_along(): lax.ppermute(value, axis, [(source, source + steps) for source in range(f...  13.6 us
    dynamic_update_slice x28, local copies, waits for them, and re-layouts, local_forward(): lax.scan(block_step, memory, (query_feat.reshape(blocks, window, width_al...  12.6 us
    unnamed x73, local copies, waits for them, and re-layouts  11.6 us
    all_gather x1, blocking collectives, entering(): lax.all_gather(part.astype(kind), axis)  9.76 us
  transfers between devices with their start and end apart: 7, of which 1 were waited for; matrix products, arithmetic and copies ran while one was open for 5% of the time, Pallas kernels for 0%

commit v1 on v0

v1 whole, which is shorter than its diff:
```python
import functools

import jax
import jax.numpy as jnp
from jax import lax
from jax.experimental import pallas as pl
from jax.experimental.pallas import tpu as pltpu
from jax.sharding import PartitionSpec as P

WINDOW = 64
LANES = 128
BAND = 16
F32 = jnp.float32
BF16 = jnp.bfloat16


def iota(shape, dim):
    return lax.broadcasted_iota(jnp.int32, shape, dim)


def split(z, count):
    parts = []
    for _ in range(count):
        high = z.astype(BF16)
        parts.append(high)
        z = z - high.astype(F32)
    return parts


def dot(a, b):
    return lax.dot_general(a, b, (((1,), (0,)), ((), ())), preferred_element_type=F32)


def dot_nt(a, b):
    return lax.dot_general(a, b, (((1,), (1,)), ((), ())), preferred_element_type=F32)


def dot_tn(a, b):
    return lax.dot_general(a, b, (((0,), (0,)), ((), ())), preferred_element_type=F32)


def mask_dot(mask, z, count):
    return sum(dot(mask, part) for part in split(z, count))


def head_table(heads, width):
    per_head = width // heads
    return (iota((heads, width), 1) // per_head == iota((heads, width), 0)).astype(BF16)


def expand(z, table, count=1):
    return sum(dot(part, table) for part in split(z, count))


def head_sum(z, table, count=1):
    return sum(dot_nt(part, table) for part in split(z, count))


def half_masks():
    lane = iota((1, LANES), 1)
    return (lane < LANES // 2).astype(BF16), (lane >= LANES // 2).astype(BF16)


def stacked(z, masks):
    return jnp.concatenate([z * masks[0], z * masks[1]], axis=0)


def one_above(z):
    columns = z.shape[1] // 2
    return jnp.concatenate([z[:, :columns], z[:, columns:]], axis=0)


def folded(z):
    rows = z.shape[0] // 2
    return jnp.where(iota((rows, LANES), 1) < LANES // 2, z[:rows], z[rows:])


def window_own(length):
    gap = iota((length, length), 0) - iota((length, length), 1)
    return ((gap >= 0) & (gap < WINDOW)).astype(BF16)


def window_own_t(length):
    gap = iota((length, length), 1) - iota((length, length), 0)
    return ((gap >= 0) & (gap < WINDOW)).astype(BF16)


def window_rim():
    return (iota((WINDOW, WINDOW), 0) < iota((WINDOW, WINDOW), 1)).astype(BF16)


def window_rim_t():
    return (iota((WINDOW, WINDOW), 1) < iota((WINDOW, WINDOW), 0)).astype(BF16)


def phi(raw, coef):
    return 0.125 * (raw + coef * raw * raw)


def is_odd(me_ref):
    return jax.lax.rem(me_ref[0], 2) == 1


def everywhere(flag, shape):
    return jnp.full(shape, flag.astype(jnp.int32)) == 1


def prep_kernel(heads, count, me_ref, q_ref, k_ref, v_ref, x_ref, g_ref, w_ref, coef_ref, rate_ref,
                wk_ref, qf_ref, small_ref, near_ref, far_ref, memory_ref, adjoint_ref,
                q_buf, k_buf, v_buf, x_buf, g_buf, w_buf, coef_buf, rate_buf, sems):
    length, width = x_ref.shape
    late = length - WINDOW
    copies = [
        pltpu.make_async_copy(source, target, sems.at[i])
        for i, (source, target) in enumerate(
            [
                (x_ref, x_buf), (w_ref, w_buf), (rate_ref, rate_buf), (k_ref, k_buf),
                (coef_ref, coef_buf), (q_ref, q_buf), (v_ref, v_buf), (g_ref, g_buf),
            ]
        )
    ]
    for copy in copies:
        copy.start()
    table = head_table(heads, width)
    lower = (iota((length, length), 1) <= iota((length, length), 0)).astype(BF16)
    copies[0].wait()
    copies[1].wait()
    x = x_buf[...]
    logits = sum(dot_nt(x, part) for part in split(w_buf[...], 2))
    decay_logit = logits[:, :heads]
    soft = jnp.maximum(decay_logit, 0.0) + jnp.log1p(jnp.exp(-jnp.abs(decay_logit)))
    slope = jax.nn.sigmoid(decay_logit)
    gamma = jax.nn.sigmoid(logits[:, heads:]) * (1.0 / WINDOW)
    copies[2].wait()
    total = mask_dot(lower, -rate_buf[...] * soft, 3)
    small_ref[...] = jnp.concatenate(
        [total, gamma, soft, slope, jnp.zeros((length, LANES - 4 * heads), F32)], axis=1
    )
    info = jnp.concatenate(
        [part.astype(F32) for part in split(total[:WINDOW], 3)]
        + [jnp.zeros((WINDOW, LANES - 3 * heads), F32)],
        axis=1,
    ).astype(BF16)
    copies[3].wait()
    copies[4].wait()
    coef = coef_buf[...]
    wk = (phi(k_buf[...].astype(F32), coef) * expand(gamma, table)).astype(BF16)
    wk_ref[...] = wk
    copies[5].wait()
    qf = phi(q_buf[...].astype(F32), coef).astype(BF16)
    qf_ref[...] = qf
    copies[6].wait()
    copies[7].wait()
    kept = mask_dot(window_own_t(length), jnp.exp(total[length - 1:] - total), 2)
    faded = jnp.exp(total[late:] - total[late - 1:late])
    scale = expand(jnp.concatenate([kept, faded], axis=0), table)
    carried = (wk.astype(F32) * scale[:length]).astype(BF16)
    faded = (g_buf[late:].astype(F32) * scale[length:]).astype(BF16)
    memory, adjoint = [], []
    for pair in range(width // LANES):
        at = slice(pair * LANES, (pair + 1) * LANES)
        memory.append(folded(dot_tn(carried[:, at], v_buf[:, at])))
        adjoint.append(folded(dot_tn(qf[late:, at], faded[:, at])))
    memory, adjoint = jnp.concatenate(memory, axis=1), jnp.concatenate(adjoint, axis=1)
    memory_ref[...] = memory
    adjoint_ref[...] = adjoint

    def pack(onward, back):
        onward[:WINDOW] = wk[late:]
        onward[WINDOW:2 * WINDOW] = v_buf[late:]
        back[:WINDOW] = qf[:WINDOW]
        back[WINDOW:2 * WINDOW] = g_buf[:WINDOW]
        onward[2 * WINDOW:2 * WINDOW + BAND] = jnp.zeros((BAND, width), BF16)
        back[2 * WINDOW:2 * WINDOW + BAND] = jnp.zeros((BAND, width), BF16)
        for step in range(WINDOW // BAND):
            band = info[step * BAND:(step + 1) * BAND]
            back[2 * WINDOW:2 * WINDOW + BAND, step * LANES:(step + 1) * LANES] = band

    odd = is_odd(me_ref)
    pl.when(odd)(lambda: pack(far_ref, near_ref))
    pl.when(jnp.logical_not(odd))(lambda: pack(near_ref, far_ref))
    near_ref[2 * WINDOW + BAND:] = jnp.where(everywhere(odd, memory.shape), adjoint, memory).astype(BF16)

    @pl.when((me_ref[0] == 0) | (me_ref[0] == count - 1))
    def _():
        far_ref[...] = jnp.zeros_like(far_ref)


def received(me_ref, near_ref, far_ref, fwd_ref, bwd_ref):
    odd = is_odd(me_ref)

    def keep(before, after):
        fwd_ref[...] = before[:2 * WINDOW + BAND]
        bwd_ref[...] = after[:2 * WINDOW + BAND]

    pl.when(odd)(lambda: keep(near_ref, far_ref))
    pl.when(jnp.logical_not(odd))(lambda: keep(far_ref, near_ref))


def next_decay(rim_ref, heads):
    info = jnp.concatenate(
        [
            rim_ref[2 * WINDOW:2 * WINDOW + BAND, step * LANES:(step + 1) * LANES]
            for step in range(WINDOW // BAND)
        ],
        axis=0,
    ).astype(F32)
    return info[:, :heads] + info[:, heads:2 * heads] + info[:, 2 * heads:3 * heads]


def join_kernel(heads, count, before_if_odd, me_ref, own_ref, edge_ref, small_ref, memory_ref, adjoint_ref, rim_ref,
                *rest):
    state_ref, part_ref, out_ref = rest if len(rest) == 3 else (None, *rest)
    width = rim_ref.shape[1]
    length = small_ref.shape[0]
    table = head_table(heads, width)
    total = small_ref[:, :heads]
    last = total[length - 1:]
    middle = total[length - WINDOW - 1:length - WINDOW]
    next_total = next_decay(rim_ref, heads)
    before = is_odd(me_ref) if before_if_odd else jnp.logical_not(is_odd(me_ref))
    kept = mask_dot(window_rim_t(), jnp.exp(middle - total[:WINDOW]), 2)
    scale = jnp.where(everywhere(before, kept.shape), kept, jnp.exp(next_total))
    fade = jnp.exp(last - middle)
    weight = jnp.where(
        everywhere(before, fade.shape), jnp.exp(last), fade * jnp.exp(next_total[WINDOW - 1:])
    )
    scale = expand(jnp.concatenate([scale, fade, weight], axis=0), table)
    scaled = (rim_ref[WINDOW:2 * WINDOW].astype(F32) * scale[:WINDOW]).astype(BF16)
    fade, weight = scale[WINDOW:WINDOW + 1], scale[WINDOW + 1:]
    if state_ref is None:
        state = rim_ref[2 * WINDOW + BAND:].astype(F32)
    else:
        edge = (me_ref[0] == 0) | (me_ref[0] == count - 1)
        state = jnp.where(everywhere(edge, state_ref.shape), 0.0, state_ref[...].astype(F32))
    base = jnp.where(everywhere(before, memory_ref.shape), memory_ref[...], adjoint_ref[...])
    base = base + weight * state
    for pair in range(width // LANES):
        at = slice(pair * LANES, (pair + 1) * LANES)
        part = folded(dot_tn(rim_ref[:WINDOW, at], scaled[:, at]))
        part_ref[:, at] = part
        out_ref[:, at] = (base[:, at] + fade[:, at] * part).astype(BF16)


def decays(column_pair, row_pair, keep):
    gap = jnp.where(keep, column_pair - row_pair, -1e30)
    return jnp.exp(gap)


def own_kernel(heads, me_ref, small_ref, wk_ref, qf_ref, v_ref, g_ref, dq_ref, dwk_ref, dv_ref, dl_ref):
    length, width = wk_ref.shape
    table = head_table(heads, width)
    masks = half_masks()
    small = small_ref[...]
    total = small[:, :heads]
    total_t = jnp.transpose(small)[:heads]
    keep = iota((length, length), 1) <= iota((length, length), 0)
    own = window_own(length).astype(F32)
    empty = jnp.zeros_like(own)
    windows = jnp.concatenate(
        [jnp.concatenate([own, empty], axis=1), jnp.concatenate([empty, own], axis=1)], axis=0
    ).astype(BF16)
    pairs = [slice(pair * LANES, (pair + 1) * LANES) for pair in range(width // LANES)]
    held = []
    for pair, at in enumerate(pairs):
        decay = jnp.concatenate(
            [decays(total[:, i:i + 1], total_t[i:i + 1], keep) for i in (2 * pair, 2 * pair + 1)], axis=1
        )
        kernel = dot(decay.astype(BF16), windows)
        scores = dot_nt(qf_ref[:, at], stacked(wk_ref[:, at], masks))
        lifted = dot_nt(g_ref[:, at], stacked(v_ref[:, at], masks))
        held.append(
            (
                decay,
                (scores * kernel).astype(BF16),
                (lifted * kernel).astype(BF16),
                (lifted * scores).astype(BF16),
            )
        )
    columns = []
    products = []
    for (decay, weights, d_scores, d_kernel), at in zip(held, pairs):
        q, g = qf_ref[:, at], g_ref[:, at]
        products.append(dot(weights, stacked(v_ref[:, at], masks)) * g.astype(F32))
        dq_ref[:, at] = dot(d_scores, stacked(wk_ref[:, at], masks))
        dwk_ref[:, at] = dot_tn(one_above(d_scores), stacked(q, masks))
        dv_ref[:, at] = dot_tn(one_above(weights), stacked(g, masks))
        column = jnp.sum(dot_nt(d_kernel, windows) * decay, axis=0, keepdims=True)
        columns += [column[:, :length], column[:, length:]]
    column = jnp.concatenate(columns + [jnp.zeros((LANES - heads, length), F32)], axis=0)
    rows = head_sum(jnp.concatenate(products, axis=1), table)
    dl_ref[...] = rows - jnp.transpose(column)[:, :heads]


def edge_decay(total, heads):
    lane = iota((WINDOW, LANES), 1)
    first = lane < LANES // 2
    keep = jnp.where(first, lane, lane - LANES // 2) <= iota((WINDOW, LANES), 0)
    doubled = jnp.concatenate([total, total], axis=0)
    doubled = jnp.concatenate([doubled, jnp.zeros((2 * WINDOW, LANES - heads), F32)], axis=1)
    rows = jnp.transpose(doubled)[:heads]
    return lambda h: decays(
        jnp.where(first, total[:, h:h + 1], total[:, h + 1:h + 2]),
        jnp.where(first, rows[h:h + 1], rows[h + 1:h + 2]),
        keep,
    )


def scales_of(heads, small_ref, scales_ref):
    length = small_ref.shape[0]
    late = length - WINDOW
    total, gamma = small_ref[:, :heads], small_ref[:, heads:2 * heads]
    last, middle = total[length - 1:], total[late - 1:late]
    own = mask_dot(window_own_t(length), jnp.exp(last - total), 2)
    grown = jnp.exp(jnp.concatenate([total[:late], total[late:] - middle], axis=0))
    rest = [jnp.exp(middle), jnp.exp(last - middle), jnp.zeros((BAND - 2, heads), F32)]
    scales = jnp.concatenate([own, grown, gamma] + rest, axis=0)
    scales_ref[...] = expand(scales, head_table(heads, scales_ref.shape[1]))


def edge_kernel(heads, before_if_odd, me_ref, small_ref, wk_ref, qf_ref, v_ref, g_ref, rim_ref,
                first_ref, second_ref, dl_ref, *rest):
    length, width = wk_ref.shape
    late = length - WINDOW
    table = head_table(heads, width)
    masks = half_masks()
    pairs = [slice(pair * LANES, (pair + 1) * LANES) for pair in range(width // LANES)]
    cell = (iota((LANES, LANES), 0), iota((LANES, LANES), 1))
    same = (cell[0] < WINDOW) == (cell[1] < WINDOW)
    windows = (same & (cell[0] < cell[1])).astype(BF16)
    before = is_odd(me_ref) if before_if_odd else jnp.logical_not(is_odd(me_ref))
    if rest:
        scales_of(heads, small_ref, rest[0])

    @pl.when(before)
    def _():
        decay_at = edge_decay(small_ref[:WINDOW, :heads], heads)
        held = []
        for pair, at in enumerate(pairs):
            keys, values = stacked(rim_ref[:WINDOW, at], masks), stacked(rim_ref[WINDOW:2 * WINDOW, at], masks)
            decay = decay_at(2 * pair)
            kernel = dot(decay.astype(BF16), windows)
            scores = dot_nt(qf_ref[:WINDOW, at], keys)
            lifted = dot_nt(g_ref[:WINDOW, at], values)
            held.append(
                (
                    keys,
                    values,
                    decay,
                    (scores * kernel).astype(BF16),
                    (lifted * kernel).astype(BF16),
                    (lifted * scores).astype(BF16),
                )
            )
        columns, products = [], []
        for (keys, values, decay, weights, d_scores, d_kernel), at in zip(held, pairs):
            products.append(dot(weights, values) * g_ref[:WINDOW, at].astype(F32))
            first_ref[:, at] = dot(d_scores, keys)
            column = jnp.sum(dot_nt(d_kernel, windows) * decay, axis=0, keepdims=True)
            columns += [column[:, :WINDOW], column[:, WINDOW:]]
        column = jnp.concatenate(columns + [jnp.zeros((LANES - heads, WINDOW), F32)], axis=0)
        column = jnp.concatenate([column, jnp.zeros((LANES, LANES - WINDOW), F32)], axis=1)
        rows = head_sum(jnp.concatenate(products, axis=1), table)
        dl_ref[...] = rows - jnp.transpose(column)[:WINDOW, :heads]

    @pl.when(jnp.logical_not(before))
    def _():
        decay_at = edge_decay(next_decay(rim_ref, heads), heads)
        held = []
        for pair, at in enumerate(pairs):
            q, g = rim_ref[:WINDOW, at], rim_ref[WINDOW:2 * WINDOW, at]
            keys, values = stacked(wk_ref[late:, at], masks), stacked(v_ref[late:, at], masks)
            kernel = dot(decay_at(2 * pair).astype(BF16), windows)
            held.append(
                (q, g, (dot_nt(q, keys) * kernel).astype(BF16), (dot_nt(g, values) * kernel).astype(BF16))
            )
        for (q, g, weights, d_scores), at in zip(held, pairs):
            first_ref[:, at] = dot_tn(one_above(d_scores), stacked(q, masks))
            second_ref[:, at] = dot_tn(one_above(weights), stacked(g, masks))


def finish_kernel(heads, count, me_ref, q_ref, k_ref, x_ref, v_ref, g_ref, coef_ref, rate_ref,
                  small_ref, wk_ref, qf_ref, near_ref, far_ref, adjoint_ref,
                  dqf_ref, dwk_ref, dvl_ref, dl_ref, scales_ref,
                  near_first_ref, near_second_ref, near_dl_ref, far_first_ref, far_second_ref, far_dl_ref,
                  near_part_ref, far_part_ref, cross_ref, passed_ref,
                  dq_out, dk_out, dv_out, logits_ref, keep_ref, give_ref,
                  fwd_ref, bwd_ref, rim_dq_ref, rim_dwk_ref, rim_dv_ref, rim_dl_ref,
                  dq_ref, dk_ref, dv_ref, sems):
    length, width = wk_ref.shape
    late = length - WINDOW
    pairs = width // LANES
    received(me_ref, near_ref, far_ref, fwd_ref, bwd_ref)

    def edges(dq, dl, dwk, dv):
        rim_dq_ref[...], rim_dl_ref[...] = dq[...], dl[...]
        rim_dwk_ref[...], rim_dv_ref[...] = dwk[...], dv[...]

    far_edge = (far_first_ref, far_dl_ref, near_first_ref, near_second_ref)
    near_edge = (near_first_ref, near_dl_ref, far_first_ref, far_second_ref)
    pl.when(is_odd(me_ref))(lambda: edges(*near_edge))
    pl.when(jnp.logical_not(is_odd(me_ref)))(lambda: edges(*far_edge))
    table = head_table(heads, width)
    masks = half_masks()
    small = small_ref[...]
    total, gamma, soft, slope = (small[:, i * heads:(i + 1) * heads] for i in range(4))
    last, middle = total[length - 1:], total[late - 1:late]
    tail = jnp.exp(last - total)
    own = mask_dot(window_own_t(length), tail, 2)
    next_total = next_decay(bwd_ref, heads)
    next_middle = next_total[WINDOW - 1:]
    onward = mask_dot(window_rim_t(), jnp.exp(next_middle - next_total), 2)
    grown = jnp.exp(jnp.concatenate([total[:late], total[late:] - middle], axis=0))
    fade = jnp.exp(last - middle)
    onward_x = expand(jnp.concatenate([onward, jnp.exp(next_middle)], axis=0), table)
    onward_x, next_x = onward_x[:WINDOW], onward_x[WINDOW:]
    own_x, grown_x, gamma_x = (scales_ref.at[i * length:(i + 1) * length] for i in range(3))
    middle_x, fade_x = (scales_ref[i:i + 1] for i in range(3 * length, 3 * length + 2))

    me = me_ref[0]
    shape = (WINDOW, width)
    odd = everywhere(is_odd(me_ref), shape)
    edge = everywhere((me == 0) | (me == count - 1), shape)
    cross = jnp.where(edge, 0.0, cross_ref[...].astype(F32))
    passed = passed_ref[...].astype(F32)
    near_part, far_part = near_part_ref[...], far_part_ref[...]
    start = jnp.where(odd, passed, cross)
    later = jnp.where(odd, cross, passed)
    after = jnp.where(odd, far_part, near_part) + next_x * later
    halfway = middle_x * start + jnp.where(odd, near_part, far_part)
    half_after = adjoint_ref[...] + fade_x * after
    d_state = jnp.sum(head_sum(after * halfway, table, 2), axis=0, keepdims=True)
    start, later, after, halfway, half_after = (
        z.astype(BF16) for z in (start, later, after, halfway, half_after)
    )

    own_products, rim_products, out_products, key_products, d_coef = [], [], [], [], []
    coef = coef_ref[...]
    for pair in range(pairs):
        at = slice(pair * LANES, (pair + 1) * LANES)
        m0, m1, a1, a0, b0 = (stacked(z[:, at], masks) for z in (start, halfway, after, half_after, later))
        qf, g, wk, v = qf_ref[:, at], g_ref[:, at], wk_ref[:, at], v_ref[:, at]
        from_q = jnp.concatenate([dot(qf[:late], m0), dot(qf[late:], m1)], axis=0)
        out_products.append(from_q * g.astype(F32))
        from_g = jnp.concatenate([dot_nt(g[:late], m0), dot_nt(g[late:], m1)], axis=0)
        dqf = dqf_ref[:, at] + grown_x[:, at] * from_g
        dqf = jnp.concatenate([dqf[:late] + rim_dq_ref[:, at], dqf[late:]], axis=0)
        from_keys = dot(wk, a1)
        own_products.append(from_keys * v.astype(F32))
        rim_products.append(dot(fwd_ref[:WINDOW, at], a0) * fwd_ref[WINDOW:2 * WINDOW, at].astype(F32))
        dwk = dwk_ref[:, at] + own_x[:, at] * dot_nt(v, a1)
        dv = dvl_ref[:, at] + own_x[:, at] * from_keys
        dwk = jnp.concatenate(
            [dwk[:late], dwk[late:] + rim_dwk_ref[:, at] + onward_x[:, at] * dot_nt(v[late:], b0)], axis=0
        )
        dv_ref[:late, at] = dv[:late].astype(BF16)
        dv_ref[late:, at] = (
            dv[late:] + rim_dv_ref[:, at] + onward_x[:, at] * dot(wk[late:], b0)
        ).astype(BF16)
        q, k = q_ref[:, at].astype(F32), k_ref[:, at].astype(F32)
        c = coef[:, at]
        key_products.append(dwk * phi(k, c))
        d_phi = dwk * gamma_x[:, at]
        dq_ref[:, at] = (dqf * (0.125 + 0.25 * c * q)).astype(BF16)
        dk_ref[:, at] = (d_phi * (0.125 + 0.25 * c * k)).astype(BF16)
        d_coef.append(jnp.sum(dqf * (0.125 * q * q) + d_phi * (0.125 * k * k), axis=0, keepdims=True))

    copies = [
        pltpu.make_async_copy(source, target, sems.at[i])
        for i, (source, target) in enumerate([(dq_ref, dq_out), (dk_ref, dk_out), (dv_ref, dv_out)])
    ]
    for copy in copies:
        copy.start()
    sums = jnp.concatenate(
        [
            jnp.concatenate(z, axis=1).astype(BF16)
            for z in (own_products, out_products, key_products, rim_products)
        ],
        axis=0,
    )
    sums = dot_nt(sums, table)
    d_own, d_out, d_gamma = (sums[i * length:(i + 1) * length] for i in range(3))
    d_rim = sums[3 * length:]
    d_tail = tail * mask_dot(window_own(length), d_own, 2)
    rim_tail = jnp.exp(middle - total[:late]) * mask_dot(window_rim(), d_rim, 2)
    at_end = jnp.sum(own * d_own, axis=0, keepdims=True) + fade * d_state
    d_total = dl_ref[...] + grown * d_out - d_tail
    d_total = jnp.concatenate([d_total[:late] + rim_dl_ref[...] - rim_tail, d_total[late:]], axis=0)
    d_total = d_total + jnp.where(iota((length, heads), 0) == length - 1, at_end, 0.0)
    upper = (iota((length, length), 1) >= iota((length, length), 0)).astype(BF16)
    d_decay = mask_dot(upper, d_total, 3)
    d_rate = -jnp.sum(d_decay * soft, axis=0, keepdims=True)
    d_logits = jnp.concatenate(
        [-rate_ref[...] * d_decay * slope, d_gamma * gamma * (1.0 - WINDOW * gamma)], axis=1
    )
    logits_ref[...] = d_logits
    gate = dot_tn(d_logits.astype(BF16), x_ref[...])
    d_rate = jnp.concatenate([d_rate, jnp.zeros((1, LANES - heads), F32)], axis=1)
    halves = []
    for half in range(2):
        blocks = range(half * pairs // 2, (half + 1) * pairs // 2)
        rest = [d_coef[i] for i in blocks] + [d_rate, jnp.zeros((BAND - 1 - len(blocks), LANES), F32)]
        rows = [gate[:, i * LANES:(i + 1) * LANES] for i in blocks]
        halves.append(jnp.concatenate(rows + rest, axis=0).astype(BF16))

    def give(mine, theirs):
        keep_ref[...] = mine
        give_ref[...] = theirs

    pl.when(is_odd(me_ref))(lambda: give(halves[1], halves[0]))
    pl.when(jnp.logical_not(is_odd(me_ref)))(lambda: give(halves[0], halves[1]))
    for copy in copies:
        copy.wait()


def inputs_kernel(me_ref, logits_ref, w_ref, dx_ref):
    high, low = (part.astype(F32) for part in split(logits_ref[...], 2))
    w_high, w_low = split(w_ref[...], 2)
    dx_ref[...] = dot(
        jnp.concatenate([high, low, high], axis=1).astype(BF16),
        jnp.concatenate([w_high, w_high, w_low], axis=0),
    ).astype(BF16)


def last_kernel(heads, me_ref, mine_ref, theirs_ref, gate_ref, coef_ref, rate_ref):
    odd = jnp.full(mine_ref.shape, jax.lax.rem(me_ref[0], 2)) == 1
    mine, theirs = mine_ref[...], theirs_ref[...]
    halves = [jnp.where(odd, theirs, mine), jnp.where(odd, mine, theirs)]
    blocks = gate_ref.shape[1] // LANES // 2
    for half in range(2):
        for i in range(blocks):
            at = slice((half * blocks + i) * LANES, (half * blocks + i + 1) * LANES)
            gate_ref[:, at] = halves[half][i * 2 * heads:(i + 1) * 2 * heads]
            coef_ref[:, at] = halves[half][blocks * 2 * heads + i:blocks * 2 * heads + i + 1]
    at = blocks * (2 * heads + 1)
    rate_ref[...] = halves[0][at:at + 1, :heads]


def call(kernel, outs, operands, name, scratch=(), in_place=(), outside=(), flops=10**8, moved=3 * 10**6):
    specs = [pl.BlockSpec(memory_space=pltpu.SMEM)]
    specs += [
        pl.BlockSpec(memory_space=pltpu.HBM if i in in_place else pltpu.VMEM)
        for i in range(1, len(operands))
    ]
    operands = [
        pltpu.with_memory_space_constraint(z, pltpu.HBM) if i in in_place else z
        for i, z in enumerate(operands)
    ]
    return pl.pallas_call(
        kernel,
        out_shape=tuple(jax.ShapeDtypeStruct(*out) for out in outs),
        in_specs=specs,
        out_specs=tuple(
            pl.BlockSpec(memory_space=pltpu.HBM if i in outside else pltpu.VMEM) for i in range(len(outs))
        ),
        scratch_shapes=list(scratch),
        compiler_params=pltpu.CompilerParams(vmem_limit_bytes=32 * 2**20),
        cost_estimate=pl.CostEstimate(flops=flops, bytes_accessed=moved, transcendentals=10**6),
        name=name,
    )(*operands)


EVERYONE = ("dp", "seq")


def swapped(value, axis, distance):
    return lax.ppermute(value, axis, [(i, i ^ distance) for i in range(lax.axis_size(axis))])


def inner_swapped(value):
    dp, seq = (lax.axis_size(axis) for axis in EVERYONE)
    pairs = []
    for i in range(dp):
        for j in range(seq):
            inner = 0 < j < seq - 1
            pairs.append((i * seq + j, i * seq + seq - 1 - j if inner else (i ^ 1) * seq + j))
    return lax.ppermute(value, EVERYONE, pairs)


def on_device(queries, key_rows, value_rows, inputs, w_gate, poly_coef, decay_rate, cotangent):
    q, k, v, x, g = (z[0] for z in (queries, key_rows, value_rows, inputs, cotangent))
    length, width = x.shape
    heads = decay_rate.shape[0]
    count = lax.axis_size("seq")
    assert count == 4 and length == 2 * WINDOW
    me = lax.axis_index("seq").astype(jnp.int32).reshape(1)
    wide, small = ((length, width), BF16), ((length, LANES), F32)
    full, half, gain = ((length, width), F32), ((WINDOW, width), F32), ((length, heads), F32)
    rim, sent = ((2 * WINDOW + BAND, width), BF16), ((WINDOW, width), BF16)
    wk, qf, gates, near, far, memory, adjoint, q, k, v, x, g, wt, coef, rate = call(
        functools.partial(prep_kernel, heads, count),
        [wide, wide, small, ((3 * WINDOW + BAND, width), BF16), rim, half, half]
        + [wide] * 5
        + [((2 * heads, width), F32), ((1, width), F32), ((1, heads), F32)],
        (me, q, k, v, x, g, w_gate.T, poly_coef.reshape(1, width), decay_rate.reshape(1, heads)),
        "prep",
        scratch=[pltpu.SemaphoreType.DMA((8,))],
        in_place=range(1, 9),
    )
    near = swapped(near, "seq", 1)
    far = inner_swapped(far)
    near_part, cross = call(
        functools.partial(join_kernel, heads, count, True),
        [half, sent],
        (me, gates, gates, gates, memory, adjoint, near),
        "join_near",
    )
    cross = inner_swapped(cross)
    own = call(
        functools.partial(own_kernel, heads),
        [full, full, full, gain],
        (me, gates, wk, qf, v, g),
        "own",
        flops=7 * 10**8,
        moved=7 * 10**6,
    )
    edge = [half, half, ((WINDOW, heads), F32)]
    *near_edge, scales = call(
        functools.partial(edge_kernel, heads, True),
        edge + [((3 * length + BAND, width), F32)],
        (me, gates, wk, qf, v, g, near),
        "edge_near",
        flops=2 * 10**8,
        moved=5 * 10**6,
    )
    far_part, passed = call(
        functools.partial(join_kernel, heads, count, False),
        [half, sent],
        (me, own[3], near_edge[2], gates, memory, adjoint, far, cross),
        "join_far",
    )
    passed = swapped(passed, "seq", 1)
    far_edge = call(
        functools.partial(edge_kernel, heads, False),
        edge,
        (me, gates, wk, qf, v, g, far),
        "edge_far",
        flops=2 * 10**8,
        moved=3 * 10**6,
    )
    half_sums = ((width // LANES // 2 * 2 * heads + BAND, LANES), BF16)
    dq, dk, dv, d_logits, keep, give = call(
        functools.partial(finish_kernel, heads, count),
        [wide, wide, wide, ((length, 2 * heads), F32), half_sums, half_sums],
        (me, q, k, x, v, g, coef, rate, gates, wk, qf, near, far, adjoint, *own, scales, *near_edge, *far_edge,
         near_part, far_part, cross, passed),
        "finish",
        scratch=[pltpu.VMEM(*z) for z in (rim, rim, half, half, half, edge[2], wide, wide, wide)]
        + [pltpu.SemaphoreType.DMA((3,))],
        outside=range(3),
    )
    dx = call(inputs_kernel, [wide], (me, d_logits, wt), "inputs")[0]
    sums = keep.astype(F32) + swapped(give, EVERYONE, 1).astype(F32)
    distance = 2
    while distance < lax.axis_size(EVERYONE):
        sums = sums.astype(BF16)
        if 2 * distance < lax.axis_size(EVERYONE):
            far, mid, one = (swapped(sums, EVERYONE, i * distance).astype(F32) for i in (3, 2, 1))
            sums = (sums.astype(F32) + one) + (mid + far)
        else:
            sums = sums.astype(F32) + swapped(sums, EVERYONE, distance).astype(F32)
        if distance == 2:
            sums, dx = lax.optimization_barrier((sums, dx))
        distance *= 4
    gate, d_coef, d_rate = call(
        functools.partial(last_kernel, heads),
        [((2 * heads, width), F32), ((1, width), F32), ((1, heads), F32)],
        (me, sums, swapped(sums, "seq", 1)),
        "last",
    )
    return (dq[None], dk[None], dv[None], dx[None], gate.T, d_coef.reshape(width), d_rate.reshape(heads))


def solution(mesh):
    rows = P("dp", "seq", None)
    return jax.shard_map(
        on_device,
        mesh=mesh,
        in_specs=(rows, rows, rows, rows, P(), P(), P(), rows),
        out_specs=(rows, rows, rows, rows, P(), P(), P()),
        check_vma=False,
    )
```

time: 307 us -> 38.5 us (0.13)
  local copies, waits for them, and re-layouts: 73.7 us -> 0 us
  blocking collectives: 69.1 us -> 0 us
  waiting for transfers between devices: 68.4 us -> 10.9 us
  matrix products: 35.3 us -> 0 us
  other arithmetic: 27.4 us -> 0.06 us
  between operations: 15.4 us -> 0.72 us
  Pallas kernels: 0 us -> 13.3 us
    psum x1 -> x0, waiting for transfers between devices: 68.3 us -> none  [on_device(): totals = lax.psum((grads[4], grads[5], grads[6]), ('dp', 'seq'))]
    psum x1 -> x0, blocking collectives: 43.2 us -> none  [on_device(): totals = lax.psum((grads[4], grads[5], grads[6]), ('dp', 'seq'))]
    dot_general x35 -> x0, matrix products: 35.3 us -> none  [the longest x8 15 us: block_step(): jnp.einsum('thd,hde->the', q_heads.astype(jnp.float32), memory, precision...]
    while x116 -> x0, local copies, waits for them, and re-layouts: 20.7 us -> none
    all_gather x2 -> x0, blocking collectives: 18.9 us -> none  [the longest x1 9.76 us: entering(): lax.all_gather(part.astype(kind), axis)]
    pallas_call x0 -> x9, Pallas kernels: none -> 13.3 us  [call(): pl.pallas_call(kernel, out_shape=tuple((jax.ShapeDtypeStruct(*out) for ou...]
    dynamic_slice x24 -> x0, local copies, waits for them, and re-layouts: 12.9 us -> none  [the longest x18 8.46 us: local_forward(): lax.scan(block_step, memory, (query_feat.reshape(blocks, window, width_al...]
    dynamic_update_slice x28 -> x0, local copies, waits for them, and re-layouts: 12.6 us -> none  [local_forward(): lax.scan(block_step, memory, (query_feat.reshape(blocks, window, width_al...]
  transfers between devices with their start and end apart: 7 -> 12, of which waited for: 1 -> 10; matrix products, arithmetic and copies ran while one was open for 5% -> 0% of each run, Pallas kernels for 0% -> 15%
where the time goes in v1:
time: 38.5 us; the launch traced here: 38.3 us
  Pallas kernels  13.3 us (35%)
  starting transfers between devices  13.3 us (35%)
  waiting for transfers between devices  10.9 us (28%)
  between operations  0.72 us (2%)
    pallas_call x9, Pallas kernels, call(): pl.pallas_call(kernel, out_shape=tuple((jax.ShapeDtypeStruct(*out) for ou...  13.3 us
    ppermute x10, waiting for transfers between devices, swapped(): lax.ppermute(value, axis, [(i, i ^ distance) for i in range(lax.axis_size...  10.4 us
    ppermute x10, starting transfers between devices, swapped(): lax.ppermute(value, axis, [(i, i ^ distance) for i in range(lax.axis_size...  8.92 us
    ppermute x2, starting transfers between devices, inner_swapped(): return lax.ppermute(value, EVERYONE, pairs)  4.37 us
  transfers between devices with their start and end apart: 12, of which 10 were waited for; matrix products, arithmetic and copies ran while one was open for 0% of the time, Pallas kernels for 15%

profile of v1, /device:TPU:0, one launch (start us, length us, event | category | flops | bytes accessed | tf_op | source)
XLA Modules:
  0.0 38.3 jit_solution(4523343496753521772)
XLA Ops:
  0.6 2.9 %prep.1 = (bf16[128,1024]{1,0:T(8,128)(2,1)S(1)}, bf16[128,1024]{1,0:T(8,128)(2,1)S(1)}, f32[128,128]{1,0:T(8,128)S(1)}, bf16[208,1024]{1,0:T(8,128)(2,1)S(1)}, ...) custom-call(s32[1]{0:T(128)} %bitcast.me_ref, ...), custom_call_target="tpu_custom_call" | custom-call | flops 100000000 | bytes 3000000 | tf_op jit(solution)/shard_map/prep/pallas_call | solution.py:549
  3.5 0.5 %collective-permute-start = (bf16[208,1024]{1,0:T(8,128)(2,1)S(1)}, bf16[208,1024]{1,0:T(8,128)(2,1)S(1)}, u32[]{:S(2)}, u32[]{:S(2)}) collective-permute-start(bf16[208,1024]{1,0:T(8,128)(2,1)S(1)} %get-tuple-element.58), channel_id=1, source_target_pairs={{0,1},{1,0},{2,3},{3,2},{4,5},{5,4},{6,7},{7,6},{8,9},{9,8},{10,11... | collective-permute-start | bytes 1277960 | tf_op jit(solution)/shard_map/ppermute | solution.py:567
  4.0 2.6 %collective-permute-start.1 = (bf16[144,1024]{1,0:T(8,128)(2,1)S(1)}, bf16[144,1024]{1,0:T(8,128)(2,1)S(1)}, u32[]{:S(2)}, u32[]{:S(2)}) collective-permute-start(bf16[144,1024]{1,0:T(8,128)(2,1)S(1)} %get-tuple-element.59), channel_id=1, source_target_pairs={{0,4},{1,2},{2,1},{3,7},{4,0},{5,6},{6,5},{7,3},{8,12},{9,10},{10,... | collective-permute-start | bytes 884744 | tf_op jit(solution)/shard_map/ppermute | solution.py:577
  6.7 0.0 collective-permute-done.rim_ref.near_ref
  6.7 0.5 %join_near.1 = (f32[64,1024]{1,0:T(8,128)S(1)}, bf16[64,1024]{1,0:T(8,128)(2,1)S(1)}) custom-call(s32[1]{0:T(128)} %bitcast.me_ref, f32[128,128]{1,0:T(8,128)S(1)} %get-tuple-element.55.small_ref.own_ref.edge_ref, f32[128,128]{1,0:T(8,128)S(1)} %get-tuple-element.55.small_ref.own_ref.edge_ref, f32[128,128]{1,0:T(8,128)S(1)} %get-tuple-element.55.small_ref.own_ref.edge_ref, ...), custom_call_target="tpu_custom_call" | custom-call | flops 100000000 | bytes 3000000 | tf_op jit(solution)/shard_map/join_near/pallas_call | solution.py:549
  7.2 1.8 %collective-permute-start.2 = (bf16[64,1024]{1,0:T(8,128)(2,1)S(1)}, bf16[64,1024]{1,0:T(8,128)(2,1)S(1)}, u32[]{:S(2)}, u32[]{:S(2)}) collective-permute-start(bf16[64,1024]{1,0:T(8,128)(2,1)S(1)} %get-tuple-element.74), channel_id=1, source_target_pairs={{0,4},{1,2},{2,1},{3,7},{4,0},{5,6},{6,5},{7,3},{8,12},{9,10},{10,... | collective-permute-start | bytes 393224 | tf_op jit(solution)/shard_map/ppermute | solution.py:577
  8.9 1.8 %own.1 = (f32[128,1024]{1,0:T(8,128)S(1)}, f32[128,1024]{1,0:T(8,128)S(1)}, f32[128,1024]{1,0:T(8,128)S(1)}, f32[128,16]{1,0:T(8,128)S(1)}) custom-call(s32[1]{0:T(128)} %bitcast.me_ref, f32[128,128]{1,0:T(8,128)S(1)} %get-tuple-element.55.small_ref.own_ref.edge_ref, bf16[128,1024]{1,0:T(8,128)(2,1)S(1)} %get-tuple-element.56.wk_ref, ...), custom_call_target="tpu_custom_call" | custom-call | flops 700000000 | bytes 7000000 | tf_op jit(solution)/shard_map/own/pallas_call | solution.py:549
  10.8 1.5 %edge_near.1 = (f32[64,1024]{1,0:T(8,128)S(1)}, f32[64,1024]{1,0:T(8,128)S(1)}, f32[64,16]{1,0:T(8,128)S(1)}, f32[400,1024]{1,0:T(8,128)S(1)}) custom-call(s32[1]{0:T(128)} %bitcast.me_ref, f32[128,128]{1,0:T(8,128)S(1)} %get-tuple-element.55.small_ref.own_ref.edge_ref, bf16[128,1024]{1,0:T(8,128)(2,1)S(1)} %get-tuple-element.56.wk_ref, ...), custom_call_target="tpu_custom_call" | custom-call | flops 200000000 | bytes 5000000 | tf_op jit(solution)/shard_map/edge_near/pallas_call | solution.py:549
  12.3 0.5 %collective-permute-done.2.rest_0_.cross_ref = bf16[64,1024]{1,0:T(8,128)(2,1)S(1)} collective-permute-done((bf16[64,1024]{1,0:T(8,128)(2,1)S(1)}, bf16[64,1024]{1,0:T(8,128)(2,1)S(1)}, u32[]{:S(2)}, u32[]{:S(2)}) %collective-permute-start.2) | collective-permute-done | bytes 131104 | tf_op jit(solution)/shard_map/ppermute | solution.py:577
  12.8 0.5 %join_far.1 = (f32[64,1024]{1,0:T(8,128)S(1)}, bf16[64,1024]{1,0:T(8,128)(2,1)S(1)}) custom-call(s32[1]{0:T(128)} %bitcast.me_ref, f32[128,16]{1,0:T(8,128)S(1)} %get-tuple-element.64.own_ref.dl_ref, f32[64,16]{1,0:T(8,128)S(1)} %get-tuple-element.68.edge_ref.near_dl_ref, f32[128,128]{1,0:T(8,128)S(1)} %get-tuple-element.55.small_ref.own_ref.edge_ref, ...), custom_call_target="tpu_custom_call" | custom-call | flops 100000000 | bytes 3000000 | tf_op jit(solution)/shard_map/join_far/pallas_call | solution.py:549
  13.3 0.1 collective-permute-start.3
  13.4 1.1 %edge_far.1 = (f32[64,1024]{1,0:T(8,128)S(1)}, f32[64,1024]{1,0:T(8,128)S(1)}, f32[64,16]{1,0:T(8,128)S(1)}) custom-call(s32[1]{0:T(128)} %bitcast.me_ref, f32[128,128]{1,0:T(8,128)S(1)} %get-tuple-element.55.small_ref.own_ref.edge_ref, bf16[128,1024]{1,0:T(8,128)(2,1)S(1)} %get-tuple-element.56.wk_ref, bf16[128,1024]{1,0:T(8,128)(2,1)S(1)} %get-tuple-element.57.qf_ref, ...), custom_call_target="tpu_custom_call" | custom-call | flops 200000000 | bytes 3000000 | tf_op jit(solution)/shard_map/edge_far/pallas_call | solution.py:549
  14.5 0.2 collective-permute-done.3.passed_ref
  14.7 3.4 %finish.1 = (bf16[128,1024]{1,0:T(8,128)(2,1)}, bf16[128,1024]{1,0:T(8,128)(2,1)}, bf16[128,1024]{1,0:T(8,128)(2,1)}, f32[128,32]{1,0:T(8,128)S(1)}, bf16[144,12...) custom-call(s32[1]{0:T(128)} %bitcast.me_ref, bf16[128,1024]{1,0:T(8,128)(2,1)S(1)} %get-tuple-element.48.q_ref, ...), custom_call_target="tpu_custom_call" | custom-call | flops 100000000 | bytes 3000000 | tf_op jit(solution)/shard_map/finish/pallas_call | solution.py:549
  18.1 0.2 collective-permute-start.4
  18.3 1.1 %collective-permute-done.4 = bf16[144,128]{1,0:T(8,128)(2,1)S(1)} collective-permute-done((bf16[144,128]{1,0:T(8,128)(2,1)S(1)}, bf16[144,128]{1,0:T(8,128)(2,1)S(1)}, u32[]{:S(2)}, u32[]{:S(2)}) %collective-permute-start.4) | collective-permute-done | bytes 36896 | tf_op jit(solution)/shard_map/ppermute | solution.py:567
  19.4 2.4 %collective-permute-start.7 = (bf16[144,128]{1,0:T(8,128)(2,1)S(1)}, bf16[144,128]{1,0:T(8,128)(2,1)S(1)}, u32[]{:S(2)}, u32[]{:S(2)}) collective-permute-start(bf16[144,128]{1,0:T(8,128)(2,1)S(1)} %add_convert_fusion), channel_id=1, source_target_pairs={{0,6},{1,7},{2,4},{3,5},{4,2},{5,3},{6,0},{7,1},{8,14},{9,15},{10,... | collective-permute-start | bytes 110600 | tf_op jit(solution)/shard_map/ppermute | solution.py:567
  21.8 0.5 %collective-permute-start.6 = (bf16[144,128]{1,0:T(8,128)(2,1)S(1)}, bf16[144,128]{1,0:T(8,128)(2,1)S(1)}, u32[]{:S(2)}, u32[]{:S(2)}) collective-permute-start(bf16[144,128]{1,0:T(8,128)(2,1)S(1)} %add_convert_fusion), channel_id=1, source_target_pairs={{0,4},{1,5},{2,6},{3,7},{4,0},{5,1},{6,2},{7,3},{8,12},{9,13},{10,... | collective-permute-start | bytes 110600 | tf_op jit(solution)/shard_map/ppermute | solution.py:567
  22.3 0.6 %collective-permute-start.5 = (bf16[144,128]{1,0:T(8,128)(2,1)S(1)}, bf16[144,128]{1,0:T(8,128)(2,1)S(1)}, u32[]{:S(2)}, u32[]{:S(2)}) collective-permute-start(bf16[144,128]{1,0:T(8,128)(2,1)S(1)} %add_convert_fusion), channel_id=1, source_target_pairs={{0,2},{1,3},{2,0},{3,1},{4,6},{5,7},{6,4},{7,5},{8,10},{9,11},{10,... | collective-permute-start | bytes 110600 | tf_op jit(solution)/shard_map/ppermute | solution.py:567
  22.9 1.0 %inputs.1 = bf16[128,1024]{1,0:T(8,128)(2,1)} custom-call(s32[1]{0:T(128)} %bitcast.me_ref, f32[128,32]{1,0:T(8,128)S(1)} %get-tuple-element.82.logits_ref, f32[32,1024]{1,0:T(8,128)S(1)} %get-tuple-element.83.w_ref), custom_call_target="tpu_custom_call" | custom-call | flops 100000000 | bytes 3000000 | tf_op jit(solution)/shard_map/inputs/pallas_call | solution.py:549
  23.9 0.4 %collective-permute-done.7 = bf16[144,128]{1,0:T(8,128)(2,1)S(1)} collective-permute-done((bf16[144,128]{1,0:T(8,128)(2,1)S(1)}, bf16[144,128]{1,0:T(8,128)(2,1)S(1)}, u32[]{:S(2)}, u32[]{:S(2)}) %collective-permute-start.7) | collective-permute-done | bytes 36896 | tf_op jit(solution)/shard_map/ppermute | solution.py:567
  24.3 1.5 %collective-permute-done.6 = bf16[144,128]{1,0:T(8,128)(2,1)S(1)} collective-permute-done((bf16[144,128]{1,0:T(8,128)(2,1)S(1)}, bf16[144,128]{1,0:T(8,128)(2,1)S(1)}, u32[]{:S(2)}, u32[]{:S(2)}) %collective-permute-start.6) | collective-permute-done | bytes 36896 | tf_op jit(solution)/shard_map/ppermute | solution.py:567
  25.8 0.5 %collective-permute-done.5 = bf16[144,128]{1,0:T(8,128)(2,1)S(1)} collective-permute-done((bf16[144,128]{1,0:T(8,128)(2,1)S(1)}, bf16[144,128]{1,0:T(8,128)(2,1)S(1)}, u32[]{:S(2)}, u32[]{:S(2)}) %collective-permute-start.5) | collective-permute-done | bytes 36896 | tf_op jit(solution)/shard_map/ppermute | solution.py:567
  26.3 2.7 %collective-permute-start.9 = (bf16[144,128]{1,0:T(8,128)(2,1)S(1)}, bf16[144,128]{1,0:T(8,128)(2,1)S(1)}, u32[]{:S(2)}, u32[]{:S(2)}) collective-permute-start(bf16[144,128]{1,0:T(8,128)(2,1)S(1)} %add_add_fusion.1), channel_id=1, source_target_pairs={{0,16},{1,17},{2,18},{3,19},{4,20},{5,21},{6,22},{7,23},{8,24},{9,... | collective-permute-start | bytes 110600 | tf_op jit(solution)/shard_map/ppermute | solution.py:567
  29.0 1.6 %collective-permute-start.8 = (bf16[144,128]{1,0:T(8,128)(2,1)S(1)}, bf16[144,128]{1,0:T(8,128)(2,1)S(1)}, u32[]{:S(2)}, u32[]{:S(2)}) collective-permute-start(bf16[144,128]{1,0:T(8,128)(2,1)S(1)} %add_add_fusion.1), channel_id=1, source_target_pairs={{0,8},{1,9},{2,10},{3,11},{4,12},{5,13},{6,14},{7,15},{8,0},{9,1},... | collective-permute-start | bytes 110600 | tf_op jit(solution)/shard_map/ppermute | solution.py:567
  30.5 0.2 collective-permute-start.10
  30.8 0.5 %collective-permute-done.9 = bf16[144,128]{1,0:T(8,128)(2,1)S(1)} collective-permute-done((bf16[144,128]{1,0:T(8,128)(2,1)S(1)}, bf16[144,128]{1,0:T(8,128)(2,1)S(1)}, u32[]{:S(2)}, u32[]{:S(2)}) %collective-permute-start.9) | collective-permute-done | bytes 36896 | tf_op jit(solution)/shard_map/ppermute | solution.py:567
  31.2 1.7 %collective-permute-done.8 = bf16[144,128]{1,0:T(8,128)(2,1)S(1)} collective-permute-done((bf16[144,128]{1,0:T(8,128)(2,1)S(1)}, bf16[144,128]{1,0:T(8,128)(2,1)S(1)}, u32[]{:S(2)}, u32[]{:S(2)}) %collective-permute-start.8) | collective-permute-done | bytes 36896 | tf_op jit(solution)/shard_map/ppermute | solution.py:567
  32.9 3.4 %collective-permute-done.10 = bf16[144,128]{1,0:T(8,128)(2,1)S(1)} collective-permute-done((bf16[144,128]{1,0:T(8,128)(2,1)S(1)}, bf16[144,128]{1,0:T(8,128)(2,1)S(1)}, u32[]{:S(2)}, u32[]{:S(2)}) %collective-permute-start.10) | collective-permute-done | bytes 36896 | tf_op jit(solution)/shard_map/ppermute | solution.py:567
  36.3 0.1 collective-permute-start.11
  36.4 1.3 %collective-permute-done.11.theirs_ref = f32[144,128]{1,0:T(8,128)S(1)} collective-permute-done((f32[144,128]{1,0:T(8,128)S(1)}, f32[144,128]{1,0:T(8,128)S(1)}, u32[]{:S(2)}, u32[]{:S(2)}) %collective-permute-start.11) | collective-permute-done | bytes 73760 | tf_op jit(solution)/shard_map/ppermute | solution.py:567
  37.7 0.7 %last.1 = (f32[32,1024]{1,0:T(8,128)}, f32[1,1024]{1,0:T(1,128)}, f32[1,16]{1,0:T(1,128)}) custom-call(s32[1]{0:T(128)} %bitcast.me_ref, f32[144,128]{1,0:T(8,128)S(1)} %add_add_fusion.mine_ref, f32[144,128]{1,0:T(8,128)S(1)} %collective-permute-done.11.theirs_ref), custom_call_target="tpu_custom_call" | custom-call | flops 100000000 | bytes 3000000 | tf_op jit(solution)/shard_map/last/pallas_call | solution.py:549
  (4 shorter events, 0.1 us)
Async XLA Ops:
  3.5 3.1 %collective-permute-start = (bf16[208,1024]{1,0:T(8,128)(2,1)S(1)}, bf16[208,1024]{1,0:T(8,128)(2,1)S(1)}, u32[]{:S(2)}, u32[]{:S(2)}) collective-permute-start(bf16[208,1024]{1,0:T(8,128)(2,1)S(1)} %get-tuple-element.58), channel_id=1, source_target_pairs={{0,1},{1,0},{2,3},{3,2},{4,5},{5,4},{6,7},{7,6},{8,9},{9,8},{10,11... | collective-permute-start | bytes 1277960 | tf_op jit(solution)/shard_map/ppermute | solution.py:567
  4.0 8.2 %collective-permute-start.1 = (bf16[144,1024]{1,0:T(8,128)(2,1)S(1)}, bf16[144,1024]{1,0:T(8,128)(2,1)S(1)}, u32[]{:S(2)}, u32[]{:S(2)}) collective-permute-start(bf16[144,1024]{1,0:T(8,128)(2,1)S(1)} %get-tuple-element.59), channel_id=1, source_target_pairs={{0,4},{1,2},{2,1},{3,7},{4,0},{5,6},{6,5},{7,3},{8,12},{9,10},{10,... | collective-permute-start | bytes 884744 | tf_op jit(solution)/shard_map/ppermute | solution.py:577
  7.2 5.6 %collective-permute-start.2 = (bf16[64,1024]{1,0:T(8,128)(2,1)S(1)}, bf16[64,1024]{1,0:T(8,128)(2,1)S(1)}, u32[]{:S(2)}, u32[]{:S(2)}) collective-permute-start(bf16[64,1024]{1,0:T(8,128)(2,1)S(1)} %get-tuple-element.74), channel_id=1, source_target_pairs={{0,4},{1,2},{2,1},{3,7},{4,0},{5,6},{6,5},{7,3},{8,12},{9,10},{10,... | collective-permute-start | bytes 393224 | tf_op jit(solution)/shard_map/ppermute | solution.py:577
  13.3 1.4 %collective-permute-start.3 = (bf16[64,1024]{1,0:T(8,128)(2,1)S(1)}, bf16[64,1024]{1,0:T(8,128)(2,1)S(1)}, u32[]{:S(2)}, u32[]{:S(2)}) collective-permute-start(bf16[64,1024]{1,0:T(8,128)(2,1)S(1)} %get-tuple-element.76), channel_id=1, source_target_pairs={{0,1},{1,0},{2,3},{3,2},{4,5},{5,4},{6,7},{7,6},{8,9},{9,8},{10,11... | collective-permute-start | bytes 393224 | tf_op jit(solution)/shard_map/ppermute | solution.py:567
  18.1 1.3 %collective-permute-start.4 = (bf16[144,128]{1,0:T(8,128)(2,1)S(1)}, bf16[144,128]{1,0:T(8,128)(2,1)S(1)}, u32[]{:S(2)}, u32[]{:S(2)}) collective-permute-start(bf16[144,128]{1,0:T(8,128)(2,1)S(1)} %get-tuple-element.81), channel_id=1, source_target_pairs={{0,1},{1,0},{2,3},{3,2},{4,5},{5,4},{6,7},{7,6},{8,9},{9,8},{10,11... | collective-permute-start | bytes 110600 | tf_op jit(solution)/shard_map/ppermute | solution.py:567
  19.4 4.9 %collective-permute-start.7 = (bf16[144,128]{1,0:T(8,128)(2,1)S(1)}, bf16[144,128]{1,0:T(8,128)(2,1)S(1)}, u32[]{:S(2)}, u32[]{:S(2)}) collective-permute-start(bf16[144,128]{1,0:T(8,128)(2,1)S(1)} %add_convert_fusion), channel_id=1, source_target_pairs={{0,6},{1,7},{2,4},{3,5},{4,2},{5,3},{6,0},{7,1},{8,14},{9,15},{10,... | collective-permute-start | bytes 110600 | tf_op jit(solution)/shard_map/ppermute | solution.py:567
  21.8 4.0 %collective-permute-start.6 = (bf16[144,128]{1,0:T(8,128)(2,1)S(1)}, bf16[144,128]{1,0:T(8,128)(2,1)S(1)}, u32[]{:S(2)}, u32[]{:S(2)}) collective-permute-start(bf16[144,128]{1,0:T(8,128)(2,1)S(1)} %add_convert_fusion), channel_id=1, source_target_pairs={{0,4},{1,5},{2,6},{3,7},{4,0},{5,1},{6,2},{7,3},{8,12},{9,13},{10,... | collective-permute-start | bytes 110600 | tf_op jit(solution)/shard_map/ppermute | solution.py:567
  22.3 4.0 %collective-permute-start.5 = (bf16[144,128]{1,0:T(8,128)(2,1)S(1)}, bf16[144,128]{1,0:T(8,128)(2,1)S(1)}, u32[]{:S(2)}, u32[]{:S(2)}) collective-permute-start(bf16[144,128]{1,0:T(8,128)(2,1)S(1)} %add_convert_fusion), channel_id=1, source_target_pairs={{0,2},{1,3},{2,0},{3,1},{4,6},{5,7},{6,4},{7,5},{8,10},{9,11},{10,... | collective-permute-start | bytes 110600 | tf_op jit(solution)/shard_map/ppermute | solution.py:567
  26.3 4.9 %collective-permute-start.9 = (bf16[144,128]{1,0:T(8,128)(2,1)S(1)}, bf16[144,128]{1,0:T(8,128)(2,1)S(1)}, u32[]{:S(2)}, u32[]{:S(2)}) collective-permute-start(bf16[144,128]{1,0:T(8,128)(2,1)S(1)} %add_add_fusion.1), channel_id=1, source_target_pairs={{0,16},{1,17},{2,18},{3,19},{4,20},{5,21},{6,22},{7,23},{8,24},{9,... | collective-permute-start | bytes 110600 | tf_op jit(solution)/shard_map/ppermute | solution.py:567
  29.0 4.0 %collective-permute-start.8 = (bf16[144,128]{1,0:T(8,128)(2,1)S(1)}, bf16[144,128]{1,0:T(8,128)(2,1)S(1)}, u32[]{:S(2)}, u32[]{:S(2)}) collective-permute-start(bf16[144,128]{1,0:T(8,128)(2,1)S(1)} %add_add_fusion.1), channel_id=1, source_target_pairs={{0,8},{1,9},{2,10},{3,11},{4,12},{5,13},{6,14},{7,15},{8,0},{9,1},... | collective-permute-start | bytes 110600 | tf_op jit(solution)/shard_map/ppermute | solution.py:567
  30.5 5.8 %collective-permute-start.10 = (bf16[144,128]{1,0:T(8,128)(2,1)S(1)}, bf16[144,128]{1,0:T(8,128)(2,1)S(1)}, u32[]{:S(2)}, u32[]{:S(2)}) collective-permute-start(bf16[144,128]{1,0:T(8,128)(2,1)S(1)} %add_add_fusion.1), channel_id=1, source_target_pairs={{0,24},{1,25},{2,26},{3,27},{4,28},{5,29},{6,30},{7,31},{8,16},{9,... | collective-permute-start | bytes 110600 | tf_op jit(solution)/shard_map/ppermute | solution.py:567
  36.3 1.3 %collective-permute-start.11 = (f32[144,128]{1,0:T(8,128)S(1)}, f32[144,128]{1,0:T(8,128)S(1)}, u32[]{:S(2)}, u32[]{:S(2)}) collective-permute-start(f32[144,128]{1,0:T(8,128)S(1)} %add_add_fusion.mine_ref), channel_id=1, source_target_pairs={{0,1},{1,0},{2,3},{3,2},{4,5},{5,4},{6,7},{7,6},{8,9},{9,8},{10,11... | collective-permute-start | bytes 221192 | tf_op jit(solution)/shard_map/ppermute | solution.py:567

commit v2 on v1

--- a/solution.py
+++ b/solution.py
@@ -63,6 +63,11 @@
 
 def stacked(z, masks):
     return jnp.concatenate([z * masks[0], z * masks[1]], axis=0)
+
+
+def stacked_group(z):
+    head = iota((1, z.shape[1]), 1) // WINDOW
+    return jnp.concatenate([z * (head == i).astype(BF16) for i in range(z.shape[1] // WINDOW)], axis=0)
 
 
 def one_above(z):
@@ -384,7 +389,7 @@
                   dqf_ref, dwk_ref, dvl_ref, dl_ref, scales_ref,
                   near_first_ref, near_second_ref, near_dl_ref, far_first_ref, far_second_ref, far_dl_ref,
                   near_part_ref, far_part_ref, cross_ref, passed_ref,
-                  dq_out, dk_out, dv_out, logits_ref, keep_ref, give_ref,
+                  dq_out, dk_out, dv_out, logits_ref, sums_ref,
                   fwd_ref, bwd_ref, rim_dq_ref, rim_dwk_ref, rim_dv_ref, rim_dl_ref,
                   dq_ref, dk_ref, dv_ref, sems):
     length, width = wk_ref.shape
@@ -401,7 +406,6 @@
     pl.when(is_odd(me_ref))(lambda: edges(*near_edge))
     pl.when(jnp.logical_not(is_odd(me_ref)))(lambda: edges(*far_edge))
     table = head_table(heads, width)
-    masks = half_masks()
     small = small_ref[...]
     total, gamma, soft, slope = (small[:, i * heads:(i + 1) * heads] for i in range(4))
     last, middle = total[length - 1:], total[late - 1:late]
@@ -436,9 +440,9 @@
 
     own_products, rim_products, out_products, key_products, d_coef = [], [], [], [], []
     coef = coef_ref[...]
-    for pair in range(pairs):
-        at = slice(pair * LANES, (pair + 1) * LANES)
-        m0, m1, a1, a0, b0 = (stacked(z[:, at], masks) for z in (start, halfway, after, half_after, later))
+    for group in range(pairs // 2):
+        at = slice(2 * group * LANES, 2 * (group + 1) * LANES)
+        m0, m1, a1, a0, b0 = (stacked_group(z[:, at]) for z in (start, halfway, after, half_after, later))
         qf, g, wk, v = qf_ref[:, at], g_ref[:, at], wk_ref[:, at], v_ref[:, at]
         from_q = jnp.concatenate([dot(qf[:late], m0), dot(qf[late:], m1)], axis=0)
         out_products.append(from_q * g.astype(F32))
@@ -463,7 +467,8 @@
         d_phi = dwk * gamma_x[:, at]
         dq_ref[:, at] = (dqf * (0.125 + 0.25 * c * q)).astype(BF16)
         dk_ref[:, at] = (d_phi * (0.125 + 0.25 * c * k)).astype(BF16)
-        d_coef.append(jnp.sum(dqf * (0.125 * q * q) + d_phi * (0.125 * k * k), axis=0, keepdims=True))
+        row = jnp.sum(dqf * (0.125 * q * q) + d_phi * (0.125 * k * k), axis=0, keepdims=True)
+        d_coef += [row[:, :LANES], row[:, LANES:]]
 
     copies = [
         pltpu.make_async_copy(source, target, sems.at[i])
@@ -496,19 +501,10 @@
     logits_ref[...] = d_logits
     gate = dot_tn(d_logits.astype(BF16), x_ref[...])
     d_rate = jnp.concatenate([d_rate, jnp.zeros((1, LANES - heads), F32)], axis=1)
-    halves = []
-    for half in range(2):
-        blocks = range(half * pairs // 2, (half + 1) * pairs // 2)
-        rest = [d_coef[i] for i in blocks] + [d_rate, jnp.zeros((BAND - 1 - len(blocks), LANES), F32)]
-        rows = [gate[:, i * LANES:(i + 1) * LANES] for i in blocks]
-        halves.append(jnp.concatenate(rows + rest, axis=0).astype(BF16))
-
-    def give(mine, theirs):
-        keep_ref[...] = mine
-        give_ref[...] = theirs
-
-    pl.when(is_odd(me_ref))(lambda: give(halves[1], halves[0]))
-    pl.when(jnp.logical_not(is_odd(me_ref)))(lambda: give(halves[0], halves[1]))
+    for i in range(pairs):
+        sums_ref[i * 2 * heads:(i + 1) * 2 * heads] = gate[:, i * LANES:(i + 1) * LANES].astype(BF16)
+    rest = d_coef + [d_rate, jnp.zeros((BAND - 1 - pairs, LANES), F32)]
+    sums_ref[pairs * 2 * heads:] = jnp.concatenate(rest, axis=0).astype(BF16)
     for copy in copies:
         copy.wait()
 
@@ -523,17 +519,18 @@
 
 
 def last_kernel(heads, me_ref, mine_ref, theirs_ref, gate_ref, coef_ref, rate_ref):
-    odd = jnp.full(mine_ref.shape, jax.lax.rem(me_ref[0], 2)) == 1
-    mine, theirs = mine_ref[...], theirs_ref[...]
-    halves = [jnp.where(odd, theirs, mine), jnp.where(odd, mine, theirs)]
-    blocks = gate_ref.shape[1] // LANES // 2
-    for half in range(2):
+    blocks = gate_ref.shape[1] // LANES
+
+    def write(sums_ref):
         for i in range(blocks):
-            at = slice((half * blocks + i) * LANES, (half * blocks + i + 1) * LANES)
-            gate_ref[:, at] = halves[half][i * 2 * heads:(i + 1) * 2 * heads]
-            coef_ref[:, at] = halves[half][blocks * 2 * heads + i:blocks * 2 * heads + i + 1]
-    at = blocks * (2 * heads + 1)
-    rate_ref[...] = halves[0][at:at + 1, :heads]
+            at = slice(i * LANES, (i + 1) * LANES)
+            gate_ref[:, at] = sums_ref[i * 2 * heads:(i + 1) * 2 * heads]
+            coef_ref[:, at] = sums_ref[blocks * 2 * heads + i:blocks * 2 * heads + i + 1]
+        at = blocks * (2 * heads + 1)
+        rate_ref[...] = sums_ref[at:at + 1, :heads]
+
+    pl.when(is_odd(me_ref))(lambda: write(mine_ref))
+    pl.when(jnp.logical_not(is_odd(me_ref)))(lambda: write(theirs_ref))
 
 
 def call(kernel, outs, operands, name, scratch=(), in_place=(), outside=(), flops=10**8, moved=3 * 10**6):
@@ -567,6 +564,12 @@
     return lax.ppermute(value, axis, [(i, i ^ distance) for i in range(lax.axis_size(axis))])
 
 
+def odd_swapped(value, distance, stage):
+    count = lax.axis_size(EVERYONE)
+    idle = 8 if stage == 2 and count > 8 else 4
+    return lax.ppermute(value, EVERYONE, [(i, i ^ (distance if i % 2 else idle)) for i in range(count)])
+
+
 def inner_swapped(value):
     dp, seq = (lax.axis_size(axis) for axis in EVERYONE)
     pairs = []
@@ -638,10 +641,10 @@
         flops=2 * 10**8,
         moved=3 * 10**6,
     )
-    half_sums = ((width // LANES // 2 * 2 * heads + BAND, LANES), BF16)
-    dq, dk, dv, d_logits, keep, give = call(
+    all_sums = ((width // LANES * 2 * heads + BAND, LANES), BF16)
+    dq, dk, dv, d_logits, sums = call(
         functools.partial(finish_kernel, heads, count),
-        [wide, wide, wide, ((length, 2 * heads), F32), half_sums, half_sums],
+        [wide, wide, wide, ((length, 2 * heads), F32), all_sums],
         (me, q, k, x, v, g, coef, rate, gates, wk, qf, near, far, adjoint, *own, scales, *near_edge, *far_edge,
          near_part, far_part, cross, passed),
         "finish",
@@ -650,15 +653,15 @@
         outside=range(3),
     )
     dx = call(inputs_kernel, [wide], (me, d_logits, wt), "inputs")[0]
-    sums = keep.astype(F32) + swapped(give, EVERYONE, 1).astype(F32)
+    sums = sums.astype(F32) + swapped(sums, EVERYONE, 1).astype(F32)
     distance = 2
     while distance < lax.axis_size(EVERYONE):
         sums = sums.astype(BF16)
         if 2 * distance < lax.axis_size(EVERYONE):
-            far, mid, one = (swapped(sums, EVERYONE, i * distance).astype(F32) for i in (3, 2, 1))
+            far, mid, one = (odd_swapped(sums, i * distance, distance).astype(F32) for i in (3, 2, 1))
             sums = (sums.astype(F32) + one) + (mid + far)
         else:
-            sums = sums.astype(F32) + swapped(sums, EVERYONE, distance).astype(F32)
+            sums = sums.astype(F32) + odd_swapped(sums, distance, distance).astype(F32)
         if distance == 2:
             sums, dx = lax.optimization_barrier((sums, dx))
         distance *= 4

time: 38.5 us -> 35.9 us (0.932)
  waiting for transfers between devices: 10.9 us -> 7.94 us
    ppermute x10 -> x4, waiting for transfers between devices: 10.4 us -> 2.31 us  [swapped(): lax.ppermute(value, axis, [(i, i ^ distance) for i in range(lax.axis_size...]
    ppermute x0 -> x6, starting transfers between devices: none -> 7.77 us  [odd_swapped(): lax.ppermute(value, EVERYONE, [(i, i ^ (distance if i % 2 else idle)) for...]
    ppermute x10 -> x4, starting transfers between devices: 8.92 us -> 1.45 us  [swapped(): lax.ppermute(value, axis, [(i, i ^ distance) for i in range(lax.axis_size...]
    ppermute x0 -> x6, waiting for transfers between devices: none -> 5.08 us  [odd_swapped(): lax.ppermute(value, EVERYONE, [(i, i ^ (distance if i % 2 else idle)) for...]
  transfers between devices with their start and end apart: 12 -> 12, of which waited for: 10 -> 9; matrix products, arithmetic and copies ran while one was open for 0% -> 0% of each run, Pallas kernels for 15% -> 16%
where the time goes in v2:
time: 35.9 us; the launch traced here: 35.7 us
  starting transfers between devices  13.6 us (38%)
  Pallas kernels  13.4 us (37%)
  waiting for transfers between devices  7.94 us (22%)
  between operations  0.71 us (2%)
    pallas_call x9, Pallas kernels, call(): pl.pallas_call(kernel, out_shape=tuple((jax.ShapeDtypeStruct(*out) for ou...  13.4 us
    ppermute x6, starting transfers between devices, odd_swapped(): lax.ppermute(value, EVERYONE, [(i, i ^ (distance if i % 2 else idle)) for...  7.77 us
    ppermute x6, waiting for transfers between devices, odd_swapped(): lax.ppermute(value, EVERYONE, [(i, i ^ (distance if i % 2 else idle)) for...  5.08 us
    ppermute x2, starting transfers between devices, inner_swapped(): return lax.ppermute(value, EVERYONE, pairs)  4.37 us
    ppermute x4, waiting for transfers between devices, swapped(): lax.ppermute(value, axis, [(i, i ^ distance) for i in range(lax.axis_size...  2.31 us
    ppermute x4, starting transfers between devices, swapped(): lax.ppermute(value, axis, [(i, i ^ distance) for i in range(lax.axis_size...  1.45 us
  transfers between devices with their start and end apart: 12, of which 9 were waited for; matrix products, arithmetic and copies ran while one was open for 0% of the time, Pallas kernels for 16%

profile of v2, /device:TPU:0, one launch (start us, length us, event | category | flops | bytes accessed | tf_op | source)
XLA Modules:
  0.0 35.7 jit_solution(18167057433437788727)
XLA Ops:
  0.6 2.9 %prep.1 = (bf16[128,1024]{1,0:T(8,128)(2,1)S(1)}, bf16[128,1024]{1,0:T(8,128)(2,1)S(1)}, f32[128,128]{1,0:T(8,128)S(1)}, bf16[208,1024]{1,0:T(8,128)(2,1)S(1)}, ...) custom-call(s32[1]{0:T(128)} %bitcast.me_ref, ...), custom_call_target="tpu_custom_call" | custom-call | flops 100000000 | bytes 3000000 | tf_op jit(solution)/shard_map/prep/pallas_call | solution.py:546
  3.5 0.5 %collective-permute-start = (bf16[208,1024]{1,0:T(8,128)(2,1)S(1)}, bf16[208,1024]{1,0:T(8,128)(2,1)S(1)}, u32[]{:S(2)}, u32[]{:S(2)}) collective-permute-start(bf16[208,1024]{1,0:T(8,128)(2,1)S(1)} %get-tuple-element.57), channel_id=1, source_target_pairs={{0,1},{1,0},{2,3},{3,2},{4,5},{5,4},{6,7},{7,6},{8,9},{9,8},{10,11... | collective-permute-start | bytes 1277960 | tf_op jit(solution)/shard_map/ppermute | solution.py:564
  4.0 2.6 %collective-permute-start.1 = (bf16[144,1024]{1,0:T(8,128)(2,1)S(1)}, bf16[144,1024]{1,0:T(8,128)(2,1)S(1)}, u32[]{:S(2)}, u32[]{:S(2)}) collective-permute-start(bf16[144,1024]{1,0:T(8,128)(2,1)S(1)} %get-tuple-element.58), channel_id=1, source_target_pairs={{0,4},{1,2},{2,1},{3,7},{4,0},{5,6},{6,5},{7,3},{8,12},{9,10},{10,... | collective-permute-start | bytes 884744 | tf_op jit(solution)/shard_map/ppermute | solution.py:580
  6.7 0.5 %join_near.1 = (f32[64,1024]{1,0:T(8,128)S(1)}, bf16[64,1024]{1,0:T(8,128)(2,1)S(1)}) custom-call(s32[1]{0:T(128)} %bitcast.me_ref, f32[128,128]{1,0:T(8,128)S(1)} %get-tuple-element.54.small_ref.own_ref.edge_ref, f32[128,128]{1,0:T(8,128)S(1)} %get-tuple-element.54.small_ref.own_ref.edge_ref, f32[128,128]{1,0:T(8,128)S(1)} %get-tuple-element.54.small_ref.own_ref.edge_ref, ...), custom_call_target="tpu_custom_call" | custom-call | flops 100000000 | bytes 3000000 | tf_op jit(solution)/shard_map/join_near/pallas_call | solution.py:546
  7.2 1.8 %collective-permute-start.2 = (bf16[64,1024]{1,0:T(8,128)(2,1)S(1)}, bf16[64,1024]{1,0:T(8,128)(2,1)S(1)}, u32[]{:S(2)}, u32[]{:S(2)}) collective-permute-start(bf16[64,1024]{1,0:T(8,128)(2,1)S(1)} %get-tuple-element.73), channel_id=1, source_target_pairs={{0,4},{1,2},{2,1},{3,7},{4,0},{5,6},{6,5},{7,3},{8,12},{9,10},{10,... | collective-permute-start | bytes 393224 | tf_op jit(solution)/shard_map/ppermute | solution.py:580
  8.9 1.8 %own.1 = (f32[128,1024]{1,0:T(8,128)S(1)}, f32[128,1024]{1,0:T(8,128)S(1)}, f32[128,1024]{1,0:T(8,128)S(1)}, f32[128,16]{1,0:T(8,128)S(1)}) custom-call(s32[1]{0:T(128)} %bitcast.me_ref, f32[128,128]{1,0:T(8,128)S(1)} %get-tuple-element.54.small_ref.own_ref.edge_ref, bf16[128,1024]{1,0:T(8,128)(2,1)S(1)} %get-tuple-element.55.wk_ref, ...), custom_call_target="tpu_custom_call" | custom-call | flops 700000000 | bytes 7000000 | tf_op jit(solution)/shard_map/own/pallas_call | solution.py:546
  10.8 1.5 %edge_near.1 = (f32[64,1024]{1,0:T(8,128)S(1)}, f32[64,1024]{1,0:T(8,128)S(1)}, f32[64,16]{1,0:T(8,128)S(1)}, f32[400,1024]{1,0:T(8,128)S(1)}) custom-call(s32[1]{0:T(128)} %bitcast.me_ref, f32[128,128]{1,0:T(8,128)S(1)} %get-tuple-element.54.small_ref.own_ref.edge_ref, bf16[128,1024]{1,0:T(8,128)(2,1)S(1)} %get-tuple-element.55.wk_ref, ...), custom_call_target="tpu_custom_call" | custom-call | flops 200000000 | bytes 5000000 | tf_op jit(solution)/shard_map/edge_near/pallas_call | solution.py:546
  12.2 0.0 collective-permute-done.1.rim_ref.far_ref
  12.2 0.5 %collective-permute-done.2.rest_0_.cross_ref = bf16[64,1024]{1,0:T(8,128)(2,1)S(1)} collective-permute-done((bf16[64,1024]{1,0:T(8,128)(2,1)S(1)}, bf16[64,1024]{1,0:T(8,128)(2,1)S(1)}, u32[]{:S(2)}, u32[]{:S(2)}) %collective-permute-start.2) | collective-permute-done | bytes 131104 | tf_op jit(solution)/shard_map/ppermute | solution.py:580
  12.8 0.5 %join_far.1 = (f32[64,1024]{1,0:T(8,128)S(1)}, bf16[64,1024]{1,0:T(8,128)(2,1)S(1)}) custom-call(s32[1]{0:T(128)} %bitcast.me_ref, f32[128,16]{1,0:T(8,128)S(1)} %get-tuple-element.63.own_ref.dl_ref, f32[64,16]{1,0:T(8,128)S(1)} %get-tuple-element.67.edge_ref.near_dl_ref, f32[128,128]{1,0:T(8,128)S(1)} %get-tuple-element.54.small_ref.own_ref.edge_ref, ...), custom_call_target="tpu_custom_call" | custom-call | flops 100000000 | bytes 3000000 | tf_op jit(solution)/shard_map/join_far/pallas_call | solution.py:546
  13.3 0.1 collective-permute-start.3
  13.4 1.1 %edge_far.1 = (f32[64,1024]{1,0:T(8,128)S(1)}, f32[64,1024]{1,0:T(8,128)S(1)}, f32[64,16]{1,0:T(8,128)S(1)}) custom-call(s32[1]{0:T(128)} %bitcast.me_ref, f32[128,128]{1,0:T(8,128)S(1)} %get-tuple-element.54.small_ref.own_ref.edge_ref, bf16[128,1024]{1,0:T(8,128)(2,1)S(1)} %get-tuple-element.55.wk_ref, bf16[128,1024]{1,0:T(8,128)(2,1)S(1)} %get-tuple-element.56.qf_ref, ...), custom_call_target="tpu_custom_call" | custom-call | flops 200000000 | bytes 3000000 | tf_op jit(solution)/shard_map/edge_far/pallas_call | solution.py:546
  14.5 0.2 collective-permute-done.3.passed_ref
  14.7 3.4 %finish.1 = (bf16[128,1024]{1,0:T(8,128)(2,1)}, bf16[128,1024]{1,0:T(8,128)(2,1)}, bf16[128,1024]{1,0:T(8,128)(2,1)}, f32[128,32]{1,0:T(8,128)S(1)}, bf16[272,128]{1,0:T(8,128)(2,1)S(1)}) custom-call(s32[1]{0:T(128)} %bitcast.me_ref, bf16[128,1024]{1,0:T(8,128)(2,1)S(1)} %get-tuple-element.47.q_ref, bf16[128,1024]{1,0:T(8,128)(2,1)S(1)} %get-tuple-element.48.k_ref, ...), custom_call_target="tpu_custom_call" | custom-call | flops 100000000 | bytes 3000000 | tf_op jit(solution)/shard_map/finish/pallas_call | solution.py:546
  18.2 0.2 collective-permute-start.4
  18.4 1.1 %collective-permute-done.4 = bf16[272,128]{1,0:T(8,128)(2,1)S(1)} collective-permute-done((bf16[272,128]{1,0:T(8,128)(2,1)S(1)}, bf16[272,128]{1,0:T(8,128)(2,1)S(1)}, u32[]{:S(2)}, u32[]{:S(2)}) %collective-permute-start.4) | collective-permute-done | bytes 69664 | tf_op jit(solution)/shard_map/ppermute | solution.py:564
  19.5 2.1 %collective-permute-start.7 = (bf16[272,128]{1,0:T(8,128)(2,1)S(1)}, bf16[272,128]{1,0:T(8,128)(2,1)S(1)}, u32[]{:S(2)}, u32[]{:S(2)}) collective-permute-start(bf16[272,128]{1,0:T(8,128)(2,1)S(1)} %add_convert_fusion), channel_id=1, source_target_pairs={{0,8},{1,7},{2,10},{3,5},{4,12},{5,3},{6,14},{7,1},{8,0},{9,15},{1... | collective-permute-start | bytes 208904 | tf_op jit(solution)/shard_map/ppermute | solution.py:570
  21.6 0.1 collective-permute-start.6
  21.7 1.9 %collective-permute-start.5 = (bf16[272,128]{1,0:T(8,128)(2,1)S(1)}, bf16[272,128]{1,0:T(8,128)(2,1)S(1)}, u32[]{:S(2)}, u32[]{:S(2)}) collective-permute-start(bf16[272,128]{1,0:T(8,128)(2,1)S(1)} %add_convert_fusion), channel_id=1, source_target_pairs={{0,8},{1,3},{2,10},{3,1},{4,12},{5,7},{6,14},{7,5},{8,0},{9,11},{1... | collective-permute-start | bytes 208904 | tf_op jit(solution)/shard_map/ppermute | solution.py:570
  23.7 1.0 %inputs.1 = bf16[128,1024]{1,0:T(8,128)(2,1)} custom-call(s32[1]{0:T(128)} %bitcast.me_ref, f32[128,32]{1,0:T(8,128)S(1)} %get-tuple-element.80.logits_ref, f32[32,1024]{1,0:T(8,128)S(1)} %get-tuple-element.81.w_ref), custom_call_target="tpu_custom_call" | custom-call | flops 100000000 | bytes 3000000 | tf_op jit(solution)/shard_map/inputs/pallas_call | solution.py:546
  24.7 0.0 collective-permute-done.7
  24.7 1.3 %collective-permute-done.6 = bf16[272,128]{1,0:T(8,128)(2,1)S(1)} collective-permute-done((bf16[272,128]{1,0:T(8,128)(2,1)S(1)}, bf16[272,128]{1,0:T(8,128)(2,1)S(1)}, u32[]{:S(2)}, u32[]{:S(2)}) %collective-permute-start.6) | collective-permute-done | bytes 69664 | tf_op jit(solution)/shard_map/ppermute | solution.py:570
  26.0 0.7 %collective-permute-done.5 = bf16[272,128]{1,0:T(8,128)(2,1)S(1)} collective-permute-done((bf16[272,128]{1,0:T(8,128)(2,1)S(1)}, bf16[272,128]{1,0:T(8,128)(2,1)S(1)}, u32[]{:S(2)}, u32[]{:S(2)}) %collective-permute-start.5) | collective-permute-done | bytes 69664 | tf_op jit(solution)/shard_map/ppermute | solution.py:570
  26.8 1.6 %collective-permute-start.9 = (bf16[272,128]{1,0:T(8,128)(2,1)S(1)}, bf16[272,128]{1,0:T(8,128)(2,1)S(1)}, u32[]{:S(2)}, u32[]{:S(2)}) collective-permute-start(bf16[272,128]{1,0:T(8,128)(2,1)S(1)} %add_add_fusion.1), channel_id=1, source_target_pairs={{0,4},{1,17},{2,6},{3,19},{4,0},{5,21},{6,2},{7,23},{8,12},{9,25},... | collective-permute-start | bytes 208904 | tf_op jit(solution)/shard_map/ppermute | solution.py:570
  28.3 0.5 %collective-permute-start.8 = (bf16[272,128]{1,0:T(8,128)(2,1)S(1)}, bf16[272,128]{1,0:T(8,128)(2,1)S(1)}, u32[]{:S(2)}, u32[]{:S(2)}) collective-permute-start(bf16[272,128]{1,0:T(8,128)(2,1)S(1)} %add_add_fusion.1), channel_id=1, source_target_pairs={{0,4},{1,9},{2,6},{3,11},{4,0},{5,13},{6,2},{7,15},{8,12},{9,1},{1... | collective-permute-start | bytes 208904 | tf_op jit(solution)/shard_map/ppermute | solution.py:570
  28.8 1.5 %collective-permute-start.10 = (bf16[272,128]{1,0:T(8,128)(2,1)S(1)}, bf16[272,128]{1,0:T(8,128)(2,1)S(1)}, u32[]{:S(2)}, u32[]{:S(2)}) collective-permute-start(bf16[272,128]{1,0:T(8,128)(2,1)S(1)} %add_add_fusion.1), channel_id=1, source_target_pairs={{0,4},{1,25},{2,6},{3,27},{4,0},{5,29},{6,2},{7,31},{8,12},{9,17},... | collective-permute-start | bytes 208904 | tf_op jit(solution)/shard_map/ppermute | solution.py:570
  30.4 0.8 %collective-permute-done.9 = bf16[272,128]{1,0:T(8,128)(2,1)S(1)} collective-permute-done((bf16[272,128]{1,0:T(8,128)(2,1)S(1)}, bf16[272,128]{1,0:T(8,128)(2,1)S(1)}, u32[]{:S(2)}, u32[]{:S(2)}) %collective-permute-start.9) | collective-permute-done | bytes 69664 | tf_op jit(solution)/shard_map/ppermute | solution.py:570
  31.1 1.5 %collective-permute-done.8 = bf16[272,128]{1,0:T(8,128)(2,1)S(1)} collective-permute-done((bf16[272,128]{1,0:T(8,128)(2,1)S(1)}, bf16[272,128]{1,0:T(8,128)(2,1)S(1)}, u32[]{:S(2)}, u32[]{:S(2)}) %collective-permute-start.8) | collective-permute-done | bytes 69664 | tf_op jit(solution)/shard_map/ppermute | solution.py:570
  32.6 0.7 %collective-permute-done.10 = bf16[272,128]{1,0:T(8,128)(2,1)S(1)} collective-permute-done((bf16[272,128]{1,0:T(8,128)(2,1)S(1)}, bf16[272,128]{1,0:T(8,128)(2,1)S(1)}, u32[]{:S(2)}, u32[]{:S(2)}) %collective-permute-start.10) | collective-permute-done | bytes 69664 | tf_op jit(solution)/shard_map/ppermute | solution.py:570
  33.4 0.6 %collective-permute-start.11 = (f32[272,128]{1,0:T(8,128)S(1)}, f32[272,128]{1,0:T(8,128)S(1)}, u32[]{:S(2)}, u32[]{:S(2)}) collective-permute-start(f32[272,128]{1,0:T(8,128)S(1)} %add_add_fusion.mine_ref), channel_id=1, source_target_pairs={{0,1},{1,0},{2,3},{3,2},{4,5},{5,4},{6,7},{7,6},{8,9},{9,8},{10,11... | collective-permute-start | bytes 417800 | tf_op jit(solution)/shard_map/ppermute | solution.py:564
  34.0 1.0 %collective-permute-done.11.theirs_ref = f32[272,128]{1,0:T(8,128)S(1)} collective-permute-done((f32[272,128]{1,0:T(8,128)S(1)}, f32[272,128]{1,0:T(8,128)S(1)}, u32[]{:S(2)}, u32[]{:S(2)}) %collective-permute-start.11) | collective-permute-done | bytes 139296 | tf_op jit(solution)/shard_map/ppermute | solution.py:564
  35.0 0.7 %last.1 = (f32[32,1024]{1,0:T(8,128)}, f32[1,1024]{1,0:T(1,128)}, f32[1,16]{1,0:T(1,128)}) custom-call(s32[1]{0:T(128)} %bitcast.me_ref, f32[272,128]{1,0:T(8,128)S(1)} %add_add_fusion.mine_ref, f32[272,128]{1,0:T(8,128)S(1)} %collective-permute-done.11.theirs_ref), custom_call_target="tpu_custom_call" | custom-call | flops 100000000 | bytes 3000000 | tf_op jit(solution)/shard_map/last/pallas_call | solution.py:546
  (4 shorter events, 0.1 us)
Async XLA Ops:
  3.5 3.1 %collective-permute-start = (bf16[208,1024]{1,0:T(8,128)(2,1)S(1)}, bf16[208,1024]{1,0:T(8,128)(2,1)S(1)}, u32[]{:S(2)}, u32[]{:S(2)}) collective-permute-start(bf16[208,1024]{1,0:T(8,128)(2,1)S(1)} %get-tuple-element.57), channel_id=1, source_target_pairs={{0,1},{1,0},{2,3},{3,2},{4,5},{5,4},{6,7},{7,6},{8,9},{9,8},{10,11... | collective-permute-start | bytes 1277960 | tf_op jit(solution)/shard_map/ppermute | solution.py:564
  4.0 8.2 %collective-permute-start.1 = (bf16[144,1024]{1,0:T(8,128)(2,1)S(1)}, bf16[144,1024]{1,0:T(8,128)(2,1)S(1)}, u32[]{:S(2)}, u32[]{:S(2)}) collective-permute-start(bf16[144,1024]{1,0:T(8,128)(2,1)S(1)} %get-tuple-element.58), channel_id=1, source_target_pairs={{0,4},{1,2},{2,1},{3,7},{4,0},{5,6},{6,5},{7,3},{8,12},{9,10},{10,... | collective-permute-start | bytes 884744 | tf_op jit(solution)/shard_map/ppermute | solution.py:580
  7.2 5.6 %collective-permute-start.2 = (bf16[64,1024]{1,0:T(8,128)(2,1)S(1)}, bf16[64,1024]{1,0:T(8,128)(2,1)S(1)}, u32[]{:S(2)}, u32[]{:S(2)}) collective-permute-start(bf16[64,1024]{1,0:T(8,128)(2,1)S(1)} %get-tuple-element.73), channel_id=1, source_target_pairs={{0,4},{1,2},{2,1},{3,7},{4,0},{5,6},{6,5},{7,3},{8,12},{9,10},{10,... | collective-permute-start | bytes 393224 | tf_op jit(solution)/shard_map/ppermute | solution.py:580
  13.3 1.4 %collective-permute-start.3 = (bf16[64,1024]{1,0:T(8,128)(2,1)S(1)}, bf16[64,1024]{1,0:T(8,128)(2,1)S(1)}, u32[]{:S(2)}, u32[]{:S(2)}) collective-permute-start(bf16[64,1024]{1,0:T(8,128)(2,1)S(1)} %get-tuple-element.75), channel_id=1, source_target_pairs={{0,1},{1,0},{2,3},{3,2},{4,5},{5,4},{6,7},{7,6},{8,9},{9,8},{10,11... | collective-permute-start | bytes 393224 | tf_op jit(solution)/shard_map/ppermute | solution.py:564
  18.2 1.3 %collective-permute-start.4 = (bf16[272,128]{1,0:T(8,128)(2,1)S(1)}, bf16[272,128]{1,0:T(8,128)(2,1)S(1)}, u32[]{:S(2)}, u32[]{:S(2)}) collective-permute-start(bf16[272,128]{1,0:T(8,128)(2,1)S(1)} %get-tuple-element.79), channel_id=1, source_target_pairs={{0,1},{1,0},{2,3},{3,2},{4,5},{5,4},{6,7},{7,6},{8,9},{9,8},{10,11... | collective-permute-start | bytes 208904 | tf_op jit(solution)/shard_map/ppermute | solution.py:564
  19.5 5.1 %collective-permute-start.7 = (bf16[272,128]{1,0:T(8,128)(2,1)S(1)}, bf16[272,128]{1,0:T(8,128)(2,1)S(1)}, u32[]{:S(2)}, u32[]{:S(2)}) collective-permute-start(bf16[272,128]{1,0:T(8,128)(2,1)S(1)} %add_convert_fusion), channel_id=1, source_target_pairs={{0,8},{1,7},{2,10},{3,5},{4,12},{5,3},{6,14},{7,1},{8,0},{9,15},{1... | collective-permute-start | bytes 208904 | tf_op jit(solution)/shard_map/ppermute | solution.py:570
  21.6 4.3 %collective-permute-start.6 = (bf16[272,128]{1,0:T(8,128)(2,1)S(1)}, bf16[272,128]{1,0:T(8,128)(2,1)S(1)}, u32[]{:S(2)}, u32[]{:S(2)}) collective-permute-start(bf16[272,128]{1,0:T(8,128)(2,1)S(1)} %add_convert_fusion), channel_id=1, source_target_pairs={{0,8},{1,5},{2,10},{3,7},{4,12},{5,1},{6,14},{7,3},{8,0},{9,13},{1... | collective-permute-start | bytes 208904 | tf_op jit(solution)/shard_map/ppermute | solution.py:570
  21.7 5.0 %collective-permute-start.5 = (bf16[272,128]{1,0:T(8,128)(2,1)S(1)}, bf16[272,128]{1,0:T(8,128)(2,1)S(1)}, u32[]{:S(2)}, u32[]{:S(2)}) collective-permute-start(bf16[272,128]{1,0:T(8,128)(2,1)S(1)} %add_convert_fusion), channel_id=1, source_target_pairs={{0,8},{1,3},{2,10},{3,1},{4,12},{5,7},{6,14},{7,5},{8,0},{9,11},{1... | collective-permute-start | bytes 208904 | tf_op jit(solution)/shard_map/ppermute | solution.py:570
  26.8 4.4 %collective-permute-start.9 = (bf16[272,128]{1,0:T(8,128)(2,1)S(1)}, bf16[272,128]{1,0:T(8,128)(2,1)S(1)}, u32[]{:S(2)}, u32[]{:S(2)}) collective-permute-start(bf16[272,128]{1,0:T(8,128)(2,1)S(1)} %add_add_fusion.1), channel_id=1, source_target_pairs={{0,4},{1,17},{2,6},{3,19},{4,0},{5,21},{6,2},{7,23},{8,12},{9,25},... | collective-permute-start | bytes 208904 | tf_op jit(solution)/shard_map/ppermute | solution.py:570
  28.3 4.3 %collective-permute-start.8 = (bf16[272,128]{1,0:T(8,128)(2,1)S(1)}, bf16[272,128]{1,0:T(8,128)(2,1)S(1)}, u32[]{:S(2)}, u32[]{:S(2)}) collective-permute-start(bf16[272,128]{1,0:T(8,128)(2,1)S(1)} %add_add_fusion.1), channel_id=1, source_target_pairs={{0,4},{1,9},{2,6},{3,11},{4,0},{5,13},{6,2},{7,15},{8,12},{9,1},{1... | collective-permute-start | bytes 208904 | tf_op jit(solution)/shard_map/ppermute | solution.py:570
  28.8 4.5 %collective-permute-start.10 = (bf16[272,128]{1,0:T(8,128)(2,1)S(1)}, bf16[272,128]{1,0:T(8,128)(2,1)S(1)}, u32[]{:S(2)}, u32[]{:S(2)}) collective-permute-start(bf16[272,128]{1,0:T(8,128)(2,1)S(1)} %add_add_fusion.1), channel_id=1, source_target_pairs={{0,4},{1,25},{2,6},{3,27},{4,0},{5,29},{6,2},{7,31},{8,12},{9,17},... | collective-permute-start | bytes 208904 | tf_op jit(solution)/shard_map/ppermute | solution.py:570
  33.4 1.6 %collective-permute-start.11 = (f32[272,128]{1,0:T(8,128)S(1)}, f32[272,128]{1,0:T(8,128)S(1)}, u32[]{:S(2)}, u32[]{:S(2)}) collective-permute-start(f32[272,128]{1,0:T(8,128)S(1)} %add_add_fusion.mine_ref), channel_id=1, source_target_pairs={{0,1},{1,0},{2,3},{3,2},{4,5},{5,4},{6,7},{7,6},{8,9},{9,8},{10,11... | collective-permute-start | bytes 417800 | tf_op jit(solution)/shard_map/ppermute | solution.py:564

commit v3 on v2

--- a/solution.py
+++ b/solution.py
@@ -63,11 +63,6 @@
 
 def stacked(z, masks):
     return jnp.concatenate([z * masks[0], z * masks[1]], axis=0)
-
-
-def stacked_group(z):
-    head = iota((1, z.shape[1]), 1) // WINDOW
-    return jnp.concatenate([z * (head == i).astype(BF16) for i in range(z.shape[1] // WINDOW)], axis=0)
 
 
 def one_above(z):
@@ -215,7 +210,7 @@
 
 def join_kernel(heads, count, before_if_odd, me_ref, own_ref, edge_ref, small_ref, memory_ref, adjoint_ref, rim_ref,
                 *rest):
-    state_ref, part_ref, out_ref = rest if len(rest) == 3 else (None, *rest)
+    part_ref, out_ref, weight_ref = rest if len(rest) == 3 else (*rest, None)
     width = rim_ref.shape[1]
     length = small_ref.shape[0]
     table = head_table(heads, width)
@@ -233,18 +228,21 @@
     scale = expand(jnp.concatenate([scale, fade, weight], axis=0), table)
     scaled = (rim_ref[WINDOW:2 * WINDOW].astype(F32) * scale[:WINDOW]).astype(BF16)
     fade, weight = scale[WINDOW:WINDOW + 1], scale[WINDOW + 1:]
-    if state_ref is None:
-        state = rim_ref[2 * WINDOW + BAND:].astype(F32)
+    base = jnp.where(everywhere(before, memory_ref.shape), memory_ref[...], adjoint_ref[...])
+    if weight_ref is None:
+        base = base + weight * rim_ref[2 * WINDOW + BAND:].astype(F32)
     else:
         edge = (me_ref[0] == 0) | (me_ref[0] == count - 1)
-        state = jnp.where(everywhere(edge, state_ref.shape), 0.0, state_ref[...].astype(F32))
-    base = jnp.where(everywhere(before, memory_ref.shape), memory_ref[...], adjoint_ref[...])
-    base = base + weight * state
+        weight_ref[...] = jnp.where(everywhere(edge, weight.shape), 0.0, weight)
     for pair in range(width // LANES):
         at = slice(pair * LANES, (pair + 1) * LANES)
         part = folded(dot_tn(rim_ref[:WINDOW, at], scaled[:, at]))
         part_ref[:, at] = part
-        out_ref[:, at] = (base[:, at] + fade[:, at] * part).astype(BF16)
+        out_ref[:, at] = (base[:, at] + fade[:, at] * part).astype(out_ref.dtype)
+
+
+def pass_kernel(me_ref, base_ref, weight_ref, state_ref, out_ref):
+    out_ref[...] = (base_ref[...] + weight_ref[...] * state_ref[...].astype(F32)).astype(BF16)
 
 
 def decays(column_pair, row_pair, keep):
@@ -389,9 +387,8 @@
                   dqf_ref, dwk_ref, dvl_ref, dl_ref, scales_ref,
                   near_first_ref, near_second_ref, near_dl_ref, far_first_ref, far_second_ref, far_dl_ref,
                   near_part_ref, far_part_ref, cross_ref, passed_ref,
-                  dq_out, dk_out, dv_out, logits_ref, sums_ref,
-                  fwd_ref, bwd_ref, rim_dq_ref, rim_dwk_ref, rim_dv_ref, rim_dl_ref,
-                  dq_ref, dk_ref, dv_ref, sems):
+                  dq_ref, dk_ref, dv_ref, logits_ref, sums_ref,
+                  fwd_ref, bwd_ref, rim_dq_ref, rim_dwk_ref, rim_dv_ref, rim_dl_ref):
     length, width = wk_ref.shape
     late = length - WINDOW
     pairs = width // LANES
@@ -406,6 +403,7 @@
     pl.when(is_odd(me_ref))(lambda: edges(*near_edge))
     pl.when(jnp.logical_not(is_odd(me_ref)))(lambda: edges(*far_edge))
     table = head_table(heads, width)
+    masks = half_masks()
     small = small_ref[...]
     total, gamma, soft, slope = (small[:, i * heads:(i + 1) * heads] for i in range(4))
     last, middle = total[length - 1:], total[late - 1:late]
@@ -440,9 +438,9 @@
 
     own_products, rim_products, out_products, key_products, d_coef = [], [], [], [], []
     coef = coef_ref[...]
-    for group in range(pairs // 2):
-        at = slice(2 * group * LANES, 2 * (group + 1) * LANES)
-        m0, m1, a1, a0, b0 = (stacked_group(z[:, at]) for z in (start, halfway, after, half_after, later))
+    for pair in range(pairs):
+        at = slice(pair * LANES, (pair + 1) * LANES)
+        m0, m1, a1, a0, b0 = (stacked(z[:, at], masks) for z in (start, halfway, after, half_after, later))
         qf, g, wk, v = qf_ref[:, at], g_ref[:, at], wk_ref[:, at], v_ref[:, at]
         from_q = jnp.concatenate([dot(qf[:late], m0), dot(qf[late:], m1)], axis=0)
         out_products.append(from_q * g.astype(F32))
@@ -465,17 +463,10 @@
         c = coef[:, at]
         key_products.append(dwk * phi(k, c))
         d_phi = dwk * gamma_x[:, at]
-        dq_ref[:, at] = (dqf * (0.125 + 0.25 * c * q)).astype(BF16)
-        dk_ref[:, at] = (d_phi * (0.125 + 0.25 * c * k)).astype(BF16)
-        row = jnp.sum(dqf * (0.125 * q * q) + d_phi * (0.125 * k * k), axis=0, keepdims=True)
-        d_coef += [row[:, :LANES], row[:, LANES:]]
-
-    copies = [
-        pltpu.make_async_copy(source, target, sems.at[i])
-        for i, (source, target) in enumerate([(dq_ref, dq_out), (dk_ref, dk_out), (dv_ref, dv_out)])
-    ]
-    for copy in copies:
-        copy.start()
+        dq_ref[:, at] = dqf
+        dk_ref[:, at] = d_phi
+        d_coef.append(jnp.sum(dqf * (0.125 * q * q) + d_phi * (0.125 * k * k), axis=0, keepdims=True))
+
     sums = jnp.concatenate(
         [
             jnp.concatenate(z, axis=1).astype(BF16)
@@ -505,17 +496,22 @@
         sums_ref[i * 2 * heads:(i + 1) * 2 * heads] = gate[:, i * LANES:(i + 1) * LANES].astype(BF16)
     rest = d_coef + [d_rate, jnp.zeros((BAND - 1 - pairs, LANES), F32)]
     sums_ref[pairs * 2 * heads:] = jnp.concatenate(rest, axis=0).astype(BF16)
-    for copy in copies:
-        copy.wait()
-
-
-def inputs_kernel(me_ref, logits_ref, w_ref, dx_ref):
+
+
+def outputs_kernel(me_ref, logits_ref, w_ref, q_ref, k_ref, coef_ref, dqf_ref, d_phi_ref, dv_ref,
+                   dx_ref, dq_ref, dk_ref, dv_out, sem):
+    copy = pltpu.make_async_copy(dv_ref, dv_out, sem)
+    copy.start()
+    coef = 0.25 * coef_ref[...]
+    dq_ref[...] = (dqf_ref[...] * (0.125 + coef * q_ref[...].astype(F32))).astype(BF16)
+    dk_ref[...] = (d_phi_ref[...] * (0.125 + coef * k_ref[...].astype(F32))).astype(BF16)
     high, low = (part.astype(F32) for part in split(logits_ref[...], 2))
     w_high, w_low = split(w_ref[...], 2)
     dx_ref[...] = dot(
         jnp.concatenate([high, low, high], axis=1).astype(BF16),
         jnp.concatenate([w_high, w_high, w_low], axis=0),
     ).astype(BF16)
+    copy.wait()
 
 
 def last_kernel(heads, me_ref, mine_ref, theirs_ref, gate_ref, coef_ref, rate_ref):
@@ -626,12 +622,13 @@
         flops=2 * 10**8,
         moved=5 * 10**6,
     )
-    far_part, passed = call(
+    far_part, base, weight = call(
         functools.partial(join_kernel, heads, count, False),
-        [half, sent],
-        (me, own[3], near_edge[2], gates, memory, adjoint, far, cross),
+        [half, half, ((1, width), F32)],
+        (me, own[3], near_edge[2], gates, memory, adjoint, far),
         "join_far",
     )
+    passed = call(pass_kernel, [sent], (me, base, weight, cross), "pass_on")[0]
     passed = swapped(passed, "seq", 1)
     far_edge = call(
         functools.partial(edge_kernel, heads, False),
@@ -642,28 +639,33 @@
         moved=3 * 10**6,
     )
     all_sums = ((width // LANES * 2 * heads + BAND, LANES), BF16)
-    dq, dk, dv, d_logits, sums = call(
+    dqf, d_phi, dv, d_logits, sums = call(
         functools.partial(finish_kernel, heads, count),
-        [wide, wide, wide, ((length, 2 * heads), F32), all_sums],
+        [full, full, wide, ((length, 2 * heads), F32), all_sums],
         (me, q, k, x, v, g, coef, rate, gates, wk, qf, near, far, adjoint, *own, scales, *near_edge, *far_edge,
          near_part, far_part, cross, passed),
         "finish",
-        scratch=[pltpu.VMEM(*z) for z in (rim, rim, half, half, half, edge[2], wide, wide, wide)]
-        + [pltpu.SemaphoreType.DMA((3,))],
-        outside=range(3),
-    )
-    dx = call(inputs_kernel, [wide], (me, d_logits, wt), "inputs")[0]
+        scratch=[pltpu.VMEM(*z) for z in (rim, rim, half, half, half, edge[2])],
+    )
+    dx, dq, dk, dv = call(
+        outputs_kernel,
+        [wide] * 4,
+        (me, d_logits, wt, q, k, coef, dqf, d_phi, dv),
+        "outputs",
+        scratch=[pltpu.SemaphoreType.DMA],
+        outside=(3,),
+    )
     sums = sums.astype(F32) + swapped(sums, EVERYONE, 1).astype(F32)
     distance = 2
     while distance < lax.axis_size(EVERYONE):
         sums = sums.astype(BF16)
         if 2 * distance < lax.axis_size(EVERYONE):
             far, mid, one = (odd_swapped(sums, i * distance, distance).astype(F32) for i in (3, 2, 1))
-            sums = (sums.astype(F32) + one) + (mid + far)
+            sums = (one + mid) + (far + sums.astype(F32))
         else:
             sums = sums.astype(F32) + odd_swapped(sums, distance, distance).astype(F32)
         if distance == 2:
-            sums, dx = lax.optimization_barrier((sums, dx))
+            sums, dx, dq, dk, dv = lax.optimization_barrier((sums, dx, dq, dk, dv))
         distance *= 4
     gate, d_coef, d_rate = call(
         functools.partial(last_kernel, heads),

time: 35.9 us -> 34.4 us (0.958)
  waiting for transfers between devices: 7.94 us -> 6.92 us
  starting transfers between devices: 13.6 us -> 13.2 us
    ppermute x6, waiting for transfers between devices: 5.08 us -> 4.39 us  [odd_swapped(): lax.ppermute(value, EVERYONE, [(i, i ^ (distance if i % 2 else idle)) for...]
    ppermute x2, waiting for transfers between devices: 0.55 us -> 0.02 us  [inner_swapped(): return lax.ppermute(value, EVERYONE, pairs)]
    ppermute x4, starting transfers between devices: 1.45 us -> 1.08 us  [swapped(): lax.ppermute(value, axis, [(i, i ^ distance) for i in range(lax.axis_size...]
    pallas_call x9 -> x10, Pallas kernels: 13.4 us -> 13.3 us  [call(): pl.pallas_call(kernel, out_shape=tuple((jax.ShapeDtypeStruct(*out) for ou...]
  transfers between devices with their start and end apart: 12 -> 12, of which waited for: 9 -> 8; matrix products, arithmetic and copies ran while one was open for 0% -> 0% of each run, Pallas kernels for 16% -> 21%
where the time goes in v3:
time: 34.4 us; the launch traced here: 34.2 us
  Pallas kernels  13.3 us (39%)
  starting transfers between devices  13.2 us (38%)
  waiting for transfers between devices  6.92 us (20%)
  between operations  0.74 us (2%)
    pallas_call x10, Pallas kernels, call(): pl.pallas_call(kernel, out_shape=tuple((jax.ShapeDtypeStruct(*out) for ou...  13.3 us
    ppermute x6, starting transfers between devices, odd_swapped(): lax.ppermute(value, EVERYONE, [(i, i ^ (distance if i % 2 else idle)) for...  7.77 us
    ppermute x6, waiting for transfers between devices, odd_swapped(): lax.ppermute(value, EVERYONE, [(i, i ^ (distance if i % 2 else idle)) for...  4.39 us
    ppermute x2, starting transfers between devices, inner_swapped(): return lax.ppermute(value, EVERYONE, pairs)  4.37 us
    ppermute x4, waiting for transfers between devices, swapped(): lax.ppermute(value, axis, [(i, i ^ distance) for i in range(lax.axis_size...  2.51 us
    ppermute x4, starting transfers between devices, swapped(): lax.ppermute(value, axis, [(i, i ^ distance) for i in range(lax.axis_size...  1.08 us
  transfers between devices with their start and end apart: 12, of which 8 were waited for; matrix products, arithmetic and copies ran while one was open for 0% of the time, Pallas kernels for 21%

profile of v3, /device:TPU:0, one launch (start us, length us, event | category | flops | bytes accessed | tf_op | source)
XLA Modules:
  0.0 34.2 jit_solution(13363142434889012214)
XLA Ops:
  0.6 2.9 %prep.1 = (bf16[128,1024]{1,0:T(8,128)(2,1)S(1)}, bf16[128,1024]{1,0:T(8,128)(2,1)S(1)}, f32[128,128]{1,0:T(8,128)S(1)}, bf16[208,1024]{1,0:T(8,128)(2,1)S(1)}, ...) custom-call(s32[1]{0:T(128)} %bitcast.me_ref, ...), custom_call_target="tpu_custom_call" | custom-call | flops 100000000 | bytes 3000000 | tf_op jit(solution)/shard_map/prep/pallas_call | solution.py:542
  3.5 0.5 %collective-permute-start = (bf16[208,1024]{1,0:T(8,128)(2,1)S(1)}, bf16[208,1024]{1,0:T(8,128)(2,1)S(1)}, u32[]{:S(2)}, u32[]{:S(2)}) collective-permute-start(bf16[208,1024]{1,0:T(8,128)(2,1)S(1)} %get-tuple-element.65), channel_id=1, source_target_pairs={{0,1},{1,0},{2,3},{3,2},{4,5},{5,4},{6,7},{7,6},{8,9},{9,8},{10,11... | collective-permute-start | bytes 1277960 | tf_op jit(solution)/shard_map/ppermute | solution.py:560
  4.0 2.6 %collective-permute-start.1 = (bf16[144,1024]{1,0:T(8,128)(2,1)S(1)}, bf16[144,1024]{1,0:T(8,128)(2,1)S(1)}, u32[]{:S(2)}, u32[]{:S(2)}) collective-permute-start(bf16[144,1024]{1,0:T(8,128)(2,1)S(1)} %get-tuple-element.66), channel_id=1, source_target_pairs={{0,4},{1,2},{2,1},{3,7},{4,0},{5,6},{6,5},{7,3},{8,12},{9,10},{10,... | collective-permute-start | bytes 884744 | tf_op jit(solution)/shard_map/ppermute | solution.py:576
  6.7 0.0 collective-permute-done.rim_ref.near_ref
  6.7 0.5 %join_near.1 = (f32[64,1024]{1,0:T(8,128)S(1)}, bf16[64,1024]{1,0:T(8,128)(2,1)S(1)}) custom-call(s32[1]{0:T(128)} %bitcast.me_ref, f32[128,128]{1,0:T(8,128)S(1)} %get-tuple-element.62.small_ref.own_ref.edge_ref, f32[128,128]{1,0:T(8,128)S(1)} %get-tuple-element.62.small_ref.own_ref.edge_ref, f32[128,128]{1,0:T(8,128)S(1)} %get-tuple-element.62.small_ref.own_ref.edge_ref, ...), custom_call_target="tpu_custom_call" | custom-call | flops 100000000 | bytes 3000000 | tf_op jit(solution)/shard_map/join_near/pallas_call | solution.py:542
  7.2 1.8 %collective-permute-start.2 = (bf16[64,1024]{1,0:T(8,128)(2,1)S(1)}, bf16[64,1024]{1,0:T(8,128)(2,1)S(1)}, u32[]{:S(2)}, u32[]{:S(2)}) collective-permute-start(bf16[64,1024]{1,0:T(8,128)(2,1)S(1)} %get-tuple-element.82), channel_id=1, source_target_pairs={{0,4},{1,2},{2,1},{3,7},{4,0},{5,6},{6,5},{7,3},{8,12},{9,10},{10,... | collective-permute-start | bytes 393224 | tf_op jit(solution)/shard_map/ppermute | solution.py:576
  8.9 1.8 %own.1 = (f32[128,1024]{1,0:T(8,128)S(1)}, f32[128,1024]{1,0:T(8,128)S(1)}, f32[128,1024]{1,0:T(8,128)S(1)}, f32[128,16]{1,0:T(8,128)S(1)}) custom-call(s32[1]{0:T(128)} %bitcast.me_ref, f32[128,128]{1,0:T(8,128)S(1)} %get-tuple-element.62.small_ref.own_ref.edge_ref, bf16[128,1024]{1,0:T(8,128)(2,1)S(1)} %get-tuple-element.63.wk_ref, ...), custom_call_target="tpu_custom_call" | custom-call | flops 700000000 | bytes 7000000 | tf_op jit(solution)/shard_map/own/pallas_call | solution.py:542
  10.8 1.5 %edge_near.1 = (f32[64,1024]{1,0:T(8,128)S(1)}, f32[64,1024]{1,0:T(8,128)S(1)}, f32[64,16]{1,0:T(8,128)S(1)}, f32[400,1024]{1,0:T(8,128)S(1)}) custom-call(s32[1]{0:T(128)} %bitcast.me_ref, f32[128,128]{1,0:T(8,128)S(1)} %get-tuple-element.62.small_ref.own_ref.edge_ref, bf16[128,1024]{1,0:T(8,128)(2,1)S(1)} %get-tuple-element.63.wk_ref, ...), custom_call_target="tpu_custom_call" | custom-call | flops 200000000 | bytes 5000000 | tf_op jit(solution)/shard_map/edge_near/pallas_call | solution.py:542
  12.2 0.0 collective-permute-done.1.rim_ref.far_ref
  12.2 0.5 %join_far.1 = (f32[64,1024]{1,0:T(8,128)S(1)}, f32[64,1024]{1,0:T(8,128)S(1)}, f32[1,1024]{1,0:T(1,128)S(1)}) custom-call(s32[1]{0:T(128)} %bitcast.me_ref, f32[128,16]{1,0:T(8,128)S(1)} %get-tuple-element.71.own_ref.dl_ref, f32[64,16]{1,0:T(8,128)S(1)} %get-tuple-element.75.edge_ref.near_dl_ref, ...), custom_call_target="tpu_custom_call" | custom-call | flops 100000000 | bytes 3000000 | tf_op jit(solution)/shard_map/join_far/pallas_call | solution.py:542
  12.7 0.0 collective-permute-done.2.state_ref.cross_ref
  12.8 0.3 collective-permute-start.3
  13.1 1.1 %edge_far.1 = (f32[64,1024]{1,0:T(8,128)S(1)}, f32[64,1024]{1,0:T(8,128)S(1)}, f32[64,16]{1,0:T(8,128)S(1)}) custom-call(s32[1]{0:T(128)} %bitcast.me_ref, f32[128,128]{1,0:T(8,128)S(1)} %get-tuple-element.62.small_ref.own_ref.edge_ref, bf16[128,1024]{1,0:T(8,128)(2,1)S(1)} %get-tuple-element.63.wk_ref, bf16[128,1024]{1,0:T(8,128)(2,1)S(1)} %get-tuple-element.64.qf_ref, ...), custom_call_target="tpu_custom_call" | custom-call | flops 200000000 | bytes 3000000 | tf_op jit(solution)/shard_map/edge_far/pallas_call | solution.py:542
  14.1 0.1 collective-permute-done.3.passed_ref
  14.2 2.6 %finish.1 = (f32[128,1024]{1,0:T(8,128)S(1)}, f32[128,1024]{1,0:T(8,128)S(1)}, bf16[128,1024]{1,0:T(8,128)(2,1)S(1)}, f32[128,32]{1,0:T(8,128)S(1)}, bf16[272,128]{1,0:T(8,128)(2,1)S(1)}) custom-call(s32[1]{0:T(128)} %bitcast.me_ref, bf16[128,1024]{1,0:T(8,128)(2,1)S(1)} %get-tuple-element.55.q_ref, bf16[128,1024]{1,0:T(8,128)(2,1)S(1)} %get-tuple-element.56.k_ref, ...), custom_call_target="tpu_custom_call" | custom-call | flops 100000000 | bytes 3000000 | tf_op jit(solution)/shard_map/finish/pallas_call | solution.py:542
  16.9 0.3 collective-permute-start.4
  17.1 1.1 %collective-permute-done.4 = bf16[272,128]{1,0:T(8,128)(2,1)S(1)} collective-permute-done((bf16[272,128]{1,0:T(8,128)(2,1)S(1)}, bf16[272,128]{1,0:T(8,128)(2,1)S(1)}, u32[]{:S(2)}, u32[]{:S(2)}) %collective-permute-start.4) | collective-permute-done | bytes 69664 | tf_op jit(solution)/shard_map/ppermute | solution.py:560
  18.2 2.1 %collective-permute-start.7 = (bf16[272,128]{1,0:T(8,128)(2,1)S(1)}, bf16[272,128]{1,0:T(8,128)(2,1)S(1)}, u32[]{:S(2)}, u32[]{:S(2)}) collective-permute-start(bf16[272,128]{1,0:T(8,128)(2,1)S(1)} %add_convert_fusion), channel_id=1, source_target_pairs={{0,8},{1,7},{2,10},{3,5},{4,12},{5,3},{6,14},{7,1},{8,0},{9,15},{1... | collective-permute-start | bytes 208904 | tf_op jit(solution)/shard_map/ppermute | solution.py:566
  20.4 0.1 collective-permute-start.6
  20.4 1.9 %collective-permute-start.5 = (bf16[272,128]{1,0:T(8,128)(2,1)S(1)}, bf16[272,128]{1,0:T(8,128)(2,1)S(1)}, u32[]{:S(2)}, u32[]{:S(2)}) collective-permute-start(bf16[272,128]{1,0:T(8,128)(2,1)S(1)} %add_convert_fusion), channel_id=1, source_target_pairs={{0,8},{1,3},{2,10},{3,1},{4,12},{5,7},{6,14},{7,5},{8,0},{9,11},{1... | collective-permute-start | bytes 208904 | tf_op jit(solution)/shard_map/ppermute | solution.py:566
  22.4 1.7 %outputs.1 = (bf16[128,1024]{1,0:T(8,128)(2,1)}, bf16[128,1024]{1,0:T(8,128)(2,1)}, bf16[128,1024]{1,0:T(8,128)(2,1)}, bf16[128,1024]{1,0:T(8,128)(2,1)}) custom-call(s32[1]{0:T(128)} %bitcast.me_ref, f32[128,32]{1,0:T(8,128)S(1)} %get-tuple-element.86.logits_ref, f32[32,1024]{1,0:T(8,128)S(1)} %get-tuple-element.87.w_ref, ...), custom_call_target="tpu_custom_call" | custom-call | flops 100000000 | bytes 3000000 | tf_op jit(solution)/shard_map/outputs/pallas_call | solution.py:542
  24.1 0.6 %collective-permute-done.6 = bf16[272,128]{1,0:T(8,128)(2,1)S(1)} collective-permute-done((bf16[272,128]{1,0:T(8,128)(2,1)S(1)}, bf16[272,128]{1,0:T(8,128)(2,1)S(1)}, u32[]{:S(2)}, u32[]{:S(2)}) %collective-permute-start.6) | collective-permute-done | bytes 69664 | tf_op jit(solution)/shard_map/ppermute | solution.py:566
  24.7 0.7 %collective-permute-done.5 = bf16[272,128]{1,0:T(8,128)(2,1)S(1)} collective-permute-done((bf16[272,128]{1,0:T(8,128)(2,1)S(1)}, bf16[272,128]{1,0:T(8,128)(2,1)S(1)}, u32[]{:S(2)}, u32[]{:S(2)}) %collective-permute-start.5) | collective-permute-done | bytes 69664 | tf_op jit(solution)/shard_map/ppermute | solution.py:566
  25.5 1.6 %collective-permute-start.10 = (bf16[272,128]{1,0:T(8,128)(2,1)S(1)}, bf16[272,128]{1,0:T(8,128)(2,1)S(1)}, u32[]{:S(2)}, u32[]{:S(2)}) collective-permute-start(bf16[272,128]{1,0:T(8,128)(2,1)S(1)} %add_add_fusion.1), channel_id=1, source_target_pairs={{0,4},{1,25},{2,6},{3,27},{4,0},{5,29},{6,2},{7,31},{8,12},{9,17},... | collective-permute-start | bytes 208904 | tf_op jit(solution)/shard_map/ppermute | solution.py:566
  27.0 0.5 %collective-permute-start.9 = (bf16[272,128]{1,0:T(8,128)(2,1)S(1)}, bf16[272,128]{1,0:T(8,128)(2,1)S(1)}, u32[]{:S(2)}, u32[]{:S(2)}) collective-permute-start(bf16[272,128]{1,0:T(8,128)(2,1)S(1)} %add_add_fusion.1), channel_id=1, source_target_pairs={{0,4},{1,17},{2,6},{3,19},{4,0},{5,21},{6,2},{7,23},{8,12},{9,25},... | collective-permute-start | bytes 208904 | tf_op jit(solution)/shard_map/ppermute | solution.py:566
  27.5 1.5 %collective-permute-start.8 = (bf16[272,128]{1,0:T(8,128)(2,1)S(1)}, bf16[272,128]{1,0:T(8,128)(2,1)S(1)}, u32[]{:S(2)}, u32[]{:S(2)}) collective-permute-start(bf16[272,128]{1,0:T(8,128)(2,1)S(1)} %add_add_fusion.1), channel_id=1, source_target_pairs={{0,4},{1,9},{2,6},{3,11},{4,0},{5,13},{6,2},{7,15},{8,12},{9,1},{1... | collective-permute-start | bytes 208904 | tf_op jit(solution)/shard_map/ppermute | solution.py:566
  29.1 0.8 %collective-permute-done.10 = bf16[272,128]{1,0:T(8,128)(2,1)S(1)} collective-permute-done((bf16[272,128]{1,0:T(8,128)(2,1)S(1)}, bf16[272,128]{1,0:T(8,128)(2,1)S(1)}, u32[]{:S(2)}, u32[]{:S(2)}) %collective-permute-start.10) | collective-permute-done | bytes 69664 | tf_op jit(solution)/shard_map/ppermute | solution.py:566
  29.8 1.5 %collective-permute-done.9 = bf16[272,128]{1,0:T(8,128)(2,1)S(1)} collective-permute-done((bf16[272,128]{1,0:T(8,128)(2,1)S(1)}, bf16[272,128]{1,0:T(8,128)(2,1)S(1)}, u32[]{:S(2)}, u32[]{:S(2)}) %collective-permute-start.9) | collective-permute-done | bytes 69664 | tf_op jit(solution)/shard_map/ppermute | solution.py:566
  31.3 0.7 %collective-permute-done.8 = bf16[272,128]{1,0:T(8,128)(2,1)S(1)} collective-permute-done((bf16[272,128]{1,0:T(8,128)(2,1)S(1)}, bf16[272,128]{1,0:T(8,128)(2,1)S(1)}, u32[]{:S(2)}, u32[]{:S(2)}) %collective-permute-start.8) | collective-permute-done | bytes 69664 | tf_op jit(solution)/shard_map/ppermute | solution.py:566
  32.1 0.1 collective-permute-start.11
  32.2 1.3 %collective-permute-done.11.theirs_ref = f32[272,128]{1,0:T(8,128)S(1)} collective-permute-done((f32[272,128]{1,0:T(8,128)S(1)}, f32[272,128]{1,0:T(8,128)S(1)}, u32[]{:S(2)}, u32[]{:S(2)}) %collective-permute-start.11) | collective-permute-done | bytes 139296 | tf_op jit(solution)/shard_map/ppermute | solution.py:560
  33.6 0.7 %last.1 = (f32[32,1024]{1,0:T(8,128)}, f32[1,1024]{1,0:T(1,128)}, f32[1,16]{1,0:T(1,128)}) custom-call(s32[1]{0:T(128)} %bitcast.me_ref, f32[272,128]{1,0:T(8,128)S(1)} %add_add_fusion.mine_ref, f32[272,128]{1,0:T(8,128)S(1)} %collective-permute-done.11.theirs_ref), custom_call_target="tpu_custom_call" | custom-call | flops 100000000 | bytes 3000000 | tf_op jit(solution)/shard_map/last/pallas_call | solution.py:542
  (5 shorter events, 0.1 us)
Async XLA Ops:
  3.5 3.1 %collective-permute-start = (bf16[208,1024]{1,0:T(8,128)(2,1)S(1)}, bf16[208,1024]{1,0:T(8,128)(2,1)S(1)}, u32[]{:S(2)}, u32[]{:S(2)}) collective-permute-start(bf16[208,1024]{1,0:T(8,128)(2,1)S(1)} %get-tuple-element.65), channel_id=1, source_target_pairs={{0,1},{1,0},{2,3},{3,2},{4,5},{5,4},{6,7},{7,6},{8,9},{9,8},{10,11... | collective-permute-start | bytes 1277960 | tf_op jit(solution)/shard_map/ppermute | solution.py:560
  4.0 8.2 %collective-permute-start.1 = (bf16[144,1024]{1,0:T(8,128)(2,1)S(1)}, bf16[144,1024]{1,0:T(8,128)(2,1)S(1)}, u32[]{:S(2)}, u32[]{:S(2)}) collective-permute-start(bf16[144,1024]{1,0:T(8,128)(2,1)S(1)} %get-tuple-element.66), channel_id=1, source_target_pairs={{0,4},{1,2},{2,1},{3,7},{4,0},{5,6},{6,5},{7,3},{8,12},{9,10},{10,... | collective-permute-start | bytes 884744 | tf_op jit(solution)/shard_map/ppermute | solution.py:576
  7.2 5.6 %collective-permute-start.2 = (bf16[64,1024]{1,0:T(8,128)(2,1)S(1)}, bf16[64,1024]{1,0:T(8,128)(2,1)S(1)}, u32[]{:S(2)}, u32[]{:S(2)}) collective-permute-start(bf16[64,1024]{1,0:T(8,128)(2,1)S(1)} %get-tuple-element.82), channel_id=1, source_target_pairs={{0,4},{1,2},{2,1},{3,7},{4,0},{5,6},{6,5},{7,3},{8,12},{9,10},{10,... | collective-permute-start | bytes 393224 | tf_op jit(solution)/shard_map/ppermute | solution.py:576
  12.8 1.4 %collective-permute-start.3 = (bf16[64,1024]{1,0:T(8,128)(2,1)S(1)}, bf16[64,1024]{1,0:T(8,128)(2,1)S(1)}, u32[]{:S(2)}, u32[]{:S(2)}) collective-permute-start(bf16[64,1024]{1,0:T(8,128)(2,1)S(1)} %pass_on.1), channel_id=1, source_target_pairs={{0,1},{1,0},{2,3},{3,2},{4,5},{5,4},{6,7},{7,6},{8,9},{9,8},{10,11... | collective-permute-start | bytes 393224 | tf_op jit(solution)/shard_map/ppermute | solution.py:560
  16.9 1.3 %collective-permute-start.4 = (bf16[272,128]{1,0:T(8,128)(2,1)S(1)}, bf16[272,128]{1,0:T(8,128)(2,1)S(1)}, u32[]{:S(2)}, u32[]{:S(2)}) collective-permute-start(bf16[272,128]{1,0:T(8,128)(2,1)S(1)} %get-tuple-element.85), channel_id=1, source_target_pairs={{0,1},{1,0},{2,3},{3,2},{4,5},{5,4},{6,7},{7,6},{8,9},{9,8},{10,11... | collective-permute-start | bytes 208904 | tf_op jit(solution)/shard_map/ppermute | solution.py:560
  18.2 5.8 %collective-permute-start.7 = (bf16[272,128]{1,0:T(8,128)(2,1)S(1)}, bf16[272,128]{1,0:T(8,128)(2,1)S(1)}, u32[]{:S(2)}, u32[]{:S(2)}) collective-permute-start(bf16[272,128]{1,0:T(8,128)(2,1)S(1)} %add_convert_fusion), channel_id=1, source_target_pairs={{0,8},{1,7},{2,10},{3,5},{4,12},{5,3},{6,14},{7,1},{8,0},{9,15},{1... | collective-permute-start | bytes 208904 | tf_op jit(solution)/shard_map/ppermute | solution.py:566
  20.4 4.3 %collective-permute-start.6 = (bf16[272,128]{1,0:T(8,128)(2,1)S(1)}, bf16[272,128]{1,0:T(8,128)(2,1)S(1)}, u32[]{:S(2)}, u32[]{:S(2)}) collective-permute-start(bf16[272,128]{1,0:T(8,128)(2,1)S(1)} %add_convert_fusion), channel_id=1, source_target_pairs={{0,8},{1,5},{2,10},{3,7},{4,12},{5,1},{6,14},{7,3},{8,0},{9,13},{1... | collective-permute-start | bytes 208904 | tf_op jit(solution)/shard_map/ppermute | solution.py:566
  20.4 5.0 %collective-permute-start.5 = (bf16[272,128]{1,0:T(8,128)(2,1)S(1)}, bf16[272,128]{1,0:T(8,128)(2,1)S(1)}, u32[]{:S(2)}, u32[]{:S(2)}) collective-permute-start(bf16[272,128]{1,0:T(8,128)(2,1)S(1)} %add_convert_fusion), channel_id=1, source_target_pairs={{0,8},{1,3},{2,10},{3,1},{4,12},{5,7},{6,14},{7,5},{8,0},{9,11},{1... | collective-permute-start | bytes 208904 | tf_op jit(solution)/shard_map/ppermute | solution.py:566
  25.5 4.4 %collective-permute-start.10 = (bf16[272,128]{1,0:T(8,128)(2,1)S(1)}, bf16[272,128]{1,0:T(8,128)(2,1)S(1)}, u32[]{:S(2)}, u32[]{:S(2)}) collective-permute-start(bf16[272,128]{1,0:T(8,128)(2,1)S(1)} %add_add_fusion.1), channel_id=1, source_target_pairs={{0,4},{1,25},{2,6},{3,27},{4,0},{5,29},{6,2},{7,31},{8,12},{9,17},... | collective-permute-start | bytes 208904 | tf_op jit(solution)/shard_map/ppermute | solution.py:566
  27.0 4.3 %collective-permute-start.9 = (bf16[272,128]{1,0:T(8,128)(2,1)S(1)}, bf16[272,128]{1,0:T(8,128)(2,1)S(1)}, u32[]{:S(2)}, u32[]{:S(2)}) collective-permute-start(bf16[272,128]{1,0:T(8,128)(2,1)S(1)} %add_add_fusion.1), channel_id=1, source_target_pairs={{0,4},{1,17},{2,6},{3,19},{4,0},{5,21},{6,2},{7,23},{8,12},{9,25},... | collective-permute-start | bytes 208904 | tf_op jit(solution)/shard_map/ppermute | solution.py:566
  27.5 4.5 %collective-permute-start.8 = (bf16[272,128]{1,0:T(8,128)(2,1)S(1)}, bf16[272,128]{1,0:T(8,128)(2,1)S(1)}, u32[]{:S(2)}, u32[]{:S(2)}) collective-permute-start(bf16[272,128]{1,0:T(8,128)(2,1)S(1)} %add_add_fusion.1), channel_id=1, source_target_pairs={{0,4},{1,9},{2,6},{3,11},{4,0},{5,13},{6,2},{7,15},{8,12},{9,1},{1... | collective-permute-start | bytes 208904 | tf_op jit(solution)/shard_map/ppermute | solution.py:566
  32.1 1.4 %collective-permute-start.11 = (f32[272,128]{1,0:T(8,128)S(1)}, f32[272,128]{1,0:T(8,128)S(1)}, u32[]{:S(2)}, u32[]{:S(2)}) collective-permute-start(f32[272,128]{1,0:T(8,128)S(1)} %add_add_fusion.mine_ref), channel_id=1, source_target_pairs={{0,1},{1,0},{2,3},{3,2},{4,5},{5,4},{6,7},{7,6},{8,9},{9,8},{10,11... | collective-permute-start | bytes 417800 | tf_op jit(solution)/shard_map/ppermute | solution.py:560

commit v4 on v3

--- a/solution.py
+++ b/solution.py
@@ -518,12 +518,12 @@
     blocks = gate_ref.shape[1] // LANES
 
     def write(sums_ref):
+        rest = sums_ref[blocks * 2 * heads:].astype(F32)
         for i in range(blocks):
             at = slice(i * LANES, (i + 1) * LANES)
-            gate_ref[:, at] = sums_ref[i * 2 * heads:(i + 1) * 2 * heads]
-            coef_ref[:, at] = sums_ref[blocks * 2 * heads + i:blocks * 2 * heads + i + 1]
-        at = blocks * (2 * heads + 1)
-        rate_ref[...] = sums_ref[at:at + 1, :heads]
+            gate_ref[:, at] = sums_ref[i * 2 * heads:(i + 1) * 2 * heads].astype(F32)
+            coef_ref[:, at] = rest[i:i + 1]
+        rate_ref[...] = rest[blocks:blocks + 1, :heads]
 
     pl.when(is_odd(me_ref))(lambda: write(mine_ref))
     pl.when(jnp.logical_not(is_odd(me_ref)))(lambda: write(theirs_ref))
@@ -562,7 +562,7 @@
 
 def odd_swapped(value, distance, stage):
     count = lax.axis_size(EVERYONE)
-    idle = 8 if stage == 2 and count > 8 else 4
+    idle = 8 if stage == 2 and count > 8 else 2 if distance == 2 * stage else 4
     return lax.ppermute(value, EVERYONE, [(i, i ^ (distance if i % 2 else idle)) for i in range(count)])
 
 
@@ -667,10 +667,11 @@
         if distance == 2:
             sums, dx, dq, dk, dv = lax.optimization_barrier((sums, dx, dq, dk, dv))
         distance *= 4
+    sums = sums.astype(BF16)
     gate, d_coef, d_rate = call(
         functools.partial(last_kernel, heads),
         [((2 * heads, width), F32), ((1, width), F32), ((1, heads), F32)],
-        (me, sums, swapped(sums, "seq", 1)),
+        (me, sums, swapped(sums, EVERYONE, 1)),
         "last",
     )
     return (dq[None], dk[None], dv[None], dx[None], gate.T, d_coef.reshape(width), d_rate.reshape(heads))

time: 34.4 us -> 34.4 us (level)
  waiting for transfers between devices: 6.92 us -> 7.59 us
  starting transfers between devices: 13.2 us -> 12.6 us
    ppermute x6, waiting for transfers between devices: 4.39 us -> 5.16 us  [odd_swapped(): lax.ppermute(value, EVERYONE, [(i, i ^ (distance if i % 2 else idle)) for...]
    ppermute x6, starting transfers between devices: 7.77 us -> 7.16 us  [odd_swapped(): lax.ppermute(value, EVERYONE, [(i, i ^ (distance if i % 2 else idle)) for...]
  transfers between devices with their start and end apart: 12 -> 12, of which waited for: 8 -> 8; matrix products, arithmetic and copies ran while one was open for 0% -> 0% of each run, Pallas kernels for 21% -> 20%
where the time goes in v4:
time: 34.4 us; the launch traced here: 34.3 us
  Pallas kernels  13.3 us (39%)
  starting transfers between devices  12.6 us (37%)
  waiting for transfers between devices  7.59 us (22%)
  between operations  0.74 us (2%)
    pallas_call x10, Pallas kernels, call(): pl.pallas_call(kernel, out_shape=tuple((jax.ShapeDtypeStruct(*out) for ou...  13.3 us
    ppermute x6, starting transfers between devices, odd_swapped(): lax.ppermute(value, EVERYONE, [(i, i ^ (distance if i % 2 else idle)) for...  7.16 us
    ppermute x6, waiting for transfers between devices, odd_swapped(): lax.ppermute(value, EVERYONE, [(i, i ^ (distance if i % 2 else idle)) for...  5.16 us
    ppermute x2, starting transfers between devices, inner_swapped(): return lax.ppermute(value, EVERYONE, pairs)  4.37 us
    ppermute x4, waiting for transfers between devices, swapped(): lax.ppermute(value, axis, [(i, i ^ distance) for i in range(lax.axis_size...  2.41 us
    ppermute x4, starting transfers between devices, swapped(): lax.ppermute(value, axis, [(i, i ^ distance) for i in range(lax.axis_size...  1.08 us
  transfers between devices with their start and end apart: 12, of which 8 were waited for; matrix products, arithmetic and copies ran while one was open for 0% of the time, Pallas kernels for 20%

profile of v4, /device:TPU:0, one launch (start us, length us, event | category | flops | bytes accessed | tf_op | source)
XLA Modules:
  0.0 34.3 jit_solution(12784698699680205266)
XLA Ops:
  0.6 2.9 %prep.1 = (bf16[128,1024]{1,0:T(8,128)(2,1)S(1)}, bf16[128,1024]{1,0:T(8,128)(2,1)S(1)}, f32[128,128]{1,0:T(8,128)S(1)}, bf16[208,1024]{1,0:T(8,128)(2,1)S(1)}, ...) custom-call(s32[1]{0:T(128)} %bitcast.me_ref, ...), custom_call_target="tpu_custom_call" | custom-call | flops 100000000 | bytes 3000000 | tf_op jit(solution)/shard_map/prep/pallas_call | solution.py:542
  3.5 0.5 %collective-permute-start = (bf16[208,1024]{1,0:T(8,128)(2,1)S(1)}, bf16[208,1024]{1,0:T(8,128)(2,1)S(1)}, u32[]{:S(2)}, u32[]{:S(2)}) collective-permute-start(bf16[208,1024]{1,0:T(8,128)(2,1)S(1)} %get-tuple-element.65), channel_id=1, source_target_pairs={{0,1},{1,0},{2,3},{3,2},{4,5},{5,4},{6,7},{7,6},{8,9},{9,8},{10,11... | collective-permute-start | bytes 1277960 | tf_op jit(solution)/shard_map/ppermute | solution.py:560
  4.0 2.6 %collective-permute-start.1 = (bf16[144,1024]{1,0:T(8,128)(2,1)S(1)}, bf16[144,1024]{1,0:T(8,128)(2,1)S(1)}, u32[]{:S(2)}, u32[]{:S(2)}) collective-permute-start(bf16[144,1024]{1,0:T(8,128)(2,1)S(1)} %get-tuple-element.66), channel_id=1, source_target_pairs={{0,4},{1,2},{2,1},{3,7},{4,0},{5,6},{6,5},{7,3},{8,12},{9,10},{10,... | collective-permute-start | bytes 884744 | tf_op jit(solution)/shard_map/ppermute | solution.py:576
  6.7 0.0 collective-permute-done.rim_ref.near_ref
  6.7 0.5 %join_near.1 = (f32[64,1024]{1,0:T(8,128)S(1)}, bf16[64,1024]{1,0:T(8,128)(2,1)S(1)}) custom-call(s32[1]{0:T(128)} %bitcast.me_ref, f32[128,128]{1,0:T(8,128)S(1)} %get-tuple-element.62.small_ref.own_ref.edge_ref, f32[128,128]{1,0:T(8,128)S(1)} %get-tuple-element.62.small_ref.own_ref.edge_ref, f32[128,128]{1,0:T(8,128)S(1)} %get-tuple-element.62.small_ref.own_ref.edge_ref, ...), custom_call_target="tpu_custom_call" | custom-call | flops 100000000 | bytes 3000000 | tf_op jit(solution)/shard_map/join_near/pallas_call | solution.py:542
  7.2 1.8 %collective-permute-start.2 = (bf16[64,1024]{1,0:T(8,128)(2,1)S(1)}, bf16[64,1024]{1,0:T(8,128)(2,1)S(1)}, u32[]{:S(2)}, u32[]{:S(2)}) collective-permute-start(bf16[64,1024]{1,0:T(8,128)(2,1)S(1)} %get-tuple-element.82), channel_id=1, source_target_pairs={{0,4},{1,2},{2,1},{3,7},{4,0},{5,6},{6,5},{7,3},{8,12},{9,10},{10,... | collective-permute-start | bytes 393224 | tf_op jit(solution)/shard_map/ppermute | solution.py:576
  8.9 1.8 %own.1 = (f32[128,1024]{1,0:T(8,128)S(1)}, f32[128,1024]{1,0:T(8,128)S(1)}, f32[128,1024]{1,0:T(8,128)S(1)}, f32[128,16]{1,0:T(8,128)S(1)}) custom-call(s32[1]{0:T(128)} %bitcast.me_ref, f32[128,128]{1,0:T(8,128)S(1)} %get-tuple-element.62.small_ref.own_ref.edge_ref, bf16[128,1024]{1,0:T(8,128)(2,1)S(1)} %get-tuple-element.63.wk_ref, ...), custom_call_target="tpu_custom_call" | custom-call | flops 700000000 | bytes 7000000 | tf_op jit(solution)/shard_map/own/pallas_call | solution.py:542
  10.8 1.5 %edge_near.1 = (f32[64,1024]{1,0:T(8,128)S(1)}, f32[64,1024]{1,0:T(8,128)S(1)}, f32[64,16]{1,0:T(8,128)S(1)}, f32[400,1024]{1,0:T(8,128)S(1)}) custom-call(s32[1]{0:T(128)} %bitcast.me_ref, f32[128,128]{1,0:T(8,128)S(1)} %get-tuple-element.62.small_ref.own_ref.edge_ref, bf16[128,1024]{1,0:T(8,128)(2,1)S(1)} %get-tuple-element.63.wk_ref, ...), custom_call_target="tpu_custom_call" | custom-call | flops 200000000 | bytes 5000000 | tf_op jit(solution)/shard_map/edge_near/pallas_call | solution.py:542
  12.2 0.0 collective-permute-done.1.rim_ref.far_ref
  12.2 0.5 %join_far.1 = (f32[64,1024]{1,0:T(8,128)S(1)}, f32[64,1024]{1,0:T(8,128)S(1)}, f32[1,1024]{1,0:T(1,128)S(1)}) custom-call(s32[1]{0:T(128)} %bitcast.me_ref, f32[128,16]{1,0:T(8,128)S(1)} %get-tuple-element.71.own_ref.dl_ref, f32[64,16]{1,0:T(8,128)S(1)} %get-tuple-element.75.edge_ref.near_dl_ref, ...), custom_call_target="tpu_custom_call" | custom-call | flops 100000000 | bytes 3000000 | tf_op jit(solution)/shard_map/join_far/pallas_call | solution.py:542
  12.7 0.0 collective-permute-done.2.state_ref.cross_ref
  12.8 0.3 collective-permute-start.3
  13.1 1.1 %edge_far.1 = (f32[64,1024]{1,0:T(8,128)S(1)}, f32[64,1024]{1,0:T(8,128)S(1)}, f32[64,16]{1,0:T(8,128)S(1)}) custom-call(s32[1]{0:T(128)} %bitcast.me_ref, f32[128,128]{1,0:T(8,128)S(1)} %get-tuple-element.62.small_ref.own_ref.edge_ref, bf16[128,1024]{1,0:T(8,128)(2,1)S(1)} %get-tuple-element.63.wk_ref, bf16[128,1024]{1,0:T(8,128)(2,1)S(1)} %get-tuple-element.64.qf_ref, ...), custom_call_target="tpu_custom_call" | custom-call | flops 200000000 | bytes 3000000 | tf_op jit(solution)/shard_map/edge_far/pallas_call | solution.py:542
  14.1 0.1 collective-permute-done.3.passed_ref
  14.2 2.6 %finish.1 = (f32[128,1024]{1,0:T(8,128)S(1)}, f32[128,1024]{1,0:T(8,128)S(1)}, bf16[128,1024]{1,0:T(8,128)(2,1)S(1)}, f32[128,32]{1,0:T(8,128)S(1)}, bf16[272,128]{1,0:T(8,128)(2,1)S(1)}) custom-call(s32[1]{0:T(128)} %bitcast.me_ref, bf16[128,1024]{1,0:T(8,128)(2,1)S(1)} %get-tuple-element.55.q_ref, bf16[128,1024]{1,0:T(8,128)(2,1)S(1)} %get-tuple-element.56.k_ref, ...), custom_call_target="tpu_custom_call" | custom-call | flops 100000000 | bytes 3000000 | tf_op jit(solution)/shard_map/finish/pallas_call | solution.py:542
  16.9 0.3 collective-permute-start.4
  17.1 1.1 %collective-permute-done.4 = bf16[272,128]{1,0:T(8,128)(2,1)S(1)} collective-permute-done((bf16[272,128]{1,0:T(8,128)(2,1)S(1)}, bf16[272,128]{1,0:T(8,128)(2,1)S(1)}, u32[]{:S(2)}, u32[]{:S(2)}) %collective-permute-start.4) | collective-permute-done | bytes 69664 | tf_op jit(solution)/shard_map/ppermute | solution.py:560
  18.2 2.1 %collective-permute-start.7 = (bf16[272,128]{1,0:T(8,128)(2,1)S(1)}, bf16[272,128]{1,0:T(8,128)(2,1)S(1)}, u32[]{:S(2)}, u32[]{:S(2)}) collective-permute-start(bf16[272,128]{1,0:T(8,128)(2,1)S(1)} %add_convert_fusion.1), channel_id=1, source_target_pairs={{0,8},{1,7},{2,10},{3,5},{4,12},{5,3},{6,14},{7,1},{8,0},{9,15},{1... | collective-permute-start | bytes 208904 | tf_op jit(solution)/shard_map/ppermute | solution.py:566
  20.4 0.1 collective-permute-start.6
  20.4 1.9 %collective-permute-start.5 = (bf16[272,128]{1,0:T(8,128)(2,1)S(1)}, bf16[272,128]{1,0:T(8,128)(2,1)S(1)}, u32[]{:S(2)}, u32[]{:S(2)}) collective-permute-start(bf16[272,128]{1,0:T(8,128)(2,1)S(1)} %add_convert_fusion.1), channel_id=1, source_target_pairs={{0,8},{1,3},{2,10},{3,1},{4,12},{5,7},{6,14},{7,5},{8,0},{9,11},{1... | collective-permute-start | bytes 208904 | tf_op jit(solution)/shard_map/ppermute | solution.py:566
  22.4 1.7 %outputs.1 = (bf16[128,1024]{1,0:T(8,128)(2,1)}, bf16[128,1024]{1,0:T(8,128)(2,1)}, bf16[128,1024]{1,0:T(8,128)(2,1)}, bf16[128,1024]{1,0:T(8,128)(2,1)}) custom-call(s32[1]{0:T(128)} %bitcast.me_ref, f32[128,32]{1,0:T(8,128)S(1)} %get-tuple-element.86.logits_ref, f32[32,1024]{1,0:T(8,128)S(1)} %get-tuple-element.87.w_ref, ...), custom_call_target="tpu_custom_call" | custom-call | flops 100000000 | bytes 3000000 | tf_op jit(solution)/shard_map/outputs/pallas_call | solution.py:542
  24.1 0.6 %collective-permute-done.6 = bf16[272,128]{1,0:T(8,128)(2,1)S(1)} collective-permute-done((bf16[272,128]{1,0:T(8,128)(2,1)S(1)}, bf16[272,128]{1,0:T(8,128)(2,1)S(1)}, u32[]{:S(2)}, u32[]{:S(2)}) %collective-permute-start.6) | collective-permute-done | bytes 69664 | tf_op jit(solution)/shard_map/ppermute | solution.py:566
  24.7 0.7 %collective-permute-done.5 = bf16[272,128]{1,0:T(8,128)(2,1)S(1)} collective-permute-done((bf16[272,128]{1,0:T(8,128)(2,1)S(1)}, bf16[272,128]{1,0:T(8,128)(2,1)S(1)}, u32[]{:S(2)}, u32[]{:S(2)}) %collective-permute-start.5) | collective-permute-done | bytes 69664 | tf_op jit(solution)/shard_map/ppermute | solution.py:566
  25.5 1.6 %collective-permute-start.10 = (bf16[272,128]{1,0:T(8,128)(2,1)S(1)}, bf16[272,128]{1,0:T(8,128)(2,1)S(1)}, u32[]{:S(2)}, u32[]{:S(2)}) collective-permute-start(bf16[272,128]{1,0:T(8,128)(2,1)S(1)} %add_add_fusion), channel_id=1, source_target_pairs={{0,4},{1,25},{2,6},{3,27},{4,0},{5,29},{6,2},{7,31},{8,12},{9,17},... | collective-permute-start | bytes 208904 | tf_op jit(solution)/shard_map/ppermute | solution.py:566
  27.0 0.9 %collective-permute-start.9 = (bf16[272,128]{1,0:T(8,128)(2,1)S(1)}, bf16[272,128]{1,0:T(8,128)(2,1)S(1)}, u32[]{:S(2)}, u32[]{:S(2)}) collective-permute-start(bf16[272,128]{1,0:T(8,128)(2,1)S(1)} %add_add_fusion), channel_id=1, source_target_pairs={{0,2},{1,17},{2,0},{3,19},{4,6},{5,21},{6,4},{7,23},{8,10},{9,25},... | collective-permute-start | bytes 208904 | tf_op jit(solution)/shard_map/ppermute | solution.py:566
  27.9 0.5 %collective-permute-start.8 = (bf16[272,128]{1,0:T(8,128)(2,1)S(1)}, bf16[272,128]{1,0:T(8,128)(2,1)S(1)}, u32[]{:S(2)}, u32[]{:S(2)}) collective-permute-start(bf16[272,128]{1,0:T(8,128)(2,1)S(1)} %add_add_fusion), channel_id=1, source_target_pairs={{0,4},{1,9},{2,6},{3,11},{4,0},{5,13},{6,2},{7,15},{8,12},{9,1},{1... | collective-permute-start | bytes 208904 | tf_op jit(solution)/shard_map/ppermute | solution.py:566
  28.4 1.4 %collective-permute-done.10 = bf16[272,128]{1,0:T(8,128)(2,1)S(1)} collective-permute-done((bf16[272,128]{1,0:T(8,128)(2,1)S(1)}, bf16[272,128]{1,0:T(8,128)(2,1)S(1)}, u32[]{:S(2)}, u32[]{:S(2)}) %collective-permute-start.10) | collective-permute-done | bytes 69664 | tf_op jit(solution)/shard_map/ppermute | solution.py:566
  29.8 1.5 %collective-permute-done.9 = bf16[272,128]{1,0:T(8,128)(2,1)S(1)} collective-permute-done((bf16[272,128]{1,0:T(8,128)(2,1)S(1)}, bf16[272,128]{1,0:T(8,128)(2,1)S(1)}, u32[]{:S(2)}, u32[]{:S(2)}) %collective-permute-start.9) | collective-permute-done | bytes 69664 | tf_op jit(solution)/shard_map/ppermute | solution.py:566
  31.3 0.9 %collective-permute-done.8 = bf16[272,128]{1,0:T(8,128)(2,1)S(1)} collective-permute-done((bf16[272,128]{1,0:T(8,128)(2,1)S(1)}, bf16[272,128]{1,0:T(8,128)(2,1)S(1)}, u32[]{:S(2)}, u32[]{:S(2)}) %collective-permute-start.8) | collective-permute-done | bytes 69664 | tf_op jit(solution)/shard_map/ppermute | solution.py:566
  32.3 0.1 collective-permute-start.11
  32.4 1.2 %collective-permute-done.11.theirs_ref = bf16[272,128]{1,0:T(8,128)(2,1)S(1)} collective-permute-done((bf16[272,128]{1,0:T(8,128)(2,1)S(1)}, bf16[272,128]{1,0:T(8,128)(2,1)S(1)}, u32[]{:S(2)}, u32[]{:S(2)}) %collective-permute-start.11) | collective-permute-done | bytes 69664 | tf_op jit(solution)/shard_map/ppermute | solution.py:560
  33.6 0.7 %last.1 = (f32[32,1024]{1,0:T(8,128)}, f32[1,1024]{1,0:T(1,128)}, f32[1,16]{1,0:T(1,128)}) custom-call(s32[1]{0:T(128)} %bitcast.me_ref, bf16[272,128]{1,0:T(8,128)(2,1)S(1)} %add_convert_fusion.mine_ref, bf16[272,128]{1,0:T(8,128)(2,1)S(1)} %collective-permute-done.11.theirs_ref), custom_call_target="tpu_custom_call" | custom-call | flops 100000000 | bytes 3000000 | tf_op jit(solution)/shard_map/last/pallas_call | solution.py:542
  (5 shorter events, 0.1 us)
Async XLA Ops:
  3.5 3.1 %collective-permute-start = (bf16[208,1024]{1,0:T(8,128)(2,1)S(1)}, bf16[208,1024]{1,0:T(8,128)(2,1)S(1)}, u32[]{:S(2)}, u32[]{:S(2)}) collective-permute-start(bf16[208,1024]{1,0:T(8,128)(2,1)S(1)} %get-tuple-element.65), channel_id=1, source_target_pairs={{0,1},{1,0},{2,3},{3,2},{4,5},{5,4},{6,7},{7,6},{8,9},{9,8},{10,11... | collective-permute-start | bytes 1277960 | tf_op jit(solution)/shard_map/ppermute | solution.py:560
  4.0 8.2 %collective-permute-start.1 = (bf16[144,1024]{1,0:T(8,128)(2,1)S(1)}, bf16[144,1024]{1,0:T(8,128)(2,1)S(1)}, u32[]{:S(2)}, u32[]{:S(2)}) collective-permute-start(bf16[144,1024]{1,0:T(8,128)(2,1)S(1)} %get-tuple-element.66), channel_id=1, source_target_pairs={{0,4},{1,2},{2,1},{3,7},{4,0},{5,6},{6,5},{7,3},{8,12},{9,10},{10,... | collective-permute-start | bytes 884744 | tf_op jit(solution)/shard_map/ppermute | solution.py:576
  7.2 5.6 %collective-permute-start.2 = (bf16[64,1024]{1,0:T(8,128)(2,1)S(1)}, bf16[64,1024]{1,0:T(8,128)(2,1)S(1)}, u32[]{:S(2)}, u32[]{:S(2)}) collective-permute-start(bf16[64,1024]{1,0:T(8,128)(2,1)S(1)} %get-tuple-element.82), channel_id=1, source_target_pairs={{0,4},{1,2},{2,1},{3,7},{4,0},{5,6},{6,5},{7,3},{8,12},{9,10},{10,... | collective-permute-start | bytes 393224 | tf_op jit(solution)/shard_map/ppermute | solution.py:576
  12.8 1.4 %collective-permute-start.3 = (bf16[64,1024]{1,0:T(8,128)(2,1)S(1)}, bf16[64,1024]{1,0:T(8,128)(2,1)S(1)}, u32[]{:S(2)}, u32[]{:S(2)}) collective-permute-start(bf16[64,1024]{1,0:T(8,128)(2,1)S(1)} %pass_on.1), channel_id=1, source_target_pairs={{0,1},{1,0},{2,3},{3,2},{4,5},{5,4},{6,7},{7,6},{8,9},{9,8},{10,11... | collective-permute-start | bytes 393224 | tf_op jit(solution)/shard_map/ppermute | solution.py:560
  16.9 1.3 %collective-permute-start.4 = (bf16[272,128]{1,0:T(8,128)(2,1)S(1)}, bf16[272,128]{1,0:T(8,128)(2,1)S(1)}, u32[]{:S(2)}, u32[]{:S(2)}) collective-permute-start(bf16[272,128]{1,0:T(8,128)(2,1)S(1)} %get-tuple-element.85), channel_id=1, source_target_pairs={{0,1},{1,0},{2,3},{3,2},{4,5},{5,4},{6,7},{7,6},{8,9},{9,8},{10,11... | collective-permute-start | bytes 208904 | tf_op jit(solution)/shard_map/ppermute | solution.py:560
  18.2 5.8 %collective-permute-start.7 = (bf16[272,128]{1,0:T(8,128)(2,1)S(1)}, bf16[272,128]{1,0:T(8,128)(2,1)S(1)}, u32[]{:S(2)}, u32[]{:S(2)}) collective-permute-start(bf16[272,128]{1,0:T(8,128)(2,1)S(1)} %add_convert_fusion.1), channel_id=1, source_target_pairs={{0,8},{1,7},{2,10},{3,5},{4,12},{5,3},{6,14},{7,1},{8,0},{9,15},{1... | collective-permute-start | bytes 208904 | tf_op jit(solution)/shard_map/ppermute | solution.py:566
  20.4 4.3 %collective-permute-start.6 = (bf16[272,128]{1,0:T(8,128)(2,1)S(1)}, bf16[272,128]{1,0:T(8,128)(2,1)S(1)}, u32[]{:S(2)}, u32[]{:S(2)}) collective-permute-start(bf16[272,128]{1,0:T(8,128)(2,1)S(1)} %add_convert_fusion.1), channel_id=1, source_target_pairs={{0,8},{1,5},{2,10},{3,7},{4,12},{5,1},{6,14},{7,3},{8,0},{9,13},{1... | collective-permute-start | bytes 208904 | tf_op jit(solution)/shard_map/ppermute | solution.py:566
  20.4 5.0 %collective-permute-start.5 = (bf16[272,128]{1,0:T(8,128)(2,1)S(1)}, bf16[272,128]{1,0:T(8,128)(2,1)S(1)}, u32[]{:S(2)}, u32[]{:S(2)}) collective-permute-start(bf16[272,128]{1,0:T(8,128)(2,1)S(1)} %add_convert_fusion.1), channel_id=1, source_target_pairs={{0,8},{1,3},{2,10},{3,1},{4,12},{5,7},{6,14},{7,5},{8,0},{9,11},{1... | collective-permute-start | bytes 208904 | tf_op jit(solution)/shard_map/ppermute | solution.py:566
  25.5 4.4 %collective-permute-start.10 = (bf16[272,128]{1,0:T(8,128)(2,1)S(1)}, bf16[272,128]{1,0:T(8,128)(2,1)S(1)}, u32[]{:S(2)}, u32[]{:S(2)}) collective-permute-start(bf16[272,128]{1,0:T(8,128)(2,1)S(1)} %add_add_fusion), channel_id=1, source_target_pairs={{0,4},{1,25},{2,6},{3,27},{4,0},{5,29},{6,2},{7,31},{8,12},{9,17},... | collective-permute-start | bytes 208904 | tf_op jit(solution)/shard_map/ppermute | solution.py:566
  27.0 4.3 %collective-permute-start.9 = (bf16[272,128]{1,0:T(8,128)(2,1)S(1)}, bf16[272,128]{1,0:T(8,128)(2,1)S(1)}, u32[]{:S(2)}, u32[]{:S(2)}) collective-permute-start(bf16[272,128]{1,0:T(8,128)(2,1)S(1)} %add_add_fusion), channel_id=1, source_target_pairs={{0,2},{1,17},{2,0},{3,19},{4,6},{5,21},{6,4},{7,23},{8,10},{9,25},... | collective-permute-start | bytes 208904 | tf_op jit(solution)/shard_map/ppermute | solution.py:566
  27.9 4.3 %collective-permute-start.8 = (bf16[272,128]{1,0:T(8,128)(2,1)S(1)}, bf16[272,128]{1,0:T(8,128)(2,1)S(1)}, u32[]{:S(2)}, u32[]{:S(2)}) collective-permute-start(bf16[272,128]{1,0:T(8,128)(2,1)S(1)} %add_add_fusion), channel_id=1, source_target_pairs={{0,4},{1,9},{2,6},{3,11},{4,0},{5,13},{6,2},{7,15},{8,12},{9,1},{1... | collective-permute-start | bytes 208904 | tf_op jit(solution)/shard_map/ppermute | solution.py:566
  32.3 1.3 %collective-permute-start.11 = (bf16[272,128]{1,0:T(8,128)(2,1)S(1)}, bf16[272,128]{1,0:T(8,128)(2,1)S(1)}, u32[]{:S(2)}, u32[]{:S(2)}) collective-permute-start(bf16[272,128]{1,0:T(8,128)(2,1)S(1)} %add_convert_fusion.mine_ref), channel_id=1, source_target_pairs={{0,1},{1,0},{2,3},{3,2},{4,5},{5,4},{6,7},{7,6},{8,9},{9,8},{10,11... | collective-permute-start | bytes 208904 | tf_op jit(solution)/shard_map/ppermute | solution.py:560

commit v5 on v4

--- a/solution.py
+++ b/solution.py
@@ -132,7 +132,7 @@
     slope = jax.nn.sigmoid(decay_logit)
     gamma = jax.nn.sigmoid(logits[:, heads:]) * (1.0 / WINDOW)
     copies[2].wait()
-    total = mask_dot(lower, -rate_buf[...] * soft, 3)
+    total = mask_dot(lower, -rate_buf[...] * soft, 2)
     small_ref[...] = jnp.concatenate(
         [total, gamma, soft, slope, jnp.zeros((length, LANES - 4 * heads), F32)], axis=1
     )
@@ -151,7 +151,7 @@
     qf_ref[...] = qf
     copies[6].wait()
     copies[7].wait()
-    kept = mask_dot(window_own_t(length), jnp.exp(total[length - 1:] - total), 2)
+    kept = mask_dot(window_own_t(length), jnp.exp(total[length - 1:] - total), 1)
     faded = jnp.exp(total[late:] - total[late - 1:late])
     scale = expand(jnp.concatenate([kept, faded], axis=0), table)
     carried = (wk.astype(F32) * scale[:length]).astype(BF16)
@@ -219,7 +219,7 @@
     middle = total[length - WINDOW - 1:length - WINDOW]
     next_total = next_decay(rim_ref, heads)
     before = is_odd(me_ref) if before_if_odd else jnp.logical_not(is_odd(me_ref))
-    kept = mask_dot(window_rim_t(), jnp.exp(middle - total[:WINDOW]), 2)
+    kept = mask_dot(window_rim_t(), jnp.exp(middle - total[:WINDOW]), 1)
     scale = jnp.where(everywhere(before, kept.shape), kept, jnp.exp(next_total))
     fade = jnp.exp(last - middle)
     weight = jnp.where(
@@ -314,7 +314,7 @@
     late = length - WINDOW
     total, gamma = small_ref[:, :heads], small_ref[:, heads:2 * heads]
     last, middle = total[length - 1:], total[late - 1:late]
-    own = mask_dot(window_own_t(length), jnp.exp(last - total), 2)
+    own = mask_dot(window_own_t(length), jnp.exp(last - total), 1)
     grown = jnp.exp(jnp.concatenate([total[:late], total[late:] - middle], axis=0))
     rest = [jnp.exp(middle), jnp.exp(last - middle), jnp.zeros((BAND - 2, heads), F32)]
     scales = jnp.concatenate([own, grown, gamma] + rest, axis=0)
@@ -408,10 +408,10 @@
     total, gamma, soft, slope = (small[:, i * heads:(i + 1) * heads] for i in range(4))
     last, middle = total[length - 1:], total[late - 1:late]
     tail = jnp.exp(last - total)
-    own = mask_dot(window_own_t(length), tail, 2)
+    own = mask_dot(window_own_t(length), tail, 1)
     next_total = next_decay(bwd_ref, heads)
     next_middle = next_total[WINDOW - 1:]
-    onward = mask_dot(window_rim_t(), jnp.exp(next_middle - next_total), 2)
+    onward = mask_dot(window_rim_t(), jnp.exp(next_middle - next_total), 1)
     grown = jnp.exp(jnp.concatenate([total[:late], total[late:] - middle], axis=0))
     fade = jnp.exp(last - middle)
     onward_x = expand(jnp.concatenate([onward, jnp.exp(next_middle)], axis=0), table)
@@ -431,7 +431,7 @@
     after = jnp.where(odd, far_part, near_part) + next_x * later
     halfway = middle_x * start + jnp.where(odd, near_part, far_part)
     half_after = adjoint_ref[...] + fade_x * after
-    d_state = jnp.sum(head_sum(after * halfway, table, 2), axis=0, keepdims=True)
+    d_state = jnp.sum(head_sum(after * halfway, table), axis=0, keepdims=True)
     start, later, after, halfway, half_after = (
         z.astype(BF16) for z in (start, later, after, halfway, half_after)
     )
@@ -477,14 +477,14 @@
     sums = dot_nt(sums, table)
     d_own, d_out, d_gamma = (sums[i * length:(i + 1) * length] for i in range(3))
     d_rim = sums[3 * length:]
-    d_tail = tail * mask_dot(window_own(length), d_own, 2)
-    rim_tail = jnp.exp(middle - total[:late]) * mask_dot(window_rim(), d_rim, 2)
+    d_tail = tail * mask_dot(window_own(length), d_own, 1)
+    rim_tail = jnp.exp(middle - total[:late]) * mask_dot(window_rim(), d_rim, 1)
     at_end = jnp.sum(own * d_own, axis=0, keepdims=True) + fade * d_state
     d_total = dl_ref[...] + grown * d_out - d_tail
     d_total = jnp.concatenate([d_total[:late] + rim_dl_ref[...] - rim_tail, d_total[late:]], axis=0)
     d_total = d_total + jnp.where(iota((length, heads), 0) == length - 1, at_end, 0.0)
     upper = (iota((length, length), 1) >= iota((length, length), 0)).astype(BF16)
-    d_decay = mask_dot(upper, d_total, 3)
+    d_decay = mask_dot(upper, d_total, 2)
     d_rate = -jnp.sum(d_decay * soft, axis=0, keepdims=True)
     d_logits = jnp.concatenate(
         [-rate_ref[...] * d_decay * slope, d_gamma * gamma * (1.0 - WINDOW * gamma)], axis=1

time: 34.4 us -> 34.5 us (level)
  transfers between devices with their start and end apart: 12 -> 12, of which waited for: 8 -> 9; matrix products, arithmetic and copies ran while one was open for 0% -> 0% of each run, Pallas kernels for 20% -> 20%
where the time goes in v5:
time: 34.5 us; the launch traced here: 34.4 us
  Pallas kernels  13.3 us (39%)
  starting transfers between devices  12.5 us (36%)
  waiting for transfers between devices  7.77 us (23%)
  between operations  0.73 us (2%)
    pallas_call x10, Pallas kernels, call(): pl.pallas_call(kernel, out_shape=tuple((jax.ShapeDtypeStruct(*out) for ou...  13.3 us
    ppermute x6, starting transfers between devices, odd_swapped(): lax.ppermute(value, EVERYONE, [(i, i ^ (distance if i % 2 else idle)) for...  7.16 us
    ppermute x6, waiting for transfers between devices, odd_swapped(): lax.ppermute(value, EVERYONE, [(i, i ^ (distance if i % 2 else idle)) for...  5.16 us
    ppermute x2, starting transfers between devices, inner_swapped(): return lax.ppermute(value, EVERYONE, pairs)  4.37 us
    ppermute x4, waiting for transfers between devices, swapped(): lax.ppermute(value, axis, [(i, i ^ distance) for i in range(lax.axis_size...  2.52 us
    ppermute x4, starting transfers between devices, swapped(): lax.ppermute(value, axis, [(i, i ^ distance) for i in range(lax.axis_size...  0.97 us
  transfers between devices with their start and end apart: 12, of which 9 were waited for; matrix products, arithmetic and copies ran while one was open for 0% of the time, Pallas kernels for 20%

profile of v5, /device:TPU:0, one launch (start us, length us, event | category | flops | bytes accessed | tf_op | source)
XLA Modules:
  0.0 34.4 jit_solution(5066729183410213036)
XLA Ops:
  0.6 2.9 %prep.1 = (bf16[128,1024]{1,0:T(8,128)(2,1)S(1)}, bf16[128,1024]{1,0:T(8,128)(2,1)S(1)}, f32[128,128]{1,0:T(8,128)S(1)}, bf16[208,1024]{1,0:T(8,128)(2,1)S(1)}, ...) custom-call(s32[1]{0:T(128)} %bitcast.me_ref, ...), custom_call_target="tpu_custom_call" | custom-call | flops 100000000 | bytes 3000000 | tf_op jit(solution)/shard_map/prep/pallas_call | solution.py:542
  3.5 0.5 %collective-permute-start = (bf16[208,1024]{1,0:T(8,128)(2,1)S(1)}, bf16[208,1024]{1,0:T(8,128)(2,1)S(1)}, u32[]{:S(2)}, u32[]{:S(2)}) collective-permute-start(bf16[208,1024]{1,0:T(8,128)(2,1)S(1)} %get-tuple-element.65), channel_id=1, source_target_pairs={{0,1},{1,0},{2,3},{3,2},{4,5},{5,4},{6,7},{7,6},{8,9},{9,8},{10,11... | collective-permute-start | bytes 1277960 | tf_op jit(solution)/shard_map/ppermute | solution.py:560
  4.0 2.6 %collective-permute-start.1 = (bf16[144,1024]{1,0:T(8,128)(2,1)S(1)}, bf16[144,1024]{1,0:T(8,128)(2,1)S(1)}, u32[]{:S(2)}, u32[]{:S(2)}) collective-permute-start(bf16[144,1024]{1,0:T(8,128)(2,1)S(1)} %get-tuple-element.66), channel_id=1, source_target_pairs={{0,4},{1,2},{2,1},{3,7},{4,0},{5,6},{6,5},{7,3},{8,12},{9,10},{10,... | collective-permute-start | bytes 884744 | tf_op jit(solution)/shard_map/ppermute | solution.py:576
  6.6 0.0 collective-permute-done.rim_ref.near_ref
  6.6 0.5 %join_near.1 = (f32[64,1024]{1,0:T(8,128)S(1)}, bf16[64,1024]{1,0:T(8,128)(2,1)S(1)}) custom-call(s32[1]{0:T(128)} %bitcast.me_ref, f32[128,128]{1,0:T(8,128)S(1)} %get-tuple-element.62.small_ref.own_ref.edge_ref, f32[128,128]{1,0:T(8,128)S(1)} %get-tuple-element.62.small_ref.own_ref.edge_ref, f32[128,128]{1,0:T(8,128)S(1)} %get-tuple-element.62.small_ref.own_ref.edge_ref, ...), custom_call_target="tpu_custom_call" | custom-call | flops 100000000 | bytes 3000000 | tf_op jit(solution)/shard_map/join_near/pallas_call | solution.py:542
  7.1 1.8 %collective-permute-start.2 = (bf16[64,1024]{1,0:T(8,128)(2,1)S(1)}, bf16[64,1024]{1,0:T(8,128)(2,1)S(1)}, u32[]{:S(2)}, u32[]{:S(2)}) collective-permute-start(bf16[64,1024]{1,0:T(8,128)(2,1)S(1)} %get-tuple-element.82), channel_id=1, source_target_pairs={{0,4},{1,2},{2,1},{3,7},{4,0},{5,6},{6,5},{7,3},{8,12},{9,10},{10,... | collective-permute-start | bytes 393224 | tf_op jit(solution)/shard_map/ppermute | solution.py:576
  8.9 1.8 %own.1 = (f32[128,1024]{1,0:T(8,128)S(1)}, f32[128,1024]{1,0:T(8,128)S(1)}, f32[128,1024]{1,0:T(8,128)S(1)}, f32[128,16]{1,0:T(8,128)S(1)}) custom-call(s32[1]{0:T(128)} %bitcast.me_ref, f32[128,128]{1,0:T(8,128)S(1)} %get-tuple-element.62.small_ref.own_ref.edge_ref, bf16[128,1024]{1,0:T(8,128)(2,1)S(1)} %get-tuple-element.63.wk_ref, ...), custom_call_target="tpu_custom_call" | custom-call | flops 700000000 | bytes 7000000 | tf_op jit(solution)/shard_map/own/pallas_call | solution.py:542
  10.7 1.4 %edge_near.1 = (f32[64,1024]{1,0:T(8,128)S(1)}, f32[64,1024]{1,0:T(8,128)S(1)}, f32[64,16]{1,0:T(8,128)S(1)}, f32[400,1024]{1,0:T(8,128)S(1)}) custom-call(s32[1]{0:T(128)} %bitcast.me_ref, f32[128,128]{1,0:T(8,128)S(1)} %get-tuple-element.62.small_ref.own_ref.edge_ref, bf16[128,1024]{1,0:T(8,128)(2,1)S(1)} %get-tuple-element.63.wk_ref, ...), custom_call_target="tpu_custom_call" | custom-call | flops 200000000 | bytes 5000000 | tf_op jit(solution)/shard_map/edge_near/pallas_call | solution.py:542
  12.1 0.5 %join_far.1 = (f32[64,1024]{1,0:T(8,128)S(1)}, f32[64,1024]{1,0:T(8,128)S(1)}, f32[1,1024]{1,0:T(1,128)S(1)}) custom-call(s32[1]{0:T(128)} %bitcast.me_ref, f32[128,16]{1,0:T(8,128)S(1)} %get-tuple-element.71.own_ref.dl_ref, f32[64,16]{1,0:T(8,128)S(1)} %get-tuple-element.75.edge_ref.near_dl_ref, ...), custom_call_target="tpu_custom_call" | custom-call | flops 100000000 | bytes 3000000 | tf_op jit(solution)/shard_map/join_far/pallas_call | solution.py:542
  12.6 0.1 collective-permute-done.2.state_ref.cross_ref
  12.8 0.2 collective-permute-start.3
  13.0 1.1 %edge_far.1 = (f32[64,1024]{1,0:T(8,128)S(1)}, f32[64,1024]{1,0:T(8,128)S(1)}, f32[64,16]{1,0:T(8,128)S(1)}) custom-call(s32[1]{0:T(128)} %bitcast.me_ref, f32[128,128]{1,0:T(8,128)S(1)} %get-tuple-element.62.small_ref.own_ref.edge_ref, bf16[128,1024]{1,0:T(8,128)(2,1)S(1)} %get-tuple-element.63.wk_ref, bf16[128,1024]{1,0:T(8,128)(2,1)S(1)} %get-tuple-element.64.qf_ref, ...), custom_call_target="tpu_custom_call" | custom-call | flops 200000000 | bytes 3000000 | tf_op jit(solution)/shard_map/edge_far/pallas_call | solution.py:542
  14.0 0.2 collective-permute-done.3.passed_ref
  14.2 2.7 %finish.1 = (f32[128,1024]{1,0:T(8,128)S(1)}, f32[128,1024]{1,0:T(8,128)S(1)}, bf16[128,1024]{1,0:T(8,128)(2,1)S(1)}, f32[128,32]{1,0:T(8,128)S(1)}, bf16[272,128]{1,0:T(8,128)(2,1)S(1)}) custom-call(s32[1]{0:T(128)} %bitcast.me_ref, bf16[128,1024]{1,0:T(8,128)(2,1)S(1)} %get-tuple-element.55.q_ref, bf16[128,1024]{1,0:T(8,128)(2,1)S(1)} %get-tuple-element.56.k_ref, ...), custom_call_target="tpu_custom_call" | custom-call | flops 100000000 | bytes 3000000 | tf_op jit(solution)/shard_map/finish/pallas_call | solution.py:542
  16.9 0.2 collective-permute-start.4
  17.1 1.1 %collective-permute-done.4 = bf16[272,128]{1,0:T(8,128)(2,1)S(1)} collective-permute-done((bf16[272,128]{1,0:T(8,128)(2,1)S(1)}, bf16[272,128]{1,0:T(8,128)(2,1)S(1)}, u32[]{:S(2)}, u32[]{:S(2)}) %collective-permute-start.4) | collective-permute-done | bytes 69664 | tf_op jit(solution)/shard_map/ppermute | solution.py:560
  18.3 2.1 %collective-permute-start.7 = (bf16[272,128]{1,0:T(8,128)(2,1)S(1)}, bf16[272,128]{1,0:T(8,128)(2,1)S(1)}, u32[]{:S(2)}, u32[]{:S(2)}) collective-permute-start(bf16[272,128]{1,0:T(8,128)(2,1)S(1)} %add_convert_fusion.1), channel_id=1, source_target_pairs={{0,8},{1,7},{2,10},{3,5},{4,12},{5,3},{6,14},{7,1},{8,0},{9,15},{1... | collective-permute-start | bytes 208904 | tf_op jit(solution)/shard_map/ppermute | solution.py:566
  20.4 0.1 collective-permute-start.6
  20.5 1.9 %collective-permute-start.5 = (bf16[272,128]{1,0:T(8,128)(2,1)S(1)}, bf16[272,128]{1,0:T(8,128)(2,1)S(1)}, u32[]{:S(2)}, u32[]{:S(2)}) collective-permute-start(bf16[272,128]{1,0:T(8,128)(2,1)S(1)} %add_convert_fusion.1), channel_id=1, source_target_pairs={{0,8},{1,3},{2,10},{3,1},{4,12},{5,7},{6,14},{7,5},{8,0},{9,11},{1... | collective-permute-start | bytes 208904 | tf_op jit(solution)/shard_map/ppermute | solution.py:566
  22.4 1.7 %outputs.1 = (bf16[128,1024]{1,0:T(8,128)(2,1)}, bf16[128,1024]{1,0:T(8,128)(2,1)}, bf16[128,1024]{1,0:T(8,128)(2,1)}, bf16[128,1024]{1,0:T(8,128)(2,1)}) custom-call(s32[1]{0:T(128)} %bitcast.me_ref, f32[128,32]{1,0:T(8,128)S(1)} %get-tuple-element.86.logits_ref, f32[32,1024]{1,0:T(8,128)S(1)} %get-tuple-element.87.w_ref, ...), custom_call_target="tpu_custom_call" | custom-call | flops 100000000 | bytes 3000000 | tf_op jit(solution)/shard_map/outputs/pallas_call | solution.py:542
  24.1 0.0 collective-permute-done.7
  24.1 0.6 %collective-permute-done.6 = bf16[272,128]{1,0:T(8,128)(2,1)S(1)} collective-permute-done((bf16[272,128]{1,0:T(8,128)(2,1)S(1)}, bf16[272,128]{1,0:T(8,128)(2,1)S(1)}, u32[]{:S(2)}, u32[]{:S(2)}) %collective-permute-start.6) | collective-permute-done | bytes 69664 | tf_op jit(solution)/shard_map/ppermute | solution.py:566
  24.7 0.7 %collective-permute-done.5 = bf16[272,128]{1,0:T(8,128)(2,1)S(1)} collective-permute-done((bf16[272,128]{1,0:T(8,128)(2,1)S(1)}, bf16[272,128]{1,0:T(8,128)(2,1)S(1)}, u32[]{:S(2)}, u32[]{:S(2)}) %collective-permute-start.5) | collective-permute-done | bytes 69664 | tf_op jit(solution)/shard_map/ppermute | solution.py:566
  25.5 1.6 %collective-permute-start.10 = (bf16[272,128]{1,0:T(8,128)(2,1)S(1)}, bf16[272,128]{1,0:T(8,128)(2,1)S(1)}, u32[]{:S(2)}, u32[]{:S(2)}) collective-permute-start(bf16[272,128]{1,0:T(8,128)(2,1)S(1)} %add_add_fusion), channel_id=1, source_target_pairs={{0,4},{1,25},{2,6},{3,27},{4,0},{5,29},{6,2},{7,31},{8,12},{9,17},... | collective-permute-start | bytes 208904 | tf_op jit(solution)/shard_map/ppermute | solution.py:566
  27.1 0.9 %collective-permute-start.9 = (bf16[272,128]{1,0:T(8,128)(2,1)S(1)}, bf16[272,128]{1,0:T(8,128)(2,1)S(1)}, u32[]{:S(2)}, u32[]{:S(2)}) collective-permute-start(bf16[272,128]{1,0:T(8,128)(2,1)S(1)} %add_add_fusion), channel_id=1, source_target_pairs={{0,2},{1,17},{2,0},{3,19},{4,6},{5,21},{6,4},{7,23},{8,10},{9,25},... | collective-permute-start | bytes 208904 | tf_op jit(solution)/shard_map/ppermute | solution.py:566
  28.0 0.5 %collective-permute-start.8 = (bf16[272,128]{1,0:T(8,128)(2,1)S(1)}, bf16[272,128]{1,0:T(8,128)(2,1)S(1)}, u32[]{:S(2)}, u32[]{:S(2)}) collective-permute-start(bf16[272,128]{1,0:T(8,128)(2,1)S(1)} %add_add_fusion), channel_id=1, source_target_pairs={{0,4},{1,9},{2,6},{3,11},{4,0},{5,13},{6,2},{7,15},{8,12},{9,1},{1... | collective-permute-start | bytes 208904 | tf_op jit(solution)/shard_map/ppermute | solution.py:566
  28.5 1.4 %collective-permute-done.10 = bf16[272,128]{1,0:T(8,128)(2,1)S(1)} collective-permute-done((bf16[272,128]{1,0:T(8,128)(2,1)S(1)}, bf16[272,128]{1,0:T(8,128)(2,1)S(1)}, u32[]{:S(2)}, u32[]{:S(2)}) %collective-permute-start.10) | collective-permute-done | bytes 69664 | tf_op jit(solution)/shard_map/ppermute | solution.py:566
  29.9 1.5 %collective-permute-done.9 = bf16[272,128]{1,0:T(8,128)(2,1)S(1)} collective-permute-done((bf16[272,128]{1,0:T(8,128)(2,1)S(1)}, bf16[272,128]{1,0:T(8,128)(2,1)S(1)}, u32[]{:S(2)}, u32[]{:S(2)}) %collective-permute-start.9) | collective-permute-done | bytes 69664 | tf_op jit(solution)/shard_map/ppermute | solution.py:566
  31.4 0.9 %collective-permute-done.8 = bf16[272,128]{1,0:T(8,128)(2,1)S(1)} collective-permute-done((bf16[272,128]{1,0:T(8,128)(2,1)S(1)}, bf16[272,128]{1,0:T(8,128)(2,1)S(1)}, u32[]{:S(2)}, u32[]{:S(2)}) %collective-permute-start.8) | collective-permute-done | bytes 69664 | tf_op jit(solution)/shard_map/ppermute | solution.py:566
  32.4 0.1 collective-permute-start.11
  32.4 1.2 %collective-permute-done.11.theirs_ref = bf16[272,128]{1,0:T(8,128)(2,1)S(1)} collective-permute-done((bf16[272,128]{1,0:T(8,128)(2,1)S(1)}, bf16[272,128]{1,0:T(8,128)(2,1)S(1)}, u32[]{:S(2)}, u32[]{:S(2)}) %collective-permute-start.11) | collective-permute-done | bytes 69664 | tf_op jit(solution)/shard_map/ppermute | solution.py:560
  33.7 0.7 %last.1 = (f32[32,1024]{1,0:T(8,128)}, f32[1,1024]{1,0:T(1,128)}, f32[1,16]{1,0:T(1,128)}) custom-call(s32[1]{0:T(128)} %bitcast.me_ref, bf16[272,128]{1,0:T(8,128)(2,1)S(1)} %add_convert_fusion.mine_ref, bf16[272,128]{1,0:T(8,128)(2,1)S(1)} %collective-permute-done.11.theirs_ref), custom_call_target="tpu_custom_call" | custom-call | flops 100000000 | bytes 3000000 | tf_op jit(solution)/shard_map/last/pallas_call | solution.py:542
  (5 shorter events, 0.1 us)
Async XLA Ops:
  3.5 3.1 %collective-permute-start = (bf16[208,1024]{1,0:T(8,128)(2,1)S(1)}, bf16[208,1024]{1,0:T(8,128)(2,1)S(1)}, u32[]{:S(2)}, u32[]{:S(2)}) collective-permute-start(bf16[208,1024]{1,0:T(8,128)(2,1)S(1)} %get-tuple-element.65), channel_id=1, source_target_pairs={{0,1},{1,0},{2,3},{3,2},{4,5},{5,4},{6,7},{7,6},{8,9},{9,8},{10,11... | collective-permute-start | bytes 1277960 | tf_op jit(solution)/shard_map/ppermute | solution.py:560
  4.0 8.1 %collective-permute-start.1 = (bf16[144,1024]{1,0:T(8,128)(2,1)S(1)}, bf16[144,1024]{1,0:T(8,128)(2,1)S(1)}, u32[]{:S(2)}, u32[]{:S(2)}) collective-permute-start(bf16[144,1024]{1,0:T(8,128)(2,1)S(1)} %get-tuple-element.66), channel_id=1, source_target_pairs={{0,4},{1,2},{2,1},{3,7},{4,0},{5,6},{6,5},{7,3},{8,12},{9,10},{10,... | collective-permute-start | bytes 884744 | tf_op jit(solution)/shard_map/ppermute | solution.py:576
  7.1 5.6 %collective-permute-start.2 = (bf16[64,1024]{1,0:T(8,128)(2,1)S(1)}, bf16[64,1024]{1,0:T(8,128)(2,1)S(1)}, u32[]{:S(2)}, u32[]{:S(2)}) collective-permute-start(bf16[64,1024]{1,0:T(8,128)(2,1)S(1)} %get-tuple-element.82), channel_id=1, source_target_pairs={{0,4},{1,2},{2,1},{3,7},{4,0},{5,6},{6,5},{7,3},{8,12},{9,10},{10,... | collective-permute-start | bytes 393224 | tf_op jit(solution)/shard_map/ppermute | solution.py:576
  12.8 1.4 %collective-permute-start.3 = (bf16[64,1024]{1,0:T(8,128)(2,1)S(1)}, bf16[64,1024]{1,0:T(8,128)(2,1)S(1)}, u32[]{:S(2)}, u32[]{:S(2)}) collective-permute-start(bf16[64,1024]{1,0:T(8,128)(2,1)S(1)} %pass_on.1), channel_id=1, source_target_pairs={{0,1},{1,0},{2,3},{3,2},{4,5},{5,4},{6,7},{7,6},{8,9},{9,8},{10,11... | collective-permute-start | bytes 393224 | tf_op jit(solution)/shard_map/ppermute | solution.py:560
  16.9 1.3 %collective-permute-start.4 = (bf16[272,128]{1,0:T(8,128)(2,1)S(1)}, bf16[272,128]{1,0:T(8,128)(2,1)S(1)}, u32[]{:S(2)}, u32[]{:S(2)}) collective-permute-start(bf16[272,128]{1,0:T(8,128)(2,1)S(1)} %get-tuple-element.85), channel_id=1, source_target_pairs={{0,1},{1,0},{2,3},{3,2},{4,5},{5,4},{6,7},{7,6},{8,9},{9,8},{10,11... | collective-permute-start | bytes 208904 | tf_op jit(solution)/shard_map/ppermute | solution.py:560
  18.3 5.8 %collective-permute-start.7 = (bf16[272,128]{1,0:T(8,128)(2,1)S(1)}, bf16[272,128]{1,0:T(8,128)(2,1)S(1)}, u32[]{:S(2)}, u32[]{:S(2)}) collective-permute-start(bf16[272,128]{1,0:T(8,128)(2,1)S(1)} %add_convert_fusion.1), channel_id=1, source_target_pairs={{0,8},{1,7},{2,10},{3,5},{4,12},{5,3},{6,14},{7,1},{8,0},{9,15},{1... | collective-permute-start | bytes 208904 | tf_op jit(solution)/shard_map/ppermute | solution.py:566
  20.4 4.3 %collective-permute-start.6 = (bf16[272,128]{1,0:T(8,128)(2,1)S(1)}, bf16[272,128]{1,0:T(8,128)(2,1)S(1)}, u32[]{:S(2)}, u32[]{:S(2)}) collective-permute-start(bf16[272,128]{1,0:T(8,128)(2,1)S(1)} %add_convert_fusion.1), channel_id=1, source_target_pairs={{0,8},{1,5},{2,10},{3,7},{4,12},{5,1},{6,14},{7,3},{8,0},{9,13},{1... | collective-permute-start | bytes 208904 | tf_op jit(solution)/shard_map/ppermute | solution.py:566
  20.5 5.0 %collective-permute-start.5 = (bf16[272,128]{1,0:T(8,128)(2,1)S(1)}, bf16[272,128]{1,0:T(8,128)(2,1)S(1)}, u32[]{:S(2)}, u32[]{:S(2)}) collective-permute-start(bf16[272,128]{1,0:T(8,128)(2,1)S(1)} %add_convert_fusion.1), channel_id=1, source_target_pairs={{0,8},{1,3},{2,10},{3,1},{4,12},{5,7},{6,14},{7,5},{8,0},{9,11},{1... | collective-permute-start | bytes 208904 | tf_op jit(solution)/shard_map/ppermute | solution.py:566
  25.5 4.4 %collective-permute-start.10 = (bf16[272,128]{1,0:T(8,128)(2,1)S(1)}, bf16[272,128]{1,0:T(8,128)(2,1)S(1)}, u32[]{:S(2)}, u32[]{:S(2)}) collective-permute-start(bf16[272,128]{1,0:T(8,128)(2,1)S(1)} %add_add_fusion), channel_id=1, source_target_pairs={{0,4},{1,25},{2,6},{3,27},{4,0},{5,29},{6,2},{7,31},{8,12},{9,17},... | collective-permute-start | bytes 208904 | tf_op jit(solution)/shard_map/ppermute | solution.py:566
  27.1 4.3 %collective-permute-start.9 = (bf16[272,128]{1,0:T(8,128)(2,1)S(1)}, bf16[272,128]{1,0:T(8,128)(2,1)S(1)}, u32[]{:S(2)}, u32[]{:S(2)}) collective-permute-start(bf16[272,128]{1,0:T(8,128)(2,1)S(1)} %add_add_fusion), channel_id=1, source_target_pairs={{0,2},{1,17},{2,0},{3,19},{4,6},{5,21},{6,4},{7,23},{8,10},{9,25},... | collective-permute-start | bytes 208904 | tf_op jit(solution)/shard_map/ppermute | solution.py:566
  28.0 4.3 %collective-permute-start.8 = (bf16[272,128]{1,0:T(8,128)(2,1)S(1)}, bf16[272,128]{1,0:T(8,128)(2,1)S(1)}, u32[]{:S(2)}, u32[]{:S(2)}) collective-permute-start(bf16[272,128]{1,0:T(8,128)(2,1)S(1)} %add_add_fusion), channel_id=1, source_target_pairs={{0,4},{1,9},{2,6},{3,11},{4,0},{5,13},{6,2},{7,15},{8,12},{9,1},{1... | collective-permute-start | bytes 208904 | tf_op jit(solution)/shard_map/ppermute | solution.py:566
  32.4 1.3 %collective-permute-start.11 = (bf16[272,128]{1,0:T(8,128)(2,1)S(1)}, bf16[272,128]{1,0:T(8,128)(2,1)S(1)}, u32[]{:S(2)}, u32[]{:S(2)}) collective-permute-start(bf16[272,128]{1,0:T(8,128)(2,1)S(1)} %add_convert_fusion.mine_ref), channel_id=1, source_target_pairs={{0,1},{1,0},{2,3},{3,2},{4,5},{5,4},{6,7},{7,6},{8,9},{9,8},{10,11... | collective-permute-start | bytes 208904 | tf_op jit(solution)/shard_map/ppermute | solution.py:560

commit v6 on v4

--- a/solution.py
+++ b/solution.py
@@ -562,7 +562,7 @@
 
 def odd_swapped(value, distance, stage):
     count = lax.axis_size(EVERYONE)
-    idle = 8 if stage == 2 and count > 8 else 2 if distance == 2 * stage else 4
+    idle = 2 if distance == 2 * stage else 8 if stage == 2 and count > 8 else 4
     return lax.ppermute(value, EVERYONE, [(i, i ^ (distance if i % 2 else idle)) for i in range(count)])
 
 

time: 34.4 us -> 34.8 us (1.012)
  waiting for transfers between devices: 7.59 us -> 8.44 us
  starting transfers between devices: 12.6 us -> 12.2 us
    ppermute x6, waiting for transfers between devices: 5.16 us -> 6.01 us  [odd_swapped(): lax.ppermute(value, EVERYONE, [(i, i ^ (distance if i % 2 else idle)) for...]
    ppermute x6, starting transfers between devices: 7.16 us -> 6.71 us  [odd_swapped(): lax.ppermute(value, EVERYONE, [(i, i ^ (distance if i % 2 else idle)) for...]
where the time goes in v6:
time: 34.8 us; the launch traced here: 34.7 us
  Pallas kernels  13.3 us (38%)
  starting transfers between devices  12.2 us (35%)
  waiting for transfers between devices  8.44 us (24%)
  between operations  0.74 us (2%)
    pallas_call x10, Pallas kernels, call(): pl.pallas_call(kernel, out_shape=tuple((jax.ShapeDtypeStruct(*out) for ou...  13.3 us
    ppermute x6, starting transfers between devices, odd_swapped(): lax.ppermute(value, EVERYONE, [(i, i ^ (distance if i % 2 else idle)) for...  6.71 us
    ppermute x6, waiting for transfers between devices, odd_swapped(): lax.ppermute(value, EVERYONE, [(i, i ^ (distance if i % 2 else idle)) for...  6.01 us
    ppermute x2, starting transfers between devices, inner_swapped(): return lax.ppermute(value, EVERYONE, pairs)  4.37 us
    ppermute x4, waiting for transfers between devices, swapped(): lax.ppermute(value, axis, [(i, i ^ distance) for i in range(lax.axis_size...  2.41 us
    ppermute x4, starting transfers between devices, swapped(): lax.ppermute(value, axis, [(i, i ^ distance) for i in range(lax.axis_size...  1.08 us
  transfers between devices with their start and end apart: 12, of which 8 were waited for; matrix products, arithmetic and copies ran while one was open for 0% of the time, Pallas kernels for 20%

profile of v6, /device:TPU:0, one launch (start us, length us, event | category | flops | bytes accessed | tf_op | source)
XLA Modules:
  0.0 34.7 jit_solution(8379597731371320837)
XLA Ops:
  0.6 2.9 %prep.1 = (bf16[128,1024]{1,0:T(8,128)(2,1)S(1)}, bf16[128,1024]{1,0:T(8,128)(2,1)S(1)}, f32[128,128]{1,0:T(8,128)S(1)}, bf16[208,1024]{1,0:T(8,128)(2,1)S(1)}, ...) custom-call(s32[1]{0:T(128)} %bitcast.me_ref, ...), custom_call_target="tpu_custom_call" | custom-call | flops 100000000 | bytes 3000000 | tf_op jit(solution)/shard_map/prep/pallas_call | solution.py:542
  3.5 0.5 %collective-permute-start = (bf16[208,1024]{1,0:T(8,128)(2,1)S(1)}, bf16[208,1024]{1,0:T(8,128)(2,1)S(1)}, u32[]{:S(2)}, u32[]{:S(2)}) collective-permute-start(bf16[208,1024]{1,0:T(8,128)(2,1)S(1)} %get-tuple-element.65), channel_id=1, source_target_pairs={{0,1},{1,0},{2,3},{3,2},{4,5},{5,4},{6,7},{7,6},{8,9},{9,8},{10,11... | collective-permute-start | bytes 1277960 | tf_op jit(solution)/shard_map/ppermute | solution.py:560
  4.0 2.6 %collective-permute-start.1 = (bf16[144,1024]{1,0:T(8,128)(2,1)S(1)}, bf16[144,1024]{1,0:T(8,128)(2,1)S(1)}, u32[]{:S(2)}, u32[]{:S(2)}) collective-permute-start(bf16[144,1024]{1,0:T(8,128)(2,1)S(1)} %get-tuple-element.66), channel_id=1, source_target_pairs={{0,4},{1,2},{2,1},{3,7},{4,0},{5,6},{6,5},{7,3},{8,12},{9,10},{10,... | collective-permute-start | bytes 884744 | tf_op jit(solution)/shard_map/ppermute | solution.py:576
  6.7 0.0 collective-permute-done.rim_ref.near_ref
  6.7 0.5 %join_near.1 = (f32[64,1024]{1,0:T(8,128)S(1)}, bf16[64,1024]{1,0:T(8,128)(2,1)S(1)}) custom-call(s32[1]{0:T(128)} %bitcast.me_ref, f32[128,128]{1,0:T(8,128)S(1)} %get-tuple-element.62.small_ref.own_ref.edge_ref, f32[128,128]{1,0:T(8,128)S(1)} %get-tuple-element.62.small_ref.own_ref.edge_ref, f32[128,128]{1,0:T(8,128)S(1)} %get-tuple-element.62.small_ref.own_ref.edge_ref, ...), custom_call_target="tpu_custom_call" | custom-call | flops 100000000 | bytes 3000000 | tf_op jit(solution)/shard_map/join_near/pallas_call | solution.py:542
  7.2 1.8 %collective-permute-start.2 = (bf16[64,1024]{1,0:T(8,128)(2,1)S(1)}, bf16[64,1024]{1,0:T(8,128)(2,1)S(1)}, u32[]{:S(2)}, u32[]{:S(2)}) collective-permute-start(bf16[64,1024]{1,0:T(8,128)(2,1)S(1)} %get-tuple-element.82), channel_id=1, source_target_pairs={{0,4},{1,2},{2,1},{3,7},{4,0},{5,6},{6,5},{7,3},{8,12},{9,10},{10,... | collective-permute-start | bytes 393224 | tf_op jit(solution)/shard_map/ppermute | solution.py:576
  8.9 1.8 %own.1 = (f32[128,1024]{1,0:T(8,128)S(1)}, f32[128,1024]{1,0:T(8,128)S(1)}, f32[128,1024]{1,0:T(8,128)S(1)}, f32[128,16]{1,0:T(8,128)S(1)}) custom-call(s32[1]{0:T(128)} %bitcast.me_ref, f32[128,128]{1,0:T(8,128)S(1)} %get-tuple-element.62.small_ref.own_ref.edge_ref, bf16[128,1024]{1,0:T(8,128)(2,1)S(1)} %get-tuple-element.63.wk_ref, ...), custom_call_target="tpu_custom_call" | custom-call | flops 700000000 | bytes 7000000 | tf_op jit(solution)/shard_map/own/pallas_call | solution.py:542
  10.8 1.5 %edge_near.1 = (f32[64,1024]{1,0:T(8,128)S(1)}, f32[64,1024]{1,0:T(8,128)S(1)}, f32[64,16]{1,0:T(8,128)S(1)}, f32[400,1024]{1,0:T(8,128)S(1)}) custom-call(s32[1]{0:T(128)} %bitcast.me_ref, f32[128,128]{1,0:T(8,128)S(1)} %get-tuple-element.62.small_ref.own_ref.edge_ref, bf16[128,1024]{1,0:T(8,128)(2,1)S(1)} %get-tuple-element.63.wk_ref, ...), custom_call_target="tpu_custom_call" | custom-call | flops 200000000 | bytes 5000000 | tf_op jit(solution)/shard_map/edge_near/pallas_call | solution.py:542
  12.2 0.5 %join_far.1 = (f32[64,1024]{1,0:T(8,128)S(1)}, f32[64,1024]{1,0:T(8,128)S(1)}, f32[1,1024]{1,0:T(1,128)S(1)}) custom-call(s32[1]{0:T(128)} %bitcast.me_ref, f32[128,16]{1,0:T(8,128)S(1)} %get-tuple-element.71.own_ref.dl_ref, f32[64,16]{1,0:T(8,128)S(1)} %get-tuple-element.75.edge_ref.near_dl_ref, ...), custom_call_target="tpu_custom_call" | custom-call | flops 100000000 | bytes 3000000 | tf_op jit(solution)/shard_map/join_far/pallas_call | solution.py:542
  12.7 0.0 collective-permute-done.2.state_ref.cross_ref
  12.8 0.3 collective-permute-start.3
  13.1 1.1 %edge_far.1 = (f32[64,1024]{1,0:T(8,128)S(1)}, f32[64,1024]{1,0:T(8,128)S(1)}, f32[64,16]{1,0:T(8,128)S(1)}) custom-call(s32[1]{0:T(128)} %bitcast.me_ref, f32[128,128]{1,0:T(8,128)S(1)} %get-tuple-element.62.small_ref.own_ref.edge_ref, bf16[128,1024]{1,0:T(8,128)(2,1)S(1)} %get-tuple-element.63.wk_ref, bf16[128,1024]{1,0:T(8,128)(2,1)S(1)} %get-tuple-element.64.qf_ref, ...), custom_call_target="tpu_custom_call" | custom-call | flops 200000000 | bytes 3000000 | tf_op jit(solution)/shard_map/edge_far/pallas_call | solution.py:542
  14.1 0.1 collective-permute-done.3.passed_ref
  14.2 2.6 %finish.1 = (f32[128,1024]{1,0:T(8,128)S(1)}, f32[128,1024]{1,0:T(8,128)S(1)}, bf16[128,1024]{1,0:T(8,128)(2,1)S(1)}, f32[128,32]{1,0:T(8,128)S(1)}, bf16[272,128]{1,0:T(8,128)(2,1)S(1)}) custom-call(s32[1]{0:T(128)} %bitcast.me_ref, bf16[128,1024]{1,0:T(8,128)(2,1)S(1)} %get-tuple-element.55.q_ref, bf16[128,1024]{1,0:T(8,128)(2,1)S(1)} %get-tuple-element.56.k_ref, ...), custom_call_target="tpu_custom_call" | custom-call | flops 100000000 | bytes 3000000 | tf_op jit(solution)/shard_map/finish/pallas_call | solution.py:542
  16.9 0.3 collective-permute-start.4
  17.1 1.1 %collective-permute-done.4 = bf16[272,128]{1,0:T(8,128)(2,1)S(1)} collective-permute-done((bf16[272,128]{1,0:T(8,128)(2,1)S(1)}, bf16[272,128]{1,0:T(8,128)(2,1)S(1)}, u32[]{:S(2)}, u32[]{:S(2)}) %collective-permute-start.4) | collective-permute-done | bytes 69664 | tf_op jit(solution)/shard_map/ppermute | solution.py:560
  18.2 2.1 %collective-permute-start.7 = (bf16[272,128]{1,0:T(8,128)(2,1)S(1)}, bf16[272,128]{1,0:T(8,128)(2,1)S(1)}, u32[]{:S(2)}, u32[]{:S(2)}) collective-permute-start(bf16[272,128]{1,0:T(8,128)(2,1)S(1)} %add_convert_fusion.1), channel_id=1, source_target_pairs={{0,8},{1,7},{2,10},{3,5},{4,12},{5,3},{6,14},{7,1},{8,0},{9,15},{1... | collective-permute-start | bytes 208904 | tf_op jit(solution)/shard_map/ppermute | solution.py:566
  20.4 0.9 %collective-permute-start.6 = (bf16[272,128]{1,0:T(8,128)(2,1)S(1)}, bf16[272,128]{1,0:T(8,128)(2,1)S(1)}, u32[]{:S(2)}, u32[]{:S(2)}) collective-permute-start(bf16[272,128]{1,0:T(8,128)(2,1)S(1)} %add_convert_fusion.1), channel_id=1, source_target_pairs={{0,2},{1,5},{2,0},{3,7},{4,6},{5,1},{6,4},{7,3},{8,10},{9,13},{10,... | collective-permute-start | bytes 208904 | tf_op jit(solution)/shard_map/ppermute | solution.py:566
  21.3 0.4 %collective-permute-start.5 = (bf16[272,128]{1,0:T(8,128)(2,1)S(1)}, bf16[272,128]{1,0:T(8,128)(2,1)S(1)}, u32[]{:S(2)}, u32[]{:S(2)}) collective-permute-start(bf16[272,128]{1,0:T(8,128)(2,1)S(1)} %add_convert_fusion.1), channel_id=1, source_target_pairs={{0,8},{1,3},{2,10},{3,1},{4,12},{5,7},{6,14},{7,5},{8,0},{9,11},{1... | collective-permute-start | bytes 208904 | tf_op jit(solution)/shard_map/ppermute | solution.py:566
  21.7 1.7 %outputs.1 = (bf16[128,1024]{1,0:T(8,128)(2,1)}, bf16[128,1024]{1,0:T(8,128)(2,1)}, bf16[128,1024]{1,0:T(8,128)(2,1)}, bf16[128,1024]{1,0:T(8,128)(2,1)}) custom-call(s32[1]{0:T(128)} %bitcast.me_ref, f32[128,32]{1,0:T(8,128)S(1)} %get-tuple-element.86.logits_ref, f32[32,1024]{1,0:T(8,128)S(1)} %get-tuple-element.87.w_ref, ...), custom_call_target="tpu_custom_call" | custom-call | flops 100000000 | bytes 3000000 | tf_op jit(solution)/shard_map/outputs/pallas_call | solution.py:542
  23.4 0.0 collective-permute-done.7
  23.4 1.4 %collective-permute-done.6 = bf16[272,128]{1,0:T(8,128)(2,1)S(1)} collective-permute-done((bf16[272,128]{1,0:T(8,128)(2,1)S(1)}, bf16[272,128]{1,0:T(8,128)(2,1)S(1)}, u32[]{:S(2)}, u32[]{:S(2)}) %collective-permute-start.6) | collective-permute-done | bytes 69664 | tf_op jit(solution)/shard_map/ppermute | solution.py:566
  24.8 0.8 %collective-permute-done.5 = bf16[272,128]{1,0:T(8,128)(2,1)S(1)} collective-permute-done((bf16[272,128]{1,0:T(8,128)(2,1)S(1)}, bf16[272,128]{1,0:T(8,128)(2,1)S(1)}, u32[]{:S(2)}, u32[]{:S(2)}) %collective-permute-start.5) | collective-permute-done | bytes 69664 | tf_op jit(solution)/shard_map/ppermute | solution.py:566
  25.6 1.6 %collective-permute-start.10 = (bf16[272,128]{1,0:T(8,128)(2,1)S(1)}, bf16[272,128]{1,0:T(8,128)(2,1)S(1)}, u32[]{:S(2)}, u32[]{:S(2)}) collective-permute-start(bf16[272,128]{1,0:T(8,128)(2,1)S(1)} %add_add_fusion), channel_id=1, source_target_pairs={{0,4},{1,25},{2,6},{3,27},{4,0},{5,29},{6,2},{7,31},{8,12},{9,17},... | collective-permute-start | bytes 208904 | tf_op jit(solution)/shard_map/ppermute | solution.py:566
  27.2 1.1 %collective-permute-start.9 = (bf16[272,128]{1,0:T(8,128)(2,1)S(1)}, bf16[272,128]{1,0:T(8,128)(2,1)S(1)}, u32[]{:S(2)}, u32[]{:S(2)}) collective-permute-start(bf16[272,128]{1,0:T(8,128)(2,1)S(1)} %add_add_fusion), channel_id=1, source_target_pairs={{0,2},{1,17},{2,0},{3,19},{4,6},{5,21},{6,4},{7,23},{8,10},{9,25},... | collective-permute-start | bytes 208904 | tf_op jit(solution)/shard_map/ppermute | solution.py:566
  28.3 0.5 %collective-permute-start.8 = (bf16[272,128]{1,0:T(8,128)(2,1)S(1)}, bf16[272,128]{1,0:T(8,128)(2,1)S(1)}, u32[]{:S(2)}, u32[]{:S(2)}) collective-permute-start(bf16[272,128]{1,0:T(8,128)(2,1)S(1)} %add_add_fusion), channel_id=1, source_target_pairs={{0,4},{1,9},{2,6},{3,11},{4,0},{5,13},{6,2},{7,15},{8,12},{9,1},{1... | collective-permute-start | bytes 208904 | tf_op jit(solution)/shard_map/ppermute | solution.py:566
  28.8 1.2 %collective-permute-done.10 = bf16[272,128]{1,0:T(8,128)(2,1)S(1)} collective-permute-done((bf16[272,128]{1,0:T(8,128)(2,1)S(1)}, bf16[272,128]{1,0:T(8,128)(2,1)S(1)}, u32[]{:S(2)}, u32[]{:S(2)}) %collective-permute-start.10) | collective-permute-done | bytes 69664 | tf_op jit(solution)/shard_map/ppermute | solution.py:566
  30.0 1.5 %collective-permute-done.9 = bf16[272,128]{1,0:T(8,128)(2,1)S(1)} collective-permute-done((bf16[272,128]{1,0:T(8,128)(2,1)S(1)}, bf16[272,128]{1,0:T(8,128)(2,1)S(1)}, u32[]{:S(2)}, u32[]{:S(2)}) %collective-permute-start.9) | collective-permute-done | bytes 69664 | tf_op jit(solution)/shard_map/ppermute | solution.py:566
  31.5 1.1 %collective-permute-done.8 = bf16[272,128]{1,0:T(8,128)(2,1)S(1)} collective-permute-done((bf16[272,128]{1,0:T(8,128)(2,1)S(1)}, bf16[272,128]{1,0:T(8,128)(2,1)S(1)}, u32[]{:S(2)}, u32[]{:S(2)}) %collective-permute-start.8) | collective-permute-done | bytes 69664 | tf_op jit(solution)/shard_map/ppermute | solution.py:566
  32.7 0.1 collective-permute-start.11
  32.8 1.2 %collective-permute-done.11.theirs_ref = bf16[272,128]{1,0:T(8,128)(2,1)S(1)} collective-permute-done((bf16[272,128]{1,0:T(8,128)(2,1)S(1)}, bf16[272,128]{1,0:T(8,128)(2,1)S(1)}, u32[]{:S(2)}, u32[]{:S(2)}) %collective-permute-start.11) | collective-permute-done | bytes 69664 | tf_op jit(solution)/shard_map/ppermute | solution.py:560
  34.0 0.7 %last.1 = (f32[32,1024]{1,0:T(8,128)}, f32[1,1024]{1,0:T(1,128)}, f32[1,16]{1,0:T(1,128)}) custom-call(s32[1]{0:T(128)} %bitcast.me_ref, bf16[272,128]{1,0:T(8,128)(2,1)S(1)} %add_convert_fusion.mine_ref, bf16[272,128]{1,0:T(8,128)(2,1)S(1)} %collective-permute-done.11.theirs_ref), custom_call_target="tpu_custom_call" | custom-call | flops 100000000 | bytes 3000000 | tf_op jit(solution)/shard_map/last/pallas_call | solution.py:542
  (5 shorter events, 0.1 us)
Async XLA Ops:
  3.5 3.1 %collective-permute-start = (bf16[208,1024]{1,0:T(8,128)(2,1)S(1)}, bf16[208,1024]{1,0:T(8,128)(2,1)S(1)}, u32[]{:S(2)}, u32[]{:S(2)}) collective-permute-start(bf16[208,1024]{1,0:T(8,128)(2,1)S(1)} %get-tuple-element.65), channel_id=1, source_target_pairs={{0,1},{1,0},{2,3},{3,2},{4,5},{5,4},{6,7},{7,6},{8,9},{9,8},{10,11... | collective-permute-start | bytes 1277960 | tf_op jit(solution)/shard_map/ppermute | solution.py:560
  4.0 8.2 %collective-permute-start.1 = (bf16[144,1024]{1,0:T(8,128)(2,1)S(1)}, bf16[144,1024]{1,0:T(8,128)(2,1)S(1)}, u32[]{:S(2)}, u32[]{:S(2)}) collective-permute-start(bf16[144,1024]{1,0:T(8,128)(2,1)S(1)} %get-tuple-element.66), channel_id=1, source_target_pairs={{0,4},{1,2},{2,1},{3,7},{4,0},{5,6},{6,5},{7,3},{8,12},{9,10},{10,... | collective-permute-start | bytes 884744 | tf_op jit(solution)/shard_map/ppermute | solution.py:576
  7.2 5.6 %collective-permute-start.2 = (bf16[64,1024]{1,0:T(8,128)(2,1)S(1)}, bf16[64,1024]{1,0:T(8,128)(2,1)S(1)}, u32[]{:S(2)}, u32[]{:S(2)}) collective-permute-start(bf16[64,1024]{1,0:T(8,128)(2,1)S(1)} %get-tuple-element.82), channel_id=1, source_target_pairs={{0,4},{1,2},{2,1},{3,7},{4,0},{5,6},{6,5},{7,3},{8,12},{9,10},{10,... | collective-permute-start | bytes 393224 | tf_op jit(solution)/shard_map/ppermute | solution.py:576
  12.8 1.4 %collective-permute-start.3 = (bf16[64,1024]{1,0:T(8,128)(2,1)S(1)}, bf16[64,1024]{1,0:T(8,128)(2,1)S(1)}, u32[]{:S(2)}, u32[]{:S(2)}) collective-permute-start(bf16[64,1024]{1,0:T(8,128)(2,1)S(1)} %pass_on.1), channel_id=1, source_target_pairs={{0,1},{1,0},{2,3},{3,2},{4,5},{5,4},{6,7},{7,6},{8,9},{9,8},{10,11... | collective-permute-start | bytes 393224 | tf_op jit(solution)/shard_map/ppermute | solution.py:560
  16.9 1.3 %collective-permute-start.4 = (bf16[272,128]{1,0:T(8,128)(2,1)S(1)}, bf16[272,128]{1,0:T(8,128)(2,1)S(1)}, u32[]{:S(2)}, u32[]{:S(2)}) collective-permute-start(bf16[272,128]{1,0:T(8,128)(2,1)S(1)} %get-tuple-element.85), channel_id=1, source_target_pairs={{0,1},{1,0},{2,3},{3,2},{4,5},{5,4},{6,7},{7,6},{8,9},{9,8},{10,11... | collective-permute-start | bytes 208904 | tf_op jit(solution)/shard_map/ppermute | solution.py:560
  18.2 5.2 %collective-permute-start.7 = (bf16[272,128]{1,0:T(8,128)(2,1)S(1)}, bf16[272,128]{1,0:T(8,128)(2,1)S(1)}, u32[]{:S(2)}, u32[]{:S(2)}) collective-permute-start(bf16[272,128]{1,0:T(8,128)(2,1)S(1)} %add_convert_fusion.1), channel_id=1, source_target_pairs={{0,8},{1,7},{2,10},{3,5},{4,12},{5,3},{6,14},{7,1},{8,0},{9,15},{1... | collective-permute-start | bytes 208904 | tf_op jit(solution)/shard_map/ppermute | solution.py:566
  20.4 4.5 %collective-permute-start.6 = (bf16[272,128]{1,0:T(8,128)(2,1)S(1)}, bf16[272,128]{1,0:T(8,128)(2,1)S(1)}, u32[]{:S(2)}, u32[]{:S(2)}) collective-permute-start(bf16[272,128]{1,0:T(8,128)(2,1)S(1)} %add_convert_fusion.1), channel_id=1, source_target_pairs={{0,2},{1,5},{2,0},{3,7},{4,6},{5,1},{6,4},{7,3},{8,10},{9,13},{10,... | collective-permute-start | bytes 208904 | tf_op jit(solution)/shard_map/ppermute | solution.py:566
  21.3 4.3 %collective-permute-start.5 = (bf16[272,128]{1,0:T(8,128)(2,1)S(1)}, bf16[272,128]{1,0:T(8,128)(2,1)S(1)}, u32[]{:S(2)}, u32[]{:S(2)}) collective-permute-start(bf16[272,128]{1,0:T(8,128)(2,1)S(1)} %add_convert_fusion.1), channel_id=1, source_target_pairs={{0,8},{1,3},{2,10},{3,1},{4,12},{5,7},{6,14},{7,5},{8,0},{9,11},{1... | collective-permute-start | bytes 208904 | tf_op jit(solution)/shard_map/ppermute | solution.py:566
  25.6 4.4 %collective-permute-start.10 = (bf16[272,128]{1,0:T(8,128)(2,1)S(1)}, bf16[272,128]{1,0:T(8,128)(2,1)S(1)}, u32[]{:S(2)}, u32[]{:S(2)}) collective-permute-start(bf16[272,128]{1,0:T(8,128)(2,1)S(1)} %add_add_fusion), channel_id=1, source_target_pairs={{0,4},{1,25},{2,6},{3,27},{4,0},{5,29},{6,2},{7,31},{8,12},{9,17},... | collective-permute-start | bytes 208904 | tf_op jit(solution)/shard_map/ppermute | solution.py:566
  27.2 4.3 %collective-permute-start.9 = (bf16[272,128]{1,0:T(8,128)(2,1)S(1)}, bf16[272,128]{1,0:T(8,128)(2,1)S(1)}, u32[]{:S(2)}, u32[]{:S(2)}) collective-permute-start(bf16[272,128]{1,0:T(8,128)(2,1)S(1)} %add_add_fusion), channel_id=1, source_target_pairs={{0,2},{1,17},{2,0},{3,19},{4,6},{5,21},{6,4},{7,23},{8,10},{9,25},... | collective-permute-start | bytes 208904 | tf_op jit(solution)/shard_map/ppermute | solution.py:566
  28.3 4.3 %collective-permute-start.8 = (bf16[272,128]{1,0:T(8,128)(2,1)S(1)}, bf16[272,128]{1,0:T(8,128)(2,1)S(1)}, u32[]{:S(2)}, u32[]{:S(2)}) collective-permute-start(bf16[272,128]{1,0:T(8,128)(2,1)S(1)} %add_add_fusion), channel_id=1, source_target_pairs={{0,4},{1,9},{2,6},{3,11},{4,0},{5,13},{6,2},{7,15},{8,12},{9,1},{1... | collective-permute-start | bytes 208904 | tf_op jit(solution)/shard_map/ppermute | solution.py:566
  32.7 1.3 %collective-permute-start.11 = (bf16[272,128]{1,0:T(8,128)(2,1)S(1)}, bf16[272,128]{1,0:T(8,128)(2,1)S(1)}, u32[]{:S(2)}, u32[]{:S(2)}) collective-permute-start(bf16[272,128]{1,0:T(8,128)(2,1)S(1)} %add_convert_fusion.mine_ref), channel_id=1, source_target_pairs={{0,1},{1,0},{2,3},{3,2},{4,5},{5,4},{6,7},{7,6},{8,9},{9,8},{10,11... | collective-permute-start | bytes 208904 | tf_op jit(solution)/shard_map/ppermute | solution.py:560
